TPU v7x, 512 devices: a whole 4x4x16 slice. The times are simulated.
512 devices in a mesh: tile: 64 (over z_hi, y, x), narrow: 8 (over z_lo, core).
Axes of the slice: x: 4, y: 4, z: 16 (z_hi: 4, z_lo: 4; z = z_hi * 4 + z_lo), core: 2. Of those that a mesh axis runs over, the one named last changes fastest.
Arguments:
- fine: bfloat16 [1024, 64, 512], P('tile', 'narrow'), may hold values from -6 to 6
- coarse: bfloat16 [256, 128, 1024], P('tile'), may hold values from -6 to 6
- block_table: int32 [64, 8], P('tile'), may hold values from 0 to 255, as said below
- shifts: int32 [2], replicated, may hold values from 1 to 7
- attn_gain: float32 [512], replicated, may hold values from 0.1 to 1.9
- w_query: bfloat16 [512, 512], replicated, may hold values from -8 to 8
- w_key: bfloat16 [512, 512], replicated, may hold values from -8 to 8
- w_value: bfloat16 [512, 512], replicated, may hold values from -0.25 to 0.25
- w_out: bfloat16 [512, 512], replicated, may hold values from -0.25 to 0.25
- coarse_key: bfloat16 [1024, 512], replicated, may hold values from -0.1875 to 0.1875
- coarse_value: bfloat16 [1024, 512], replicated, may hold values from -0.1875 to 0.1875
- mlp_gain: float32 [512], replicated, may hold values from 0.1 to 1.9
- w_gate: bfloat16 [512, 2048], replicated, may hold values from -0.25 to 0.25
- w_up: bfloat16 [512, 2048], replicated, may hold values from -0.25 to 0.25
- w_down: bfloat16 [2048, 512], replicated, may hold values from -0.125 to 0.125
Outputs:
- output: bfloat16 [1024, 64, 512], P('tile', 'narrow')
Inputs may be any that keep to these rules, and one draw needn't show every extreme that they name: `block_table`: row s names 8 distinct blocks, all among blocks (s - 1) * 4 to (s + 2) * 4 - 1 taken modulo 256, at least one of them below s * 4 and at least one at or above (s + 1) * 4 in that range.
All inputs are finite; a program needn't handle non-finite values.
Results may differ from a plain program's by a relative error of at most 0.0073.
Values may be sent and summed in bfloat16 or wider, within the bound.
No kernel may reach another device: no remote copies, remote signals or barrier semaphores. Data moves between devices by JAX's collectives and lax.ppermute only.
A program may use at most 64 MiB of HBM per device.

v0:
```python
import jax
import jax.numpy as jnp
from jax import lax
from jax.sharding import PartitionSpec as P

HEADS = 8
CW = 1024
WS = 8
HD = 64


def passed_along(x, axis, by):
    count = lax.axis_size(axis)
    return lax.ppermute(x, axis, [(i, (i + by) % count) for i in range(count)])


def with_halo(x, sides, width):
    for axis, dim in sides:
        count, length = (lax.axis_size(axis), x.shape[dim])
        up = [(i, (i + 1) % count) for i in range(count)]
        down = [(j, i) for i, j in up]
        last = lax.slice_in_dim(x, length - width, length, axis=dim)
        initial = lax.slice_in_dim(x, 0, width, axis=dim)
        before = lax.ppermute(last, axis, up)
        after = lax.ppermute(initial, axis, down)
        x = jnp.concatenate([before, x, after], axis=dim)
    return x


def rms_scale(source, gain_vec):
    values = source.astype(jnp.float32)
    mean_square = jnp.mean(values * values, axis=-1, keepdims=True)
    return values * lax.rsqrt(mean_square + 1e-06) * gain_vec


def to_windows(source):
    lead_count = source.shape[0] // WS
    across = source.shape[1] // WS
    reordered = source.reshape((lead_count, WS, across, WS) + source.shape[2:])
    reordered = jnp.swapaxes(reordered, 1, 2)
    return reordered.reshape((lead_count * across, WS * WS) + source.shape[2:])


def from_windows(source, row_count, column_count):
    reordered = source.reshape((row_count // WS, column_count // WS, WS, WS) + source.shape[2:])
    reordered = jnp.swapaxes(reordered, 1, 2)
    return reordered.reshape((row_count, column_count) + source.shape[2:])


def attend(queries, keys_fine, values_fine, coarse_keys, coarse_values, row_flag, column_flag):
    row_count, column_count = (queries.shape[0], queries.shape[1])
    labels = row_flag.astype(jnp.int32)[:, None] * 2 + column_flag.astype(jnp.int32)[None, :]
    labels = to_windows(labels)
    allowed = labels[:, :, None] == labels[:, None, :]
    query_win = to_windows(queries)
    key_win = to_windows(keys_fine)
    value_win = to_windows(values_fine)
    score_self = jnp.einsum(
        "wqhd,wkhd->whqk", query_win, key_win, preferred_element_type=jnp.float32
    )
    score_self = jnp.where(allowed[:, None], score_self, -jnp.inf)
    score_cross = jnp.einsum(
        "wqhd,khd->whqk", query_win, coarse_keys, preferred_element_type=jnp.float32
    )
    maxima = jnp.maximum(
        jnp.max(score_self, axis=-1, keepdims=True), jnp.max(score_cross, axis=-1, keepdims=True)
    )
    exp_self = jnp.exp(score_self - maxima)
    exp_cross = jnp.exp(score_cross - maxima)
    totals = jnp.sum(exp_self, axis=-1, keepdims=True) + jnp.sum(exp_cross, axis=-1, keepdims=True)
    prob_self = (exp_self / totals).astype(jnp.bfloat16)
    prob_cross = (exp_cross / totals).astype(jnp.bfloat16)
    mixture = jnp.einsum(
        "whqk,wkhd->wqhd", prob_self, value_win, preferred_element_type=jnp.float32
    )
    mixture = mixture + jnp.einsum(
        "whqk,khd->wqhd", prob_cross, coarse_values, preferred_element_type=jnp.float32
    )
    return from_windows(mixture.astype(jnp.bfloat16), row_count, column_count)


def local(
    fine,
    coarse,
    block_table,
    shifts,
    attn_gain,
    w_query,
    w_key,
    w_value,
    w_out,
    coarse_key,
    coarse_value,
    mlp_gain,
    w_gate,
    w_up,
    w_down,
):
    strip_count = lax.axis_size("tile")
    strip_index = lax.axis_index("tile")
    member_count = lax.axis_size("narrow")
    member_index = lax.axis_index("narrow")
    rows_dev, columns, feature_width = fine.shape
    shift_row = shifts[0]
    shift_col = shifts[1]
    zero_index = jnp.zeros((), jnp.int32)
    right_cols = passed_along(fine, "narrow", -1)
    widened = jnp.concatenate([fine, right_cols], axis=1)
    lower_rows = passed_along(widened[:WS], "tile", -1)
    extended = jnp.concatenate([widened, lower_rows], axis=0)
    rolled = lax.dynamic_slice(
        extended, (shift_row, shift_col, zero_index), (rows_dev, columns, feature_width)
    )
    flat_rows = rolled.reshape(-1, feature_width)
    normed = rms_scale(flat_rows, attn_gain).astype(jnp.bfloat16)
    query_scale = 1.0 / HD**0.5
    queries = (jnp.dot(normed, w_query, preferred_element_type=jnp.float32) * query_scale).astype(
        jnp.bfloat16
    )
    keys_fine = jnp.dot(normed, w_key, preferred_element_type=jnp.float32).astype(jnp.bfloat16)
    values_fine = jnp.dot(normed, w_value, preferred_element_type=jnp.float32).astype(jnp.bfloat16)
    queries = queries.reshape(rows_dev, columns, HEADS, HD)
    keys_fine = keys_fine.reshape(rows_dev, columns, HEADS, HD)
    values_fine = values_fine.reshape(rows_dev, columns, HEADS, HD)
    blocks_dev = coarse.shape[0]
    total_blocks = blocks_dev * strip_count
    local_index = jnp.mod(block_table[0] - (strip_index - 1) * blocks_dev, total_blocks)
    nearby = with_halo(coarse, (("tile", 0),), blocks_dev)
    chosen = jnp.take(nearby, local_index, axis=0).reshape(-1, CW)
    coarse_keys = jnp.dot(chosen, coarse_key, preferred_element_type=jnp.float32).astype(
        jnp.bfloat16
    )
    coarse_values = jnp.dot(chosen, coarse_value, preferred_element_type=jnp.float32).astype(
        jnp.bfloat16
    )
    coarse_keys = coarse_keys.reshape(-1, HEADS, HD)
    coarse_values = coarse_values.reshape(-1, HEADS, HD)
    row_total = rows_dev * strip_count
    column_total = columns * member_count
    row_flag = (
        strip_index * rows_dev + jnp.arange(rows_dev, dtype=jnp.int32) + shift_row >= row_total
    )
    column_flag = (
        member_index * columns + jnp.arange(columns, dtype=jnp.int32) + shift_col >= column_total
    )
    head_out = attend(
        queries, keys_fine, values_fine, coarse_keys, coarse_values, row_flag, column_flag
    )
    attn_sum = jnp.dot(
        head_out.reshape(-1, feature_width), w_out, preferred_element_type=jnp.float32
    )
    mid = flat_rows.astype(jnp.float32) + attn_sum
    normed_mid = rms_scale(mid, mlp_gain).astype(jnp.bfloat16)
    gate_term = jnp.dot(normed_mid, w_gate, preferred_element_type=jnp.float32)
    up_term = jnp.dot(normed_mid, w_up, preferred_element_type=jnp.float32)
    hidden = (jax.nn.silu(gate_term) * up_term).astype(jnp.bfloat16)
    mlp_sum = jnp.dot(hidden, w_down, preferred_element_type=jnp.float32)
    block_out = (mid + mlp_sum).astype(jnp.bfloat16).reshape(rows_dev, columns, feature_width)
    left_cols = passed_along(block_out, "narrow", 1)
    widened_out = jnp.concatenate([left_cols, block_out], axis=1)
    upper_rows = passed_along(widened_out[rows_dev - WS :], "tile", 1)
    joined = jnp.concatenate([upper_rows, widened_out], axis=0)
    return lax.dynamic_slice(
        joined, (WS - shift_row, WS - shift_col, zero_index), (rows_dev, columns, feature_width)
    )


def solution(mesh):
    placed = (
        P("tile", "narrow", None),
        P("tile", None, None),
        P("tile", None),
        P(),
        P(),
        P(),
        P(),
        P(),
        P(),
        P(),
        P(),
        P(),
        P(),
        P(),
        P(),
    )
    return jax.shard_map(
        local, mesh=mesh, in_specs=placed, out_specs=P("tile", "narrow", None), check_vma=False
    )
```

profile of v0, /device:TPU:1, one launch (start us, length us, event | category | flops | bytes accessed | tf_op | source)
XLA Modules:
  0.0 191.7 jit_solution(3258887429599395367)
XLA Ops:
  0.0 4.1 %collective-permute-start.2 = (bf16[4,128,1024]{2,1,0:T(8,128)(2,1)}, bf16[4,128,1024]{2,1,0:T(8,128)(2,1)}, u32[]{:S(2)}, u32[]{:S(2)}) collective-permute-start(bf16[4,128,1024]{2,1,0:T(8,128)(2,1)} %param.16), channel_id=1, source_target_pairs={{0,8},{8,16},{16,24},{24,32},{32,40},{40,48},{48,56},{56,64},{64,7... | collective-permute-start | bytes 3145736 | tf_op jit(solution)/shard_map/ppermute | solution.py:24
  4.1 15.9 %collective-permute-start.3 = (bf16[4,128,1024]{2,1,0:T(8,128)(2,1)}, bf16[4,128,1024]{2,1,0:T(8,128)(2,1)}, u32[]{:S(2)}, u32[]{:S(2)}) collective-permute-start(bf16[4,128,1024]{2,1,0:T(8,128)(2,1)} %param.16), channel_id=1, source_target_pairs={{8,0},{16,8},{24,16},{32,24},{40,32},{48,40},{56,48},{64,56},{72,6... | collective-permute-start | bytes 3145736 | tf_op jit(solution)/shard_map/ppermute | solution.py:25
  20.0 2.9 %collective-permute-start = (bf16[16,8,512]{2,1,0:T(8,128)(2,1)}, bf16[16,8,512]{2,1,0:T(8,128)(2,1)S(1)}, u32[]{:S(2)}, u32[]{:S(2)}) collective-permute-start(bf16[16,8,512]{2,1,0:T(8,128)(2,1)} %param.15), channel_id=1, source_target_pairs={{0,7},{1,0},{2,1},{3,2},{4,3},{5,4},{6,5},{7,6},{8,15},{9,8},{10,9... | collective-permute-start | bytes 393224 | tf_op jit(solution)/shard_map/ppermute | solution.py:14
  22.9 1.4 fusion.52
  24.3 0.7 compare_convert_fusion
  25.0 0.1 add.167
  25.1 0.6 compare_select_fusion.6
  25.8 0.1 add.161
  25.9 0.7 broadcast_compare_fusion
  26.6 0.7 compare_and_fusion
  27.3 0.1 broadcast_bitcast_fusion
  27.3 0.9 constant_dynamic-update-slice_fusion.1
  28.3 88.5 %collective-permute-done = bf16[16,8,512]{2,1,0:T(8,128)(2,1)S(1)} collective-permute-done((bf16[16,8,512]{2,1,0:T(8,128)(2,1)}, bf16[16,8,512]{2,1,0:T(8,128)(2,1)S(1)}, u32[]{:S(2)}, u32[]{:S(2)}) %collective-permute-start) | collective-permute-done | bytes 131104 | tf_op jit(solution)/shard_map/ppermute | solution.py:14
  116.8 1.9 %collective-permute-start.1 = (bf16[8,16,512]{2,1,0:T(8,128)(2,1)S(1)}, bf16[8,16,512]{2,1,0:T(8,128)(2,1)S(1)}, u32[]{:S(2)}, u32[]{:S(2)}) collective-permute-start(bf16[8,16,512]{2,1,0:T(8,128)(2,1)S(1)} %slice.18), channel_id=1, source_target_pairs={{0,504},{8,0},{16,8},{24,16},{32,24},{40,32},{48,40},{56,48},{64,5... | collective-permute-start | bytes 393224 | tf_op jit(solution)/shard_map/ppermute | solution.py:14
  118.8 0.7 fusion.46
  123.4 4.7 %collective-permute-done.1 = bf16[8,16,512]{2,1,0:T(8,128)(2,1)S(1)} collective-permute-done((bf16[8,16,512]{2,1,0:T(8,128)(2,1)S(1)}, bf16[8,16,512]{2,1,0:T(8,128)(2,1)S(1)}, u32[]{:S(2)}, u32[]{:S(2)}) %collective-permute-start.1) | collective-permute-done | bytes 131104 | tf_op jit(solution)/shard_map/ppermute | solution.py:14
  128.1 0.3 fusion.28
  128.4 0.1 rsqrt.20
  128.5 2.0 %fusion.15 = bf16[128,512]{1,0:T(8,128)(2,1)} fusion(bf16[512,512]{1,0:T(8,128)(2,1)} %param.20, bf16[16,8,512]{2,1,0:T(8,128)(2,1)S(1)} %get-tuple-element.6, f32[512]{0:T(512)} %param.19, f32[128]{0:T(128)S(1)} %rsqrt.20), kind=kOutput, calls=%fused_computation.21 | convolution fusion | flops 67502080 | bytes 788992 | tf_op jit(solution)/shard_map/dot_general | solution.py:117
  130.4 1.2 reshape_transpose_reshape_reshape.10
  131.6 2.0 %convolution_convert_fusion.3 = bf16[128,512]{1,0:T(8,128)(2,1)} fusion(bf16[512,512]{1,0:T(8,128)(2,1)} %param.22, bf16[16,8,512]{2,1,0:T(8,128)(2,1)S(1)} %get-tuple-element.6, f32[512]{0:T(512)S(1)} %copy-done.7, f32[128]{0:T(128)S(1)} %rsqrt.20), kind=kOutput, calls=%fused_computation.23 | convolution fusion | flops 67436544 | bytes 788992 | tf_op jit(solution)/shard_map/dot_general | solution.py:121
  133.6 1.8 reshape_transpose_reshape_reshape.9
  135.4 2.0 %convolution_convert_fusion.2 = bf16[128,512]{1,0:T(8,128)(2,1)} fusion(bf16[512,512]{1,0:T(8,128)(2,1)} %param.21, bf16[16,8,512]{2,1,0:T(8,128)(2,1)S(1)} %get-tuple-element.6, f32[512]{0:T(512)S(1)} %copy-done.7, f32[128]{0:T(128)S(1)} %rsqrt.20), kind=kOutput, calls=%fused_computation.22 | convolution fusion | flops 67436544 | bytes 788992 | tf_op jit(solution)/shard_map/dot_general | solution.py:120
  137.4 1.8 reshape_transpose_reshape_reshape.11
  139.2 0.8 copy.44
  140.0 2.0 %fusion.53 = (f32[2,8,64]{2,1,0:T(8,128)S(1)}, f32[2,8,64,64]{2,3,1,0:T(8,128)}) fusion(bf16[2,64,8,64]{3,2,1,0:T(8,128)(2,1)} %reshape_transpose_reshape_reshape.11, bf16[2,64,8,64]{3,2,1,0:T(8,128)(2,1)S(1)} %reshape_transpose_reshape_reshape.10, pred[2,64,64]{1,2,0:T(8,128)(4,1)} %broadcast_compare_fusion), kind=kOutput, calls=%fused_computation.88 | convolution fusion | flops 8518656 | bytes 536576 | tf_op jit(solution)/shard_map/wqhd,wkhd->whqk/dot_general | solution.py:58
  142.0 3.1 %pad_maximum_fusion = bf16[12,128,1024]{2,1,0:T(8,128)(2,1)} fusion(bf16[4,128,1024]{2,1,0:T(8,128)(2,1)} %collective-permute-done.3, bf16[4,128,1024]{2,1,0:T(8,128)(2,1)S(1)} %copy-done.2, bf16[4,128,1024]{2,1,0:T(8,128)(2,1)} %collective-permute-done.2), kind=kLoop, calls=%fused_computation.4 | loop fusion | flops 3145728 | bytes 6291456 | tf_op jit(solution)/shard_map/concatenate | solution.py:26
  145.1 3.9 %gather_fusion = bf16[8,128,1024]{2,1,0:T(8,128)(2,1)} fusion(bf16[12,128,1024]{2,1,0:T(8,128)(2,1)} %pad_maximum_fusion, s32[1024]{0:T(1024)S(1)} %pad_clamp_fusion), kind=kCustom, calls=%fused_computation | custom fusion | bytes 4194336 | tf_op jit(solution)/shard_map/jit(_take)/gather | solution.py:129
  149.0 1.9 %bitcast_select_fusion = bf16[1024,1024]{1,0:T(8,128)(2,1)S(1)} fusion(bf16[8,128,1024]{2,1,0:T(8,128)(2,1)} %gather_fusion, pred[1024]{0:T(1024)(128)(4,1)S(1)} %broadcast_bitcast_fusion), kind=kLoop, calls=%fused_computation.7 | loop fusion | flops 1048576 | bytes 4195328 | tf_op jit(solution)/shard_map/jit(_take)/select_n | solution.py:129
  150.9 2.3 %convolution_convert_fusion = bf16[1024,512]{0,1:T(8,128)(2,1)} fusion(bf16[1024,1024]{1,0:T(8,128)(2,1)S(1)} %bitcast_select_fusion, bf16[1024,512]{1,0:T(8,128)(2,1)S(1)} %copy-done.9), kind=kOutput, calls=%fused_computation.10 | convolution fusion | flops 1074266112 | bytes 4194304 | tf_op jit(solution)/shard_map/dot_general | solution.py:133
  153.3 1.3 convolution_convert_fusion.1
  154.6 2.6 %fusion.54 = f32[8,1024,128]{1,2,0} fusion(bf16[8,64,128]{1,2,0:T(8,128)(2,1)S(1)} %bitcast.68, bf16[1024,8,64]{0,2,1:T(8,128)(2,1)S(1)} %bitcast.67), kind=kOutput, calls=%fused_computation.89 | convolution fusion | flops 134217728 | bytes 5373952
  157.2 2.5 %reduce_max.19 = f32[2,8,64]{2,0,1:T(2,128)S(1)} reduce(f32[2,8,64,1024]{3,2,0,1:T(8,128)} %bitcast.65, f32[]{:T(128)} %constant.69.clone.1), dimensions={3}, to_apply=%region_2.3 | reduce | flops 1047552 | bytes 4198404 | tf_op jit(solution)/shard_map/reduce_max | solution.py:66
  159.8 3.1 %fusion = f32[2,8,64]{2,0,1:T(2,128)S(1)} fusion(f32[2,8,64,1024]{3,2,0,1:T(8,128)} %bitcast.66, f32[2,8,64]{2,0,1:T(2,128)S(1)} %copy.46), kind=kLoop, calls=%fused_computation.3 | loop fusion | flops 2096128 | bytes 4202496 | tf_op jit(solution)/shard_map/reduce_sum | solution.py:70
  162.9 0.1 fusion.24
  163.0 0.3 convolution_bitcast_fusion
  163.3 0.9 copy-done.11
  164.2 1.5 fusion.11
  165.7 0.2 copy.52
  165.9 0.2 reshape_reshape_transpose_reshape.3
  166.2 0.3 multiply_reduce_fusion
  166.5 0.5 fusion.34
  167.0 3.1 %fusion.17 = bf16[16,8,512]{2,1,0:T(8,128)(2,1)S(1)} fusion(f32[128,512]{1,0:T(8,128)S(1)} %get-tuple-element.12, bf16[2048,512]{1,0:T(8,128)(2,1)} %param.29, bf16[512,2048]{1,0:T(8,128)(2,1)} %param.28, f32[128,2048]{1,0:T(8,128)S(1)} %fusion.34, f32[512]{0:T(512)S(1)} %copy-done.8, f32[128]{0:T(128)S(1)} %add_rsqrt_fusion.1), kind=kOutput, calls=%fused_computation.25 | convolution fusion | flops 538771456 | bytes 5638656 | tf_op jit(solution)/shard_map/dot_general | solution.py:157
  170.1 1.9 %collective-permute-start.4 = (bf16[16,8,512]{2,1,0:T(8,128)(2,1)S(1)}, bf16[16,8,512]{2,1,0:T(8,128)(2,1)S(1)}, u32[]{:S(2)}, u32[]{:S(2)}) collective-permute-start(bf16[16,8,512]{2,1,0:T(8,128)(2,1)S(1)} %fusion.17), channel_id=1, source_target_pairs={{0,1},{1,2},{2,3},{3,4},{4,5},{5,6},{6,7},{7,0},{8,9},{9,10},{10,1... | collective-permute-start | bytes 393224 | tf_op jit(solution)/shard_map/ppermute | solution.py:14
  172.0 1.9 %collective-permute-done.4 = bf16[16,8,512]{2,1,0:T(8,128)(2,1)S(1)} collective-permute-done((bf16[16,8,512]{2,1,0:T(8,128)(2,1)S(1)}, bf16[16,8,512]{2,1,0:T(8,128)(2,1)S(1)}, u32[]{:S(2)}, u32[]{:S(2)}) %collective-permute-start.4) | collective-permute-done | bytes 131104 | tf_op jit(solution)/shard_map/ppermute | solution.py:14
  174.0 1.9 %collective-permute-start.5 = (bf16[8,16,512]{2,1,0:T(8,128)(2,1)S(1)}, bf16[8,16,512]{2,1,0:T(8,128)(2,1)S(1)}, u32[]{:S(2)}, u32[]{:S(2)}) collective-permute-start(bf16[8,16,512]{2,1,0:T(8,128)(2,1)S(1)} %pad_maximum_fusion.1), channel_id=1, source_target_pairs={{0,8},{8,16},{16,24},{24,32},{32,40},{40,48},{48,56},{56,64},{64,7... | collective-permute-start | bytes 393224 | tf_op jit(solution)/shard_map/ppermute | solution.py:14
  178.5 12.4 %collective-permute-done.5 = bf16[8,16,512]{2,1,0:T(8,128)(2,1)S(1)} collective-permute-done((bf16[8,16,512]{2,1,0:T(8,128)(2,1)S(1)}, bf16[8,16,512]{2,1,0:T(8,128)(2,1)S(1)}, u32[]{:S(2)}, u32[]{:S(2)}) %collective-permute-start.5) | collective-permute-done | bytes 131104 | tf_op jit(solution)/shard_map/ppermute | solution.py:14
  190.9 0.9 fusion.35
  (38 shorter events, 0.2 us)
Async XLA Ops:
  0.0 166.5 %copy-start = (bf16[512,2048]{1,0:T(8,128)(2,1)S(1)}, bf16[512,2048]{1,0:T(8,128)(2,1)}, u32[]{:S(2)}) copy-start(bf16[512,2048]{1,0:T(8,128)(2,1)} %param.27) | copy-start | bytes 6291460
  0.0 131.6 %copy-start.7 = (f32[512]{0:T(512)S(1)}, f32[512]{0:T(512)}, u32[]{:S(2)}) copy-start(f32[512]{0:T(512)} %param.19) | copy-start | bytes 6148
  0.0 142.0 %collective-permute-start.2 = (bf16[4,128,1024]{2,1,0:T(8,128)(2,1)}, bf16[4,128,1024]{2,1,0:T(8,128)(2,1)}, u32[]{:S(2)}, u32[]{:S(2)}) collective-permute-start(bf16[4,128,1024]{2,1,0:T(8,128)(2,1)} %param.16), channel_id=1, source_target_pairs={{0,8},{8,16},{16,24},{24,32},{32,40},{40,48},{48,56},{56,64},{64,7... | collective-permute-start | bytes 3145736 | tf_op jit(solution)/shard_map/ppermute | solution.py:24
  4.1 137.9 %collective-permute-start.3 = (bf16[4,128,1024]{2,1,0:T(8,128)(2,1)}, bf16[4,128,1024]{2,1,0:T(8,128)(2,1)}, u32[]{:S(2)}, u32[]{:S(2)}) collective-permute-start(bf16[4,128,1024]{2,1,0:T(8,128)(2,1)} %param.16), channel_id=1, source_target_pairs={{8,0},{16,8},{24,16},{32,24},{40,32},{48,40},{56,48},{64,56},{72,6... | collective-permute-start | bytes 3145736 | tf_op jit(solution)/shard_map/ppermute | solution.py:25
  20.0 96.8 %collective-permute-start = (bf16[16,8,512]{2,1,0:T(8,128)(2,1)}, bf16[16,8,512]{2,1,0:T(8,128)(2,1)S(1)}, u32[]{:S(2)}, u32[]{:S(2)}) collective-permute-start(bf16[16,8,512]{2,1,0:T(8,128)(2,1)} %param.15), channel_id=1, source_target_pairs={{0,7},{1,0},{2,1},{3,2},{4,3},{5,4},{6,5},{7,6},{8,15},{9,8},{10,9... | collective-permute-start | bytes 393224 | tf_op jit(solution)/shard_map/ppermute | solution.py:14
  116.8 11.3 %collective-permute-start.1 = (bf16[8,16,512]{2,1,0:T(8,128)(2,1)S(1)}, bf16[8,16,512]{2,1,0:T(8,128)(2,1)S(1)}, u32[]{:S(2)}, u32[]{:S(2)}) collective-permute-start(bf16[8,16,512]{2,1,0:T(8,128)(2,1)S(1)} %slice.18), channel_id=1, source_target_pairs={{0,504},{8,0},{16,8},{24,16},{32,24},{40,32},{48,40},{56,48},{64,5... | collective-permute-start | bytes 393224 | tf_op jit(solution)/shard_map/ppermute | solution.py:14
  130.4 11.6 %copy-start.2 = (bf16[4,128,1024]{2,1,0:T(8,128)(2,1)S(1)}, bf16[4,128,1024]{2,1,0:T(8,128)(2,1)}, u32[]{:S(2)}) copy-start(bf16[4,128,1024]{2,1,0:T(8,128)(2,1)} %param.16) | copy-start | bytes 3145732
  149.0 2.0 %copy-start.9 = (bf16[1024,512]{1,0:T(8,128)(2,1)S(1)}, bf16[1024,512]{1,0:T(8,128)(2,1)}, u32[]{:S(2)}) copy-start(bf16[1024,512]{1,0:T(8,128)(2,1)} %param.25) | copy-start | bytes 3145732
  150.9 2.3 %copy-start.10 = (bf16[1024,512]{1,0:T(8,128)(2,1)S(1)}, bf16[1024,512]{1,0:T(8,128)(2,1)}, u32[]{:S(2)}) copy-start(bf16[1024,512]{1,0:T(8,128)(2,1)} %param.24) | copy-start | bytes 3145732
  153.3 1.3 copy-start.3
  157.2 5.7 %copy-start.4 = (f32[2,8,64,64]{2,3,1,0:T(8,128)S(1)}, f32[2,8,64,64]{2,3,1,0:T(8,128)}, u32[]{:S(2)}) copy-start(f32[2,8,64,64]{2,3,1,0:T(8,128)} %get-tuple-element.10) | copy-start | bytes 786436
  159.8 3.3 %copy-start.6 = (bf16[2,64,8,64]{3,2,1,0:T(8,128)(2,1)S(1)}, bf16[2,64,8,64]{3,2,1,0:T(8,128)(2,1)}, u32[]{:S(2)}) copy-start(bf16[2,64,8,64]{3,2,1,0:T(8,128)(2,1)} %reshape_transpose_reshape_reshape.9) | copy-start | bytes 393220
  159.8 3.5 %copy-start.1 = (f32[8,1024,128]{1,2,0:S(1)}, f32[8,1024,128]{1,2,0}, u32[]{:S(2)}) copy-start(f32[8,1024,128]{1,2,0} %fusion.54) | copy-start | bytes 12582916
  162.9 1.3 copy-start.11
  164.2 2.0 %copy-start.5 = (bf16[512,512]{1,0:T(8,128)(2,1)S(1)}, bf16[512,512]{1,0:T(8,128)(2,1)}, u32[]{:S(2)}) copy-start(bf16[512,512]{1,0:T(8,128)(2,1)} %param.23) | copy-start | bytes 1572868
  164.2 2.3 %copy-start.8 = (f32[512]{0:T(512)S(1)}, f32[512]{0:T(512)}, u32[]{:S(2)}) copy-start(f32[512]{0:T(512)} %param.26) | copy-start | bytes 6148
  170.1 3.9 %collective-permute-start.4 = (bf16[16,8,512]{2,1,0:T(8,128)(2,1)S(1)}, bf16[16,8,512]{2,1,0:T(8,128)(2,1)S(1)}, u32[]{:S(2)}, u32[]{:S(2)}) collective-permute-start(bf16[16,8,512]{2,1,0:T(8,128)(2,1)S(1)} %fusion.17), channel_id=1, source_target_pairs={{0,1},{1,2},{2,3},{3,4},{4,5},{5,6},{6,7},{7,0},{8,9},{9,10},{10,1... | collective-permute-start | bytes 393224 | tf_op jit(solution)/shard_map/ppermute | solution.py:14
  174.0 16.9 %collective-permute-start.5 = (bf16[8,16,512]{2,1,0:T(8,128)(2,1)S(1)}, bf16[8,16,512]{2,1,0:T(8,128)(2,1)S(1)}, u32[]{:S(2)}, u32[]{:S(2)}) collective-permute-start(bf16[8,16,512]{2,1,0:T(8,128)(2,1)S(1)} %pad_maximum_fusion.1), channel_id=1, source_target_pairs={{0,8},{8,16},{16,24},{24,32},{32,40},{40,48},{48,56},{56,64},{64,7... | collective-permute-start | bytes 393224 | tf_op jit(solution)/shard_map/ppermute | solution.py:14
where the time goes:
time: 194 us; the launch traced here: 192 us
  waiting for transfers between devices  108 us (56%)
  starting transfers between devices  28.6 us (15%)
  matrix products  19.9 us (10%)
  other arithmetic  15.2 us (8%)
  local copies, waits for them, and re-layouts  13.5 us (7%)
  between operations  6.89 us (4%)
    ppermute x4, waiting for transfers between devices, passed_along(): return lax.ppermute(x, axis, [(i, (i + by) % count) for i in range(count)])  108 us
    ppermute x1, starting transfers between devices, with_halo(): after = lax.ppermute(initial, axis, down)  15.9 us
    ppermute x4, starting transfers between devices, passed_along(): return lax.ppermute(x, axis, [(i, (i + by) % count) for i in range(count)])  8.67 us
    another operation x4, local copies, waits for them, and re-layouts, to_windows(): return reordered.reshape((lead_count * across, WS * WS) + source.shape[2:])  5.55 us
    ppermute x1, starting transfers between devices, with_halo(): before = lax.ppermute(last, axis, up)  4.07 us
    gather x1, local copies, waits for them, and re-layouts, local(): chosen = jnp.take(nearby, local_index, axis=0).reshape(-1, CW)  3.91 us
  transfers between devices with their start and end apart: 6, of which 4 were waited for; matrix products, arithmetic and copies ran while one was open for 10% of the time, Pallas kernels for 0%

commit v1 on v0

v1 whole, which is shorter than its diff:
```python
import jax
import jax.numpy as jnp
from jax import lax
from jax.experimental import pallas as pl
from jax.experimental.pallas import tpu as pltpu
from jax.sharding import PartitionSpec as P

HEADS = 8
HD = 64
WS = 8
EPS = 1e-06
F32 = jnp.float32
BF16 = jnp.bfloat16
LOW = -1e30
VMEM_LIMIT = 40 * 1024 * 1024


def iota(shape, dim):
    return lax.broadcasted_iota(jnp.int32, shape, dim)


def rms(x, gain):
    mean_square = jnp.mean(x * x, axis=-1, keepdims=True)
    return x * lax.rsqrt(mean_square + EPS) * gain


def local_blocks(ids, table, per_strip, total):
    first = (ids[0] - 1) * per_strip
    return [lax.rem(table[i] - first + 2 * total, total) for i in range(table.shape[0])]


def project_kernel(total, ids, table, coarse, w_k, w_v, fine, gain, w_q, kv, pay_o, pay_e, q_nat, q_t):
    step = pl.program_id(0)
    rows = coarse.shape[0]
    odd_head = lax.rem(ids[1], 2) == 1
    low = iota((rows, 128), 1) < HD
    tokens = coarse[...]
    key = jnp.dot(tokens, w_k[...], preferred_element_type=F32)
    value = jnp.dot(tokens, w_v[...], preferred_element_type=F32)
    key = jnp.where(odd_head, pltpu.roll(key, HD, 1), key)
    value = jnp.where(odd_head, value, pltpu.roll(value, HD, 1))
    both = jnp.where(low, key, value).astype(BF16)
    at = pl.ds(pl.multiple_of(step * rows, rows), rows)
    kv[at, :] = both
    pay_o[at, :] = both
    pay_e[at, :] = both

    @pl.when(step == 0)
    def _():
        x = fine[...]
        n_tok, width = x.shape
        base = kv.shape[0]
        half = n_tok // 2
        even = lax.rem(ids[0], 2) == 0
        top, bottom = x[:half], x[half:]
        for c in range(width // 128):
            lanes = slice(128 * c, 128 * c + 128)
            at_c = slice(base + half * c, base + half * (c + 1))
            t_c, b_c = top[:, lanes], bottom[:, lanes]
            pay_o[at_c, :] = jnp.where(even, t_c, b_c)
            pay_e[at_c, :] = jnp.where(even, b_c, t_c)
        chosen = local_blocks(ids, table, base // 128, total)
        lane = iota((16, 128), 1)
        marks = jnp.zeros((16, 128), F32)
        for i, b in enumerate(chosen):
            marks = jnp.where(lane == i, b.astype(F32), marks)
        end = base + half * (width // 128)
        pay_o[end : end + 16, :] = marks.astype(BF16)
        pay_e[end : end + 16, :] = marks.astype(BF16)
        normed = rms(x.astype(F32), gain[...]).astype(BF16)
        q = jnp.dot(normed, w_q[...], preferred_element_type=F32) * (1.0 / HD**0.5)
        q_nat[...] = q.astype(BF16)
        q_t[...] = q.T.astype(BF16).reshape(q_t.shape)


def project(ids, table, coarse, w_k, w_v, fine, gain, w_q, total):
    n_coarse, cw = coarse.shape
    n_tok, width = fine.shape
    steps = n_coarse // 128
    pay_rows = n_coarse + (n_tok // 2) * (width // 128) + 16
    whole = lambda *shape: pl.BlockSpec(shape, lambda i, *_: (0,) * len(shape))
    head_cols = pl.BlockSpec((cw, 128), lambda i, ids, table: (0, ids[1] // 2))
    return pl.pallas_call(
        lambda *refs: project_kernel(total, *refs),
        grid_spec=pltpu.PrefetchScalarGridSpec(
            num_scalar_prefetch=2,
            grid=(steps,),
            in_specs=[
                pl.BlockSpec((128, cw), lambda i, *_: (i, 0)),
                head_cols,
                head_cols,
                whole(n_tok, width),
                whole(1, width),
                whole(width, width),
            ],
            out_specs=[
                whole(n_coarse, 128),
                whole(pay_rows, 128),
                whole(pay_rows, 128),
                whole(n_tok, width),
                whole(HEADS, HD, n_tok),
            ],
        ),
        out_shape=[
            jax.ShapeDtypeStruct((n_coarse, 128), BF16),
            jax.ShapeDtypeStruct((pay_rows, 128), BF16),
            jax.ShapeDtypeStruct((pay_rows, 128), BF16),
            jax.ShapeDtypeStruct((n_tok, width), BF16),
            jax.ShapeDtypeStruct((HEADS, HD, n_tok), BF16),
        ],
        compiler_params=pltpu.CompilerParams(vmem_limit_bytes=VMEM_LIMIT),
        cost_estimate=pl.CostEstimate(flops=350_000_000, bytes_accessed=4_000_000, transcendentals=0),
        name="project",
    )(ids, table, coarse, w_k, w_v, fine, gain, w_q)


def stack_kernel(ids, base, got_o, got_e, fine, out):
    n_tok, width = fine.shape
    half = n_tok // 2
    out[half : half + n_tok, :] = fine[...]
    even = lax.rem(ids[0], 2) == 0
    for c in range(width // 128):
        lanes = slice(128 * c, 128 * c + 128)
        at = slice(base + half * c, base + half * (c + 1))
        a, b = got_o[at, :], got_e[at, :]
        out[0:half, lanes] = jnp.where(even, a, b)
        out[half + n_tok :, lanes] = jnp.where(even, b, a)


def stack_rows(ids, got_o, got_e, fine, base):
    n_tok, width = fine.shape
    vmem = pl.BlockSpec(memory_space=pltpu.VMEM)
    return pl.pallas_call(
        lambda ids, a, b, x, out: stack_kernel(ids, base, a, b, x, out),
        in_specs=[pl.BlockSpec(memory_space=pltpu.SMEM), vmem, vmem, vmem],
        out_specs=vmem,
        out_shape=jax.ShapeDtypeStruct((2 * n_tok, width), BF16),
        compiler_params=pltpu.CompilerParams(vmem_limit_bytes=VMEM_LIMIT),
        cost_estimate=pl.CostEstimate(flops=0, bytes_accessed=1_000_000, transcendentals=0),
        name="stack_rows",
    )(ids, got_o, got_e, fine)


def window_kernel(last, ids, shifts, left, mid, right, q, gain, w_k, w_v, out, lse):
    span = left.shape[0]
    side = span - 64
    strip, member = ids[0], ids[1]
    shift_row, shift_col = shifts[0], shifts[1]
    fine = jnp.concatenate([left[...], mid[...], right[...]], axis=0).astype(F32)
    normed = rms(fine, gain[...]).astype(BF16)
    keys = jnp.dot(normed, w_k[...], preferred_element_type=F32).astype(BF16)
    values = jnp.dot(normed, w_v[...], preferred_element_type=F32).astype(BF16)
    shape = (128, 3 * side)
    query = lax.rem(iota(shape, 0), 64)
    column_q = lax.rem(query, 8)
    key = iota(shape, 1)
    part = (key >= side).astype(jnp.int32) + (key >= 2 * side).astype(jnp.int32)
    within = key - part * side
    column_k = (part - 1) * 8 + lax.rem(within, 8)
    same_col = lax.shift_right_arithmetic(column_q - shift_col + 16, 3) == lax.shift_right_arithmetic(
        column_k - shift_col + 16, 3
    )
    wrap_col = ((column_k < 0) & (member == 0)) | ((column_k > 7) & (member == last[1]))
    lane = iota((64, 128), 1)
    low = lane < HD
    low_rows = iota((128, 128), 0) < 64
    low_lanes = iota((128, 128), 1) < HD
    own = low_rows == low_lanes
    for half in range(2):
        row_q = 8 * half + lax.shift_right_arithmetic(query, 3)
        row_k = 8 * half - 8 + lax.shift_right_arithmetic(within, 3)
        same_row = lax.shift_right_arithmetic(row_q - shift_row + 16, 3) == lax.shift_right_arithmetic(
            row_k - shift_row + 16, 3
        )
        wrap_row = ((row_k < 0) & (strip == 0)) | ((row_k > 15) & (strip == last[0]))
        seen = same_row & same_col & jnp.logical_not(wrap_row | wrap_col)
        rows = slice(64 * half, 64 * half + 64)
        pick = lambda a: jnp.concatenate(
            [a[span * b + 64 * half : span * b + 64 * half + side] for b in range(3)], axis=0
        )
        keys_h, values_h = pick(keys), pick(values)
        marks = jnp.zeros((64, 128), F32)
        for pair in range(HEADS // 2):
            lanes = slice(128 * pair, 128 * pair + 128)
            q_pair = q[rows, lanes]
            q_both = jnp.concatenate([q_pair, q_pair], axis=0)
            q_both = jnp.where(own, q_both, jnp.zeros_like(q_both))
            score = lax.dot_general(
                q_both, keys_h[:, lanes], (((1,), (1,)), ((), ())), preferred_element_type=F32
            )
            score = jnp.where(seen, score, LOW)
            peak = jnp.max(score, axis=-1, keepdims=True)
            weight = jnp.exp(score - peak)
            total = jnp.sum(weight, axis=-1, keepdims=True)
            mixed = jnp.dot(weight.astype(BF16), values_h[:, lanes], preferred_element_type=F32) / total
            out[rows, lanes] = jnp.where(low, mixed[:64], mixed[64:])
            level = peak + jnp.log(total)
            marks = jnp.where(lane == 2 * pair, level[:64], marks)
            marks = jnp.where(lane == 2 * pair + 1, level[64:], marks)
        lse[rows, :] = marks


def window_attention(ids, shifts, left, mid, right, q, gain, w_k, w_v, last):
    n_tok, width = q.shape
    vmem = pl.BlockSpec(memory_space=pltpu.VMEM)
    smem = pl.BlockSpec(memory_space=pltpu.SMEM)
    return pl.pallas_call(
        lambda *refs: window_kernel(last, *refs),
        in_specs=[smem, smem] + [vmem] * 7,
        out_specs=[vmem, vmem],
        out_shape=[
            jax.ShapeDtypeStruct((n_tok, width), F32),
            jax.ShapeDtypeStruct((n_tok, 128), F32),
        ],
        compiler_params=pltpu.CompilerParams(vmem_limit_bytes=VMEM_LIMIT),
        cost_estimate=pl.CostEstimate(flops=2_000_000_000, bytes_accessed=3_000_000, transcendentals=600_000),
        name="window_attention",
    )(ids, shifts, left, mid, right, q, gain, w_k, w_v)


def coarse_kernel(total, ids, shifts, table, table_before, q_t, own, got_o, got_e, far_even, far_odd, out, store):
    n_own = own.shape[0]
    per_strip = n_own // 128
    even = lax.rem(ids[0], 2) == 0
    store[2 * per_strip : 3 * per_strip] = own[...].reshape(per_strip, 128, 128)

    @pl.when(even)
    def _():
        store[0:per_strip] = far_even[...].reshape(per_strip, 128, 128)
        store[per_strip : 2 * per_strip] = got_o[0:n_own, :].reshape(per_strip, 128, 128)
        store[3 * per_strip :] = got_e[0:n_own, :].reshape(per_strip, 128, 128)

    @pl.when(jnp.logical_not(even))
    def _():
        store[0:per_strip] = far_odd[0:n_own, :].reshape(per_strip, 128, 128)
        store[per_strip : 2 * per_strip] = got_e[0:n_own, :].reshape(per_strip, 128, 128)
        store[3 * per_strip :] = got_o[0:n_own, :].reshape(per_strip, 128, 128)

    here = [b + per_strip for b in local_blocks(ids, table, per_strip, total)]
    before = [table_before[i] for i in range(table_before.shape[0])]
    kv_here = jnp.concatenate([store[b] for b in here], axis=0)
    kv_before = jnp.concatenate([store[b] for b in before], axis=0)
    kv_here_t = kv_here.astype(F32).T.astype(BF16)
    kv_before_t = kv_before.astype(F32).T.astype(BF16)
    shift_row = shifts[0]
    lane = lax.rem(iota((1, 256), 1), 128)
    earlier = lane < WS * shift_row
    line = iota((16, 256), 0)
    members = q_t.shape[0]
    for p in range(members // 2):
        q = jnp.concatenate([q_t[2 * p], q_t[2 * p + 1]], axis=1)
        q = jnp.concatenate([q, jnp.zeros_like(q)], axis=0)
        score = jnp.where(
            earlier,
            jnp.dot(kv_before, q, preferred_element_type=F32),
            jnp.dot(kv_here, q, preferred_element_type=F32),
        )
        peak = jnp.max(score, axis=0, keepdims=True)
        weight = jnp.exp(score - peak)
        sums = jnp.sum(weight, axis=0, keepdims=True)
        weight = weight.astype(BF16)
        mixed = jnp.where(
            earlier,
            jnp.dot(kv_before_t, weight, preferred_element_type=F32),
            jnp.dot(kv_here_t, weight, preferred_element_type=F32),
        )
        mixed = (mixed[HD:] / sums).astype(BF16)
        level = peak + jnp.log(sums)
        first = level.astype(BF16).astype(F32)
        second = (level - first).astype(BF16).astype(F32)
        third = level - first - second
        marks = jnp.where(line == 0, first, jnp.where(line == 1, second, jnp.where(line == 2, third, 0.0)))
        marks = marks.astype(BF16)
        for k in range(2):
            lanes = slice(128 * k, 128 * k + 128)
            out[2 * p + k, 0:HD, :] = mixed[:, lanes]
            out[2 * p + k, HD : HD + 16, :] = marks[:, lanes]


def coarse_attention(ids, shifts, table, table_before, q_t, own, got_o, got_e, far_even, far_odd, total):
    vmem = pl.BlockSpec(memory_space=pltpu.VMEM)
    smem = pl.BlockSpec(memory_space=pltpu.SMEM)
    members, _, n_tok = q_t.shape
    return pl.pallas_call(
        lambda *refs: coarse_kernel(total, *refs),
        in_specs=[smem] * 4 + [vmem] * 6,
        out_specs=vmem,
        out_shape=jax.ShapeDtypeStruct((members, HD + 16, n_tok), BF16),
        scratch_shapes=[pltpu.VMEM((4 * own.shape[0] // 128, 128, 128), BF16)],
        compiler_params=pltpu.CompilerParams(vmem_limit_bytes=VMEM_LIMIT),
        cost_estimate=pl.CostEstimate(flops=1_600_000_000, bytes_accessed=1_500_000, transcendentals=1_000_000),
        name="coarse_attention",
    )(ids, shifts, table, table_before, q_t, own, got_o, got_e, far_even, far_odd)


def finish_kernel(fine, near, near_lse, coarse, w_out, gain, w_gate, w_up, w_down, out, mid, normed, acc):
    step = pl.program_id(0)

    @pl.when(step == 0)
    def _():
        heads = coarse.shape[0]
        far = jnp.concatenate([coarse[h, 0:HD, :].astype(F32) for h in range(heads)], axis=0).T
        marks = [coarse[h, HD : HD + 16, :].astype(F32) for h in range(heads)]
        level = jnp.concatenate([m[0:1] + m[1:2] + m[2:3] for m in marks], axis=0).T
        diff = near_lse[:, 0:heads] - level
        share = 1.0 / (1.0 + jnp.exp(diff))
        share = jnp.concatenate(
            [jnp.broadcast_to(share[:, h : h + 1], (share.shape[0], HD)) for h in range(heads)], axis=1
        )
        head_out = (near[...] * (1.0 - share) + far * share).astype(BF16)
        m = fine[...].astype(F32) + jnp.dot(head_out, w_out[...], preferred_element_type=F32)
        mid[...] = m
        normed[...] = rms(m, gain[...]).astype(BF16)
        acc[...] = jnp.zeros_like(acc)

    gate = jnp.dot(normed[...], w_gate[...], preferred_element_type=F32)
    up = jnp.dot(normed[...], w_up[...], preferred_element_type=F32)
    hidden = (gate * (1.0 / (1.0 + jnp.exp(-gate))) * up).astype(BF16)
    acc[...] += jnp.dot(hidden, w_down[...], preferred_element_type=F32)

    @pl.when(step == pl.num_programs(0) - 1)
    def _():
        out[...] = (mid[...] + acc[...]).astype(BF16)


def finish(fine, near, near_lse, coarse, w_out, gain, w_gate, w_up, w_down):
    n_tok, width = fine.shape
    ff = w_gate.shape[1]
    chunk = 512
    whole = lambda *shape: pl.BlockSpec(shape, lambda i: (0,) * len(shape))
    return pl.pallas_call(
        finish_kernel,
        grid=(ff // chunk,),
        in_specs=[
            whole(n_tok, width),
            whole(n_tok, width),
            whole(*near_lse.shape),
            whole(*coarse.shape),
            whole(width, width),
            whole(1, width),
            pl.BlockSpec((width, chunk), lambda i: (0, i)),
            pl.BlockSpec((width, chunk), lambda i: (0, i)),
            pl.BlockSpec((chunk, width), lambda i: (i, 0)),
        ],
        out_specs=whole(n_tok, width),
        out_shape=jax.ShapeDtypeStruct((n_tok, width), BF16),
        scratch_shapes=[
            pltpu.VMEM((n_tok, width), F32),
            pltpu.VMEM((n_tok, width), BF16),
            pltpu.VMEM((n_tok, width), F32),
        ],
        compiler_params=pltpu.CompilerParams(vmem_limit_bytes=VMEM_LIMIT),
        cost_estimate=pl.CostEstimate(flops=900_000_000, bytes_accessed=7_500_000, transcendentals=300_000),
        name="finish",
    )(fine, near, near_lse, coarse, w_out, gain, w_gate, w_up, w_down)


def local(
    fine,
    coarse,
    block_table,
    shifts,
    attn_gain,
    w_query,
    w_key,
    w_value,
    w_out,
    coarse_key,
    coarse_value,
    mlp_gain,
    w_gate,
    w_up,
    w_down,
):
    strips = lax.axis_size("tile")
    members = lax.axis_size("narrow")
    strip = lax.axis_index("tile").astype(jnp.int32)
    member = lax.axis_index("narrow").astype(jnp.int32)
    ids = jnp.stack([strip, member])
    rows, columns, width = fine.shape
    blocks, block_tokens, cw = coarse.shape
    total = blocks * strips
    n_own = blocks * block_tokens
    flat = fine.reshape(rows * columns, width)
    table = block_table.reshape(-1)
    gain = attn_gain.reshape(1, width)

    kv, pay_o, pay_e, q, q_t = project(
        ids, table, coarse.reshape(n_own, cw), coarse_key, coarse_value, flat, gain, w_query, total
    )
    odd_pairs = [(i, (i - 1) % strips if i % 2 == 0 else (i + 1) % strips) for i in range(strips)]
    even_pairs = [(i, i ^ 1) for i in range(strips)]
    got_o = lax.ppermute(pay_o, "tile", odd_pairs)
    got_e = lax.ppermute(pay_e, "tile", even_pairs)
    far_even = lax.ppermute(kv, "tile", [(i, (i + 2) % strips) for i in range(0, strips, 2)])
    q_head = lax.all_to_all(q_t, "narrow", 0, 0, tiled=True)
    far_odd = lax.ppermute(got_o, "tile", [(i, i + 1) for i in range(0, strips, 2)])

    stacked = stack_rows(ids, got_o, got_e, flat, n_own)
    right_of = lax.ppermute(stacked, "narrow", [(i, (i - 1) % members) for i in range(members)])
    left_of = lax.ppermute(stacked, "narrow", [(i, (i + 1) % members) for i in range(members)])
    mark_row = n_own + rows * columns // 2 * (width // 128)
    table_before = jnp.where(strip % 2 == 0, got_o[mark_row, :8], got_e[mark_row, :8]).astype(jnp.int32)

    far = coarse_attention(
        ids, shifts, table, table_before, q_head, kv, got_o, got_e, far_even, far_odd, total
    )
    far = lax.all_to_all(far, "narrow", 0, 0, tiled=True)
    near, near_lse = window_attention(
        ids, shifts, left_of, stacked, right_of, q, gain, w_key, w_value, (strips - 1, members - 1)
    )
    out = finish(
        flat, near, near_lse, far, w_out, mlp_gain.reshape(1, width), w_gate, w_up, w_down
    )
    return out.reshape(rows, columns, width)


def solution(mesh):
    placed = (
        P("tile", "narrow", None),
        P("tile", None, None),
        P("tile", None),
    ) + (P(),) * 12
    return jax.shard_map(
        local, mesh=mesh, in_specs=placed, out_specs=P("tile", "narrow", None), check_vma=False
    )
```

time: 194 us -> 95 us (0.49)
  the two profiles are of different devices: /device:TPU:1 before, /device:TPU:2 now
where the time goes in v1:
time: 95 us; the launch traced here: 94.2 us
  starting transfers between devices  45.4 us (48%)
  waiting for transfers between devices  20.4 us (21%)
  Pallas kernels  15.9 us (17%)
  local copies, waits for them, and re-layouts  12.2 us (13%)
    ppermute x1, starting transfers between devices, local(): got_e = lax.ppermute(pay_e, 'tile', even_pairs)  13.9 us
    all_to_all x1, starting transfers between devices, local(): far = lax.all_to_all(far, 'narrow', 0, 0, tiled=True)  12.9 us
    unnamed x36, local copies, waits for them, and re-layouts  12.2 us
    ppermute x1, waiting for transfers between devices, local(): lax.ppermute(got_o, 'tile', [(i, i + 1) for i in range(0, strips, 2)])  9.07 us
    all_to_all x1, starting transfers between devices, local(): q_head = lax.all_to_all(q_t, 'narrow', 0, 0, tiled=True)  5.91 us
    ppermute x1, starting transfers between devices, local(): lax.ppermute(stacked, 'narrow', [(i, (i - 1) % members) for i in range(me...  5.48 us
    ppermute x1, waiting for transfers between devices, local(): lax.ppermute(stacked, 'narrow', [(i, (i - 1) % members) for i in range(me...  4.65 us
    pallas_call x1, Pallas kernels, window_attention(): pl.pallas_call(lambda *refs: window_kernel(last, *refs), in_specs=[smem,...  4.21 us
  transfers between devices with their start and end apart: 8, of which 4 were waited for; matrix products, arithmetic and copies ran while one was open for 0% of the time, Pallas kernels for 5%

profile of v1, /device:TPU:2, one launch (start us, length us, event | category | flops | bytes accessed | tf_op | source)
XLA Modules:
  0.0 94.2 jit_solution(18174793077493231272)
XLA Ops:
  0.0 0.0 copy-start.14
  0.0 0.0 copy-start.17
  0.0 0.1 pad_add_fusion.refs_0_.ids
  0.1 0.0 copy-start.3
  0.1 0.9 copy-done.3
  1.0 0.0 copy-start.5
  1.0 1.2 %copy-done.5 = bf16[4,128,1024]{2,1,0:T(8,128)(2,1)S(1)} copy-done((bf16[4,128,1024]{2,1,0:T(8,128)(2,1)S(1)}, bf16[4,128,1024]{2,1,0:T(8,128)(2,1)}, u32[]{:S(2)}) %copy-start.5) | copy-done | bytes 1048600
  2.2 0.0 copy-start.6
  2.2 1.2 %copy-done.6 = bf16[1024,512]{1,0:T(8,128)(2,1)S(1)} copy-done((bf16[1024,512]{1,0:T(8,128)(2,1)S(1)}, bf16[1024,512]{1,0:T(8,128)(2,1)}, u32[]{:S(2)}) %copy-start.6) | copy-done | bytes 1048600
  3.4 0.0 copy-start.7
  3.4 1.2 %copy-done.7 = bf16[1024,512]{1,0:T(8,128)(2,1)S(1)} copy-done((bf16[1024,512]{1,0:T(8,128)(2,1)S(1)}, bf16[1024,512]{1,0:T(8,128)(2,1)}, u32[]{:S(2)}) %copy-start.7) | copy-done | bytes 1048600
  4.7 0.0 copy-start.9
  4.7 1.0 %copy-done.9 = bf16[512,512]{1,0:T(8,128)(2,1)S(1)} copy-done((bf16[512,512]{1,0:T(8,128)(2,1)S(1)}, bf16[512,512]{1,0:T(8,128)(2,1)}, u32[]{:S(2)}) %copy-start.9) | copy-done | bytes 524312
  5.7 0.7 copy-done.10
  6.4 0.7 copy-done.13
  7.0 3.2 %project.1 = (bf16[512,128]{1,0:T(8,128)(2,1)S(1)}, bf16[784,128]{1,0:T(8,128)(2,1)S(1)}, bf16[784,128]{1,0:T(8,128)(2,1)S(1)}, bf16[128,512]{1,0:T(8,128)(2,1)S(1)}, bf16[8,64,128]{2,1,0:T(8,128)(2,1)}) custom-call(s32[2]{0:T(128)S(1)} %pad_add_fusion.refs_0_.ids, s32[8]{0:T(128)S(1)} %bitcast.20, bf16[512,1024]{1,0:T(8,128)(2,1)S(1)} %bitcast.16, ...), custom_call_target="tpu_custom_call" | custom-call | flops 350000000 | bytes 4000000 | tf_op jit(solution)/shard_map/project/pallas_call | solution.py:83
  10.3 5.9 %all-to-all-start = ((bf16[8,64,128]{2,1,0:T(8,128)(2,1)}), bf16[8,64,128]{2,1,0:T(8,128)(2,1)S(1)}, u32[]{:S(2)}, u32[]{:S(2)}) async-start(bf16[8,64,128]{2,1,0:T(8,128)(2,1)} %get-tuple-element.17), calls=%async_computation | async-start | bytes 262144 | tf_op jit(solution)/shard_map/all_to_all | solution.py:396
  16.2 3.4 %collective-permute-start = (bf16[784,128]{1,0:T(8,128)(2,1)S(1)}, bf16[784,128]{1,0:T(8,128)(2,1)S(1)}, u32[]{:S(2)}, u32[]{:S(2)}) collective-permute-start(bf16[784,128]{1,0:T(8,128)(2,1)S(1)} %get-tuple-element.12), channel_id=1, source_target_pairs={{0,504},{8,16},{16,8},{24,32},{32,24},{40,48},{48,40},{56,64},{64,... | collective-permute-start | bytes 602120 | tf_op jit(solution)/shard_map/ppermute | solution.py:393
  19.6 13.9 %collective-permute-start.1 = (bf16[784,128]{1,0:T(8,128)(2,1)S(1)}, bf16[784,128]{1,0:T(8,128)(2,1)S(1)}, u32[]{:S(2)}, u32[]{:S(2)}) collective-permute-start(bf16[784,128]{1,0:T(8,128)(2,1)S(1)} %get-tuple-element.13), channel_id=1, source_target_pairs={{0,8},{8,0},{16,24},{24,16},{32,40},{40,32},{48,56},{56,48},{64,72... | collective-permute-start | bytes 602120 | tf_op jit(solution)/shard_map/ppermute | solution.py:394
  33.5 0.7 collective-permute-start.4
  34.2 0.0 collective-permute-done.a.refs_6_
  34.2 1.3 %collective-permute-start.5 = (bf16[784,128]{1,0:T(8,128)(2,1)S(1)}, bf16[784,128]{1,0:T(8,128)(2,1)S(1)}, u32[]{:S(2)}, u32[]{:S(2)}) collective-permute-start(bf16[784,128]{1,0:T(8,128)(2,1)S(1)} %collective-permute-done.a.refs_6_), channel_id=1, source_target_pairs={{0,8},{16,24},{32,40},{48,56},{64,72},{80,88},{96,104},{112,120},{... | collective-permute-start | bytes 602120 | tf_op jit(solution)/shard_map/ppermute | solution.py:397
  35.5 3.8 %collective-permute-done.1.b.refs_7_ = bf16[784,128]{1,0:T(8,128)(2,1)S(1)} collective-permute-done((bf16[784,128]{1,0:T(8,128)(2,1)S(1)}, bf16[784,128]{1,0:T(8,128)(2,1)S(1)}, u32[]{:S(2)}, u32[]{:S(2)}) %collective-permute-start.1) | collective-permute-done | bytes 200736 | tf_op jit(solution)/shard_map/ppermute | solution.py:394
  39.3 0.0 collective-permute-done.4.refs_8_
  39.3 9.1 %collective-permute-done.5.refs_9_ = bf16[784,128]{1,0:T(8,128)(2,1)S(1)} collective-permute-done((bf16[784,128]{1,0:T(8,128)(2,1)S(1)}, bf16[784,128]{1,0:T(8,128)(2,1)S(1)}, u32[]{:S(2)}, u32[]{:S(2)}) %collective-permute-start.5) | collective-permute-done | bytes 200736 | tf_op jit(solution)/shard_map/ppermute | solution.py:397
  48.4 0.0 all-to-all-done.refs_4_
  48.4 0.0 copy-done.14
  48.4 0.0 copy-done.17
  48.4 4.2 %coarse_attention.1 = bf16[8,80,128]{2,1,0:T(8,128)(2,1)} custom-call(s32[2]{0:T(128)S(1)} %pad_add_fusion.refs_0_.ids, s32[2]{0:T(128)S(1)} %copy-done.17, s32[8]{0:T(128)S(1)} %bitcast.21, s32[8]{0:T(128)S(1)} %fusion.1.refs_3_, bf16[8,64,128]{2,1,0:T(8,128)(2,1)S(1)} %all-to-all-done.refs_4_, bf16[512,128]{1,0:T(8,128)(2,1)S(1)} %get-tuple-element.18.refs_5_, ...), custom_call_target="tpu_custom_call" | custom-call | flops 1600000000 | bytes 1500000 | tf_op jit(solution)/shard_map/coarse_attention/pallas_call | solution.py:284
  52.6 12.9 %all-to-all-start.1 = ((bf16[8,80,128]{2,1,0:T(8,128)(2,1)}), bf16[8,80,128]{2,1,0:T(8,128)(2,1)S(1)}, u32[]{:S(2)}, u32[]{:S(2)}) async-start(bf16[8,80,128]{2,1,0:T(8,128)(2,1)} %coarse_attention.1), calls=%async_computation.1 | async-start | bytes 327680 | tf_op jit(solution)/shard_map/all_to_all | solution.py:408
  65.4 0.0 copy-done.4
  65.4 0.6 stack_rows.1.refs_3_
  66.0 5.5 %collective-permute-start.3 = (bf16[256,512]{1,0:T(8,128)(2,1)S(1)}, bf16[256,512]{1,0:T(8,128)(2,1)S(1)}, u32[]{:S(2)}, u32[]{:S(2)}) collective-permute-start(bf16[256,512]{1,0:T(8,128)(2,1)S(1)} %stack_rows.1.refs_3_), channel_id=1, source_target_pairs={{0,7},{1,0},{2,1},{3,2},{4,3},{5,4},{6,5},{7,6},{8,15},{9,8},{10,9... | collective-permute-start | bytes 786440 | tf_op jit(solution)/shard_map/ppermute | solution.py:400
  71.5 1.9 %collective-permute-start.2 = (bf16[256,512]{1,0:T(8,128)(2,1)S(1)}, bf16[256,512]{1,0:T(8,128)(2,1)S(1)}, u32[]{:S(2)}, u32[]{:S(2)}) collective-permute-start(bf16[256,512]{1,0:T(8,128)(2,1)S(1)} %stack_rows.1.refs_3_), channel_id=1, source_target_pairs={{0,1},{1,2},{2,3},{3,4},{4,5},{5,6},{6,7},{7,0},{8,9},{9,10},{10,1... | collective-permute-start | bytes 786440 | tf_op jit(solution)/shard_map/ppermute | solution.py:401
  73.4 4.7 %collective-permute-done.3.refs_4_ = bf16[256,512]{1,0:T(8,128)(2,1)S(1)} collective-permute-done((bf16[256,512]{1,0:T(8,128)(2,1)S(1)}, bf16[256,512]{1,0:T(8,128)(2,1)S(1)}, u32[]{:S(2)}, u32[]{:S(2)}) %collective-permute-start.3) | collective-permute-done | bytes 262176 | tf_op jit(solution)/shard_map/ppermute | solution.py:400
  78.1 2.9 %collective-permute-done.2.refs_2_ = bf16[256,512]{1,0:T(8,128)(2,1)S(1)} collective-permute-done((bf16[256,512]{1,0:T(8,128)(2,1)S(1)}, bf16[256,512]{1,0:T(8,128)(2,1)S(1)}, u32[]{:S(2)}, u32[]{:S(2)}) %collective-permute-start.2) | collective-permute-done | bytes 262176 | tf_op jit(solution)/shard_map/ppermute | solution.py:401
  81.0 0.0 copy-done.11
  81.0 1.0 %copy-done.15 = bf16[512,512]{1,0:T(8,128)(2,1)S(1)} copy-done((bf16[512,512]{1,0:T(8,128)(2,1)S(1)}, bf16[512,512]{1,0:T(8,128)(2,1)}, u32[]{:S(2)}) %copy-start.15) | copy-done | bytes 524312
  82.0 1.0 %copy-done.16 = bf16[512,512]{1,0:T(8,128)(2,1)S(1)} copy-done((bf16[512,512]{1,0:T(8,128)(2,1)S(1)}, bf16[512,512]{1,0:T(8,128)(2,1)}, u32[]{:S(2)}) %copy-start.16) | copy-done | bytes 524312
  83.1 4.2 %window_attention.1 = (f32[128,512]{1,0:T(8,128)S(1)}, f32[128,128]{1,0:T(8,128)S(1)}) custom-call(s32[2]{0:T(128)S(1)} %pad_add_fusion.refs_0_.ids, s32[2]{0:T(128)S(1)} %copy-done.17, bf16[256,512]{1,0:T(8,128)(2,1)S(1)} %collective-permute-done.2.refs_2_, bf16[256,512]{1,0:T(8,128)(2,1)S(1)} %stack_rows.1.refs_3_, ...), custom_call_target="tpu_custom_call" | custom-call | flops 2000000000 | bytes 3000000 | tf_op jit(solution)/shard_map/window_attention/pallas_call | solution.py:207
  87.3 0.0 all-to-all-done.1.coarse
  87.3 0.0 copy-done
  87.3 0.0 copy-done.8
  87.3 0.0 copy-done.12
  87.4 0.0 copy-start.1
  87.4 1.6 %copy-done.1 = bf16[512,2048]{1,0:T(8,128)(2,1)S(1)} copy-done((bf16[512,2048]{1,0:T(8,128)(2,1)S(1)}, bf16[512,2048]{1,0:T(8,128)(2,1)}, u32[]{:S(2)}) %copy-start.1) | copy-done | bytes 2097176
  89.0 1.6 %copy-done.2 = bf16[2048,512]{1,0:T(8,128)(2,1)S(1)} copy-done((bf16[2048,512]{1,0:T(8,128)(2,1)S(1)}, bf16[2048,512]{1,0:T(8,128)(2,1)}, u32[]{:S(2)}) %copy-start.2) | copy-done | bytes 2097176
  90.5 3.6 %finish.1 = bf16[128,512]{1,0:T(8,128)(2,1)} custom-call(bf16[128,512]{1,0:T(8,128)(2,1)S(1)} %bitcast.15, f32[128,512]{1,0:T(8,128)S(1)} %get-tuple-element.15.near, f32[128,128]{1,0:T(8,128)S(1)} %get-tuple-element.16.near_lse, bf16[8,80,128]{2,1,0:T(8,128)(2,1)S(1)} %all-to-all-done.1.coarse, bf16[512,512]{1,0:T(8,128)(2,1)S(1)} %copy-done.8, ...), custom_call_target="tpu_custom_call" | custom-call | flops 900000000 | bytes 7500000 | tf_op jit(solution)/shard_map/finish/pallas_call | solution.py:331
  (11 shorter events, 0.0 us)
Async XLA Ops:
  0.0 48.4 %copy-start.14 = (s32[1,8]{1,0:T(1,128)S(1)}, s32[1,8]{1,0:T(1,128)}, u32[]{:S(2)}) copy-start(s32[1,8]{1,0:T(1,128)} %param.17) | copy-start | bytes 100
  0.0 48.4 %copy-start.17 = (s32[2]{0:T(128)S(1)}, s32[2]{0:T(128)}, u32[]{:S(2)}) copy-start(s32[2]{0:T(128)} %refs_1_.3) | copy-start | bytes 28
  0.1 0.9 copy-start.3
  1.0 1.2 %copy-start.5 = (bf16[4,128,1024]{2,1,0:T(8,128)(2,1)S(1)}, bf16[4,128,1024]{2,1,0:T(8,128)(2,1)}, u32[]{:S(2)}) copy-start(bf16[4,128,1024]{2,1,0:T(8,128)(2,1)} %param.16) | copy-start | bytes 3145732
  2.2 1.2 %copy-start.6 = (bf16[1024,512]{1,0:T(8,128)(2,1)S(1)}, bf16[1024,512]{1,0:T(8,128)(2,1)}, u32[]{:S(2)}) copy-start(bf16[1024,512]{1,0:T(8,128)(2,1)} %refs_3_.1) | copy-start | bytes 3145732
  3.4 1.2 %copy-start.7 = (bf16[1024,512]{1,0:T(8,128)(2,1)S(1)}, bf16[1024,512]{1,0:T(8,128)(2,1)}, u32[]{:S(2)}) copy-start(bf16[1024,512]{1,0:T(8,128)(2,1)} %refs_4_.1) | copy-start | bytes 3145732
  4.7 1.0 %copy-start.9 = (bf16[512,512]{1,0:T(8,128)(2,1)S(1)}, bf16[512,512]{1,0:T(8,128)(2,1)}, u32[]{:S(2)}) copy-start(bf16[512,512]{1,0:T(8,128)(2,1)} %refs_7_.2) | copy-start | bytes 1572868
  5.7 0.7 copy-start.10
  6.4 0.7 copy-start.13
  10.3 38.1 %all-to-all-start = ((bf16[8,64,128]{2,1,0:T(8,128)(2,1)}), bf16[8,64,128]{2,1,0:T(8,128)(2,1)S(1)}, u32[]{:S(2)}, u32[]{:S(2)}) async-start(bf16[8,64,128]{2,1,0:T(8,128)(2,1)} %get-tuple-element.17), calls=%async_computation | async-start | bytes 262144 | tf_op jit(solution)/shard_map/all_to_all | solution.py:396
  16.2 18.0 %collective-permute-start = (bf16[784,128]{1,0:T(8,128)(2,1)S(1)}, bf16[784,128]{1,0:T(8,128)(2,1)S(1)}, u32[]{:S(2)}, u32[]{:S(2)}) collective-permute-start(bf16[784,128]{1,0:T(8,128)(2,1)S(1)} %get-tuple-element.12), channel_id=1, source_target_pairs={{0,504},{8,16},{16,8},{24,32},{32,24},{40,48},{48,40},{56,64},{64,... | collective-permute-start | bytes 602120 | tf_op jit(solution)/shard_map/ppermute | solution.py:393
  19.6 19.7 %collective-permute-start.1 = (bf16[784,128]{1,0:T(8,128)(2,1)S(1)}, bf16[784,128]{1,0:T(8,128)(2,1)S(1)}, u32[]{:S(2)}, u32[]{:S(2)}) collective-permute-start(bf16[784,128]{1,0:T(8,128)(2,1)S(1)} %get-tuple-element.13), channel_id=1, source_target_pairs={{0,8},{8,0},{16,24},{24,16},{32,40},{40,32},{48,56},{56,48},{64,72... | collective-permute-start | bytes 602120 | tf_op jit(solution)/shard_map/ppermute | solution.py:394
  33.5 5.8 %collective-permute-start.4 = (bf16[512,128]{1,0:T(8,128)(2,1)S(1)}, bf16[512,128]{1,0:T(8,128)(2,1)S(1)}, u32[]{:S(2)}, u32[]{:S(2)}) collective-permute-start(bf16[512,128]{1,0:T(8,128)(2,1)S(1)} %get-tuple-element.18.refs_5_), channel_id=1, source_target_pairs={{0,16},{16,32},{32,48},{48,64},{64,80},{80,96},{96,112},{112,128},... | collective-permute-start | bytes 393224 | tf_op jit(solution)/shard_map/ppermute | solution.py:395
  34.2 14.2 %collective-permute-start.5 = (bf16[784,128]{1,0:T(8,128)(2,1)S(1)}, bf16[784,128]{1,0:T(8,128)(2,1)S(1)}, u32[]{:S(2)}, u32[]{:S(2)}) collective-permute-start(bf16[784,128]{1,0:T(8,128)(2,1)S(1)} %collective-permute-done.a.refs_6_), channel_id=1, source_target_pairs={{0,8},{16,24},{32,40},{48,56},{64,72},{80,88},{96,104},{112,120},{... | collective-permute-start | bytes 602120 | tf_op jit(solution)/shard_map/ppermute | solution.py:397
  39.3 26.2 %copy-start.4 = (bf16[16,8,512]{2,1,0:T(8,128)(2,1)S(1)}, bf16[16,8,512]{2,1,0:T(8,128)(2,1)}, u32[]{:S(2)}) copy-start(bf16[16,8,512]{2,1,0:T(8,128)(2,1)} %param.15) | copy-start | bytes 393220
  39.3 41.7 %copy-start.11 = (f32[512]{0:T(512)S(1)}, f32[512]{0:T(512)}, u32[]{:S(2)}) copy-start(f32[512]{0:T(512)} %param.19) | copy-start | bytes 6148
  52.6 34.7 %all-to-all-start.1 = ((bf16[8,80,128]{2,1,0:T(8,128)(2,1)}), bf16[8,80,128]{2,1,0:T(8,128)(2,1)S(1)}, u32[]{:S(2)}, u32[]{:S(2)}) async-start(bf16[8,80,128]{2,1,0:T(8,128)(2,1)} %coarse_attention.1), calls=%async_computation.1 | async-start | bytes 327680 | tf_op jit(solution)/shard_map/all_to_all | solution.py:408
  66.0 12.1 %collective-permute-start.3 = (bf16[256,512]{1,0:T(8,128)(2,1)S(1)}, bf16[256,512]{1,0:T(8,128)(2,1)S(1)}, u32[]{:S(2)}, u32[]{:S(2)}) collective-permute-start(bf16[256,512]{1,0:T(8,128)(2,1)S(1)} %stack_rows.1.refs_3_), channel_id=1, source_target_pairs={{0,7},{1,0},{2,1},{3,2},{4,3},{5,4},{6,5},{7,6},{8,15},{9,8},{10,9... | collective-permute-start | bytes 786440 | tf_op jit(solution)/shard_map/ppermute | solution.py:400
  71.5 9.5 %collective-permute-start.2 = (bf16[256,512]{1,0:T(8,128)(2,1)S(1)}, bf16[256,512]{1,0:T(8,128)(2,1)S(1)}, u32[]{:S(2)}, u32[]{:S(2)}) collective-permute-start(bf16[256,512]{1,0:T(8,128)(2,1)S(1)} %stack_rows.1.refs_3_), channel_id=1, source_target_pairs={{0,1},{1,2},{2,3},{3,4},{4,5},{5,6},{6,7},{7,0},{8,9},{9,10},{10,1... | collective-permute-start | bytes 786440 | tf_op jit(solution)/shard_map/ppermute | solution.py:401
  81.0 1.0 %copy-start.15 = (bf16[512,512]{1,0:T(8,128)(2,1)S(1)}, bf16[512,512]{1,0:T(8,128)(2,1)}, u32[]{:S(2)}) copy-start(bf16[512,512]{1,0:T(8,128)(2,1)} %refs_7_.3) | copy-start | bytes 1572868
  82.0 1.0 %copy-start.16 = (bf16[512,512]{1,0:T(8,128)(2,1)S(1)}, bf16[512,512]{1,0:T(8,128)(2,1)}, u32[]{:S(2)}) copy-start(bf16[512,512]{1,0:T(8,128)(2,1)} %refs_8_.1) | copy-start | bytes 1572868
  83.1 4.2 %copy-start = (bf16[512,2048]{1,0:T(8,128)(2,1)S(1)}, bf16[512,2048]{1,0:T(8,128)(2,1)}, u32[]{:S(2)}) copy-start(bf16[512,2048]{1,0:T(8,128)(2,1)} %w_gate.1) | copy-start | bytes 6291460
  83.1 4.2 %copy-start.8 = (bf16[512,512]{1,0:T(8,128)(2,1)S(1)}, bf16[512,512]{1,0:T(8,128)(2,1)}, u32[]{:S(2)}) copy-start(bf16[512,512]{1,0:T(8,128)(2,1)} %w_out.1) | copy-start | bytes 1572868
  83.1 4.3 %copy-start.12 = (f32[512]{0:T(512)S(1)}, f32[512]{0:T(512)}, u32[]{:S(2)}) copy-start(f32[512]{0:T(512)} %param.26) | copy-start | bytes 6148
  87.4 1.6 %copy-start.1 = (bf16[512,2048]{1,0:T(8,128)(2,1)S(1)}, bf16[512,2048]{1,0:T(8,128)(2,1)}, u32[]{:S(2)}) copy-start(bf16[512,2048]{1,0:T(8,128)(2,1)} %w_up.1) | copy-start | bytes 6291460
  88.9 1.6 %copy-start.2 = (bf16[2048,512]{1,0:T(8,128)(2,1)S(1)}, bf16[2048,512]{1,0:T(8,128)(2,1)}, u32[]{:S(2)}) copy-start(bf16[2048,512]{1,0:T(8,128)(2,1)} %w_down.1) | copy-start | bytes 6291460

commit v2 on v1

v2 whole, which is shorter than its diff:
```python
import jax
import jax.numpy as jnp
from jax import lax
from jax.experimental import pallas as pl
from jax.experimental.pallas import tpu as pltpu
from jax.sharding import PartitionSpec as P

HEADS = 8
HD = 64
WS = 8
EPS = 1e-06
F32 = jnp.float32
BF16 = jnp.bfloat16
LOW = -1e30
VMEM_LIMIT = 24 * 1024 * 1024
COST = pl.CostEstimate(flops=1000, bytes_accessed=1000, transcendentals=0)


def iota(shape, dim):
    return lax.broadcasted_iota(jnp.int32, shape, dim)


def rms(x, gain):
    mean_square = jnp.mean(x * x, axis=-1, keepdims=True)
    return x * lax.rsqrt(mean_square + EPS) * gain


def local_blocks(ids, table, per_strip, total):
    first = (ids[0] - 1) * per_strip
    return [lax.rem(table[i] - first + 2 * total, total) for i in range(table.shape[0])]


def project_kernel(total, ids, table, coarse, w_k, w_v, fine, kv, pay_o, pay_e, c_buf, k_buf, v_buf, x_buf, sems):
    chunks = c_buf.shape[0]
    rows = c_buf.shape[1]
    cols = pl.ds(pl.multiple_of(ids[1] // 2 * 128, 128), 128)
    loads = [
        pltpu.make_async_copy(w_k.at[:, cols], k_buf, sems.at[0]),
        pltpu.make_async_copy(w_v.at[:, cols], v_buf, sems.at[1]),
        pltpu.make_async_copy(fine, x_buf, sems.at[2]),
    ]
    parts = [
        pltpu.make_async_copy(coarse.at[pl.ds(rows * i, rows)], c_buf.at[i], sems.at[3 + i])
        for i in range(chunks)
    ]
    for copy in (loads[0], loads[1], parts[0], loads[2], *parts[1:]):
        copy.start()
    odd_head = lax.rem(ids[1], 2) == 1
    even = lax.rem(ids[0], 2) == 0
    low = iota((rows, 128), 1) < HD
    base = kv.shape[0]
    n_tok, width = x_buf.shape
    half = n_tok // 2
    chosen = local_blocks(ids, table, base // 128, total)
    lane = iota((16, 128), 1)
    marks = jnp.zeros((16, 128), F32)
    for i, b in enumerate(chosen):
        marks = jnp.where(lane == i, b.astype(F32), marks)
    end = base + half * (width // 128)
    pay_o[end : end + 16, :] = marks.astype(BF16)
    pay_e[end : end + 16, :] = marks.astype(BF16)
    loads[0].wait()
    loads[1].wait()
    for i in range(chunks):
        parts[i].wait()
        tokens = c_buf[i]
        key = jnp.dot(tokens, k_buf[...], preferred_element_type=F32)
        value = jnp.dot(tokens, v_buf[...], preferred_element_type=F32)
        key = jnp.where(odd_head, pltpu.roll(key, HD, 1), key)
        value = jnp.where(odd_head, value, pltpu.roll(value, HD, 1))
        both = jnp.where(low, key, value).astype(BF16)
        at = slice(rows * i, rows * i + rows)
        kv[at, :] = both
        pay_o[at, :] = both
        pay_e[at, :] = both
    loads[2].wait()
    for c in range(width // 128):
        lanes = slice(128 * c, 128 * c + 128)
        at = slice(base + half * c, base + half * (c + 1))
        top, bottom = x_buf[0:half, lanes], x_buf[half:, lanes]
        pay_o[at, :] = jnp.where(even, top, bottom)
        pay_e[at, :] = jnp.where(even, bottom, top)


def project(ids, table, coarse, w_k, w_v, fine, total):
    n_coarse, cw = coarse.shape
    n_tok, width = fine.shape
    chunks = 4
    pay_rows = n_coarse + (n_tok // 2) * (width // 128) + 16
    smem = pl.BlockSpec(memory_space=pltpu.SMEM)
    hbm = pl.BlockSpec(memory_space=pltpu.HBM)
    vmem = pl.BlockSpec(memory_space=pltpu.VMEM)
    return pl.pallas_call(
        lambda *refs: project_kernel(total, *refs),
        in_specs=[smem, smem] + [hbm] * 4,
        out_specs=[vmem] * 3,
        out_shape=[
            jax.ShapeDtypeStruct((n_coarse, 128), BF16),
            jax.ShapeDtypeStruct((pay_rows, 128), BF16),
            jax.ShapeDtypeStruct((pay_rows, 128), BF16),
        ],
        scratch_shapes=[
            pltpu.VMEM((chunks, n_coarse // chunks, cw), BF16),
            pltpu.VMEM((cw, 128), BF16),
            pltpu.VMEM((cw, 128), BF16),
            pltpu.VMEM((n_tok, width), BF16),
            pltpu.SemaphoreType.DMA((3 + chunks,)),
        ],
        compiler_params=pltpu.CompilerParams(vmem_limit_bytes=VMEM_LIMIT),
        cost_estimate=COST,
        name="project",
    )(ids, table, coarse, w_k, w_v, fine)


def query_kernel(after, fine, gain, w_q, q_nat, q_t, x_buf, q_buf, sems):
    first = pltpu.make_async_copy(fine, x_buf, sems.at[0])
    second = pltpu.make_async_copy(w_q, q_buf, sems.at[1])
    first.start()
    second.start()
    first.wait()
    normed = rms(x_buf[...].astype(F32), gain[...]).astype(BF16)
    second.wait()
    q = jnp.dot(normed, q_buf[...], preferred_element_type=F32) * (1.0 / HD**0.5)
    q_nat[...] = q.astype(BF16)
    q_t[...] = q.T.astype(BF16).reshape(q_t.shape)


def queries(after, fine, gain, w_q):
    n_tok, width = fine.shape
    hbm = pl.BlockSpec(memory_space=pltpu.HBM)
    vmem = pl.BlockSpec(memory_space=pltpu.VMEM)
    return pl.pallas_call(
        query_kernel,
        in_specs=[pl.BlockSpec(memory_space=pl.ANY), hbm, vmem, hbm],
        out_specs=[vmem] * 2,
        out_shape=[
            jax.ShapeDtypeStruct((n_tok, width), BF16),
            jax.ShapeDtypeStruct((HEADS, HD, n_tok), BF16),
        ],
        scratch_shapes=[
            pltpu.VMEM((n_tok, width), BF16),
            pltpu.VMEM((width, width), BF16),
            pltpu.SemaphoreType.DMA((2,)),
        ],
        compiler_params=pltpu.CompilerParams(vmem_limit_bytes=VMEM_LIMIT),
        cost_estimate=COST,
        name="queries",
    )(after, fine, gain, w_q)


def stack_kernel(ids, base, got_o, got_e, fine, out):
    n_tok, width = fine.shape
    half = n_tok // 2
    out[half : half + n_tok, :] = fine[...]
    even = lax.rem(ids[0], 2) == 0
    for c in range(width // 128):
        lanes = slice(128 * c, 128 * c + 128)
        at = slice(base + half * c, base + half * (c + 1))
        a, b = got_o[at, :], got_e[at, :]
        out[0:half, lanes] = jnp.where(even, a, b)
        out[half + n_tok :, lanes] = jnp.where(even, b, a)


def stack_rows(ids, got_o, got_e, fine, base):
    n_tok, width = fine.shape
    vmem = pl.BlockSpec(memory_space=pltpu.VMEM)
    return pl.pallas_call(
        lambda ids, a, b, x, out: stack_kernel(ids, base, a, b, x, out),
        in_specs=[pl.BlockSpec(memory_space=pltpu.SMEM), vmem, vmem, vmem],
        out_specs=vmem,
        out_shape=jax.ShapeDtypeStruct((2 * n_tok, width), BF16),
        compiler_params=pltpu.CompilerParams(vmem_limit_bytes=VMEM_LIMIT),
        cost_estimate=pl.CostEstimate(flops=10000000000, bytes_accessed=33333333, transcendentals=0),
        name="stack_rows",
    )(ids, got_o, got_e, fine)


def window_kernel(last, ids, shifts, left, mid, right, q, gain, w_k, w_v, out, lse, k_buf, v_buf, sems):
    loads = [pltpu.make_async_copy(w_k, k_buf, sems.at[0]), pltpu.make_async_copy(w_v, v_buf, sems.at[1])]
    for copy in loads:
        copy.start()
    span = left.shape[0]
    side = span - 64
    strip, member = ids[0], ids[1]
    shift_row, shift_col = shifts[0], shifts[1]
    fine = jnp.concatenate([left[...], mid[...], right[...]], axis=0).astype(F32)
    normed = rms(fine, gain[...]).astype(BF16)
    loads[0].wait()
    keys = jnp.dot(normed, k_buf[...], preferred_element_type=F32).astype(BF16)
    loads[1].wait()
    values = jnp.dot(normed, v_buf[...], preferred_element_type=F32).astype(BF16)
    shape = (128, 3 * side)
    query = lax.rem(iota(shape, 0), 64)
    column_q = lax.rem(query, 8)
    key = iota(shape, 1)
    part = (key >= side).astype(jnp.int32) + (key >= 2 * side).astype(jnp.int32)
    within = key - part * side
    column_k = (part - 1) * 8 + lax.rem(within, 8)
    same_col = lax.shift_right_arithmetic(column_q - shift_col + 16, 3) == lax.shift_right_arithmetic(
        column_k - shift_col + 16, 3
    )
    wrap_col = ((column_k < 0) & (member == 0)) | ((column_k > 7) & (member == last[1]))
    lane = iota((64, 128), 1)
    low = lane < HD
    low_rows = iota((128, 128), 0) < 64
    low_lanes = iota((128, 128), 1) < HD
    own = low_rows == low_lanes
    for half in range(2):
        row_q = 8 * half + lax.shift_right_arithmetic(query, 3)
        row_k = 8 * half - 8 + lax.shift_right_arithmetic(within, 3)
        same_row = lax.shift_right_arithmetic(row_q - shift_row + 16, 3) == lax.shift_right_arithmetic(
            row_k - shift_row + 16, 3
        )
        wrap_row = ((row_k < 0) & (strip == 0)) | ((row_k > 15) & (strip == last[0]))
        seen = same_row & same_col & jnp.logical_not(wrap_row | wrap_col)
        rows = slice(64 * half, 64 * half + 64)
        pick = lambda a: jnp.concatenate(
            [a[span * b + 64 * half : span * b + 64 * half + side] for b in range(3)], axis=0
        )
        keys_h, values_h = pick(keys), pick(values)
        marks = jnp.zeros((64, 128), F32)
        for pair in range(HEADS // 2):
            lanes = slice(128 * pair, 128 * pair + 128)
            q_pair = q[rows, lanes]
            q_both = jnp.concatenate([q_pair, q_pair], axis=0)
            q_both = jnp.where(own, q_both, jnp.zeros_like(q_both))
            score = lax.dot_general(
                q_both, keys_h[:, lanes], (((1,), (1,)), ((), ())), preferred_element_type=F32
            )
            score = jnp.where(seen, score, LOW)
            peak = jnp.max(score, axis=-1, keepdims=True)
            weight = jnp.exp(score - peak)
            total = jnp.sum(weight, axis=-1, keepdims=True)
            mixed = jnp.dot(weight.astype(BF16), values_h[:, lanes], preferred_element_type=F32) / total
            out[rows, lanes] = jnp.where(low, mixed[:64], mixed[64:])
            level = peak + jnp.log(total)
            marks = jnp.where(lane == 2 * pair, level[:64], marks)
            marks = jnp.where(lane == 2 * pair + 1, level[64:], marks)
        lse[rows, :] = marks


def window_attention(ids, shifts, left, mid, right, q, gain, w_k, w_v, last):
    n_tok, width = q.shape
    vmem = pl.BlockSpec(memory_space=pltpu.VMEM)
    smem = pl.BlockSpec(memory_space=pltpu.SMEM)
    return pl.pallas_call(
        lambda *refs: window_kernel(last, *refs),
        in_specs=[smem, smem] + [vmem] * 5 + [pl.BlockSpec(memory_space=pltpu.HBM)] * 2,
        out_specs=[vmem, vmem],
        out_shape=[
            jax.ShapeDtypeStruct((n_tok, width), F32),
            jax.ShapeDtypeStruct((n_tok, 128), F32),
        ],
        scratch_shapes=[
            pltpu.VMEM((width, width), BF16),
            pltpu.VMEM((width, width), BF16),
            pltpu.SemaphoreType.DMA((2,)),
        ],
        compiler_params=pltpu.CompilerParams(vmem_limit_bytes=VMEM_LIMIT),
        cost_estimate=COST,
        name="window_attention",
    )(ids, shifts, left, mid, right, q, gain, w_k, w_v)


def coarse_kernel(total, after, after_too, ids, shifts, table, table_before, q_t, own, got_o, got_e, far_even, far_odd, out, store):
    n_own = own.shape[0]
    per_strip = n_own // 128
    even = lax.rem(ids[0], 2) == 0
    store[2 * per_strip : 3 * per_strip] = own[...].reshape(per_strip, 128, 128)

    @pl.when(even)
    def _():
        store[0:per_strip] = far_even[...].reshape(per_strip, 128, 128)
        store[per_strip : 2 * per_strip] = got_o[0:n_own, :].reshape(per_strip, 128, 128)
        store[3 * per_strip :] = got_e[0:n_own, :].reshape(per_strip, 128, 128)

    @pl.when(jnp.logical_not(even))
    def _():
        store[0:per_strip] = far_odd[0:n_own, :].reshape(per_strip, 128, 128)
        store[per_strip : 2 * per_strip] = got_e[0:n_own, :].reshape(per_strip, 128, 128)
        store[3 * per_strip :] = got_o[0:n_own, :].reshape(per_strip, 128, 128)

    here = [b + per_strip for b in local_blocks(ids, table, per_strip, total)]
    before = [table_before[i] for i in range(table_before.shape[0])]
    kv_here = jnp.concatenate([store[b] for b in here], axis=0)
    kv_before = jnp.concatenate([store[b] for b in before], axis=0)
    kv_here_t = kv_here.astype(F32).T.astype(BF16)
    kv_before_t = kv_before.astype(F32).T.astype(BF16)
    shift_row = shifts[0]
    lane = lax.rem(iota((1, 256), 1), 128)
    earlier = lane < WS * shift_row
    line = iota((16, 256), 0)
    members = q_t.shape[0]
    for p in range(members // 2):
        q = jnp.concatenate([q_t[2 * p], q_t[2 * p + 1]], axis=1)
        q = jnp.concatenate([q, jnp.zeros_like(q)], axis=0)
        score = jnp.where(
            earlier,
            jnp.dot(kv_before, q, preferred_element_type=F32),
            jnp.dot(kv_here, q, preferred_element_type=F32),
        )
        peak = jnp.max(score, axis=0, keepdims=True)
        weight = jnp.exp(score - peak)
        sums = jnp.sum(weight, axis=0, keepdims=True)
        weight = weight.astype(BF16)
        mixed = jnp.where(
            earlier,
            jnp.dot(kv_before_t, weight, preferred_element_type=F32),
            jnp.dot(kv_here_t, weight, preferred_element_type=F32),
        )
        mixed = (mixed[HD:] / sums).astype(BF16)
        level = peak + jnp.log(sums)
        first = level.astype(BF16).astype(F32)
        second = (level - first).astype(BF16).astype(F32)
        third = level - first - second
        marks = jnp.where(line == 0, first, jnp.where(line == 1, second, jnp.where(line == 2, third, 0.0)))
        marks = marks.astype(BF16)
        for k in range(2):
            lanes = slice(128 * k, 128 * k + 128)
            out[2 * p + k, 0:HD, :] = mixed[:, lanes]
            out[2 * p + k, HD : HD + 16, :] = marks[:, lanes]


def coarse_attention(after, after_too, ids, shifts, table, table_before, q_t, own, got_o, got_e, far_even, far_odd, total):
    vmem = pl.BlockSpec(memory_space=pltpu.VMEM)
    smem = pl.BlockSpec(memory_space=pltpu.SMEM)
    members, _, n_tok = q_t.shape
    return pl.pallas_call(
        lambda *refs: coarse_kernel(total, *refs),
        in_specs=[pl.BlockSpec(memory_space=pl.ANY)] * 2 + [smem] * 4 + [vmem] * 6,
        out_specs=vmem,
        out_shape=jax.ShapeDtypeStruct((members, HD + 16, n_tok), BF16),
        scratch_shapes=[pltpu.VMEM((4 * own.shape[0] // 128, 128, 128), BF16)],
        compiler_params=pltpu.CompilerParams(vmem_limit_bytes=VMEM_LIMIT),
        cost_estimate=COST,
        name="coarse_attention",
    )(after, after_too, ids, shifts, table, table_before, q_t, own, got_o, got_e, far_even, far_odd)


def finish_kernel(
    fine, near, near_lse, coarse, gain, w_out, w_gate, w_up, w_down, out, o_buf, g_buf, u_buf, d_buf, sems
):
    steps, width, chunk = g_buf.shape
    first = pltpu.make_async_copy(w_out, o_buf, sems.at[0])
    first.start()
    loads = []
    for i in range(steps):
        at = pl.ds(chunk * i, chunk)
        loads.append(
            [
                pltpu.make_async_copy(w_gate.at[:, at], g_buf.at[i], sems.at[1 + 3 * i]),
                pltpu.make_async_copy(w_up.at[:, at], u_buf.at[i], sems.at[2 + 3 * i]),
                pltpu.make_async_copy(w_down.at[at], d_buf.at[i], sems.at[3 + 3 * i]),
            ]
        )
        for copy in loads[i]:
            copy.start()
    heads = coarse.shape[0]
    far = jnp.concatenate([coarse[h, 0:HD, :].astype(F32) for h in range(heads)], axis=0).T
    marks = [coarse[h, HD : HD + 16, :].astype(F32) for h in range(heads)]
    level = jnp.concatenate([m[0:1] + m[1:2] + m[2:3] for m in marks], axis=0).T
    diff = near_lse[:, 0:heads] - level
    share = 1.0 / (1.0 + jnp.exp(diff))
    share = jnp.concatenate(
        [jnp.broadcast_to(share[:, h : h + 1], (share.shape[0], HD)) for h in range(heads)], axis=1
    )
    head_out = (near[...] * (1.0 - share) + far * share).astype(BF16)
    first.wait()
    mid = fine[...].astype(F32) + jnp.dot(head_out, o_buf[...], preferred_element_type=F32)
    normed = rms(mid, gain[...]).astype(BF16)
    total = mid
    for i in range(steps):
        loads[i][0].wait()
        gate = jnp.dot(normed, g_buf[i], preferred_element_type=F32)
        loads[i][1].wait()
        up = jnp.dot(normed, u_buf[i], preferred_element_type=F32)
        hidden = (gate * (1.0 / (1.0 + jnp.exp(-gate))) * up).astype(BF16)
        loads[i][2].wait()
        total = total + jnp.dot(hidden, d_buf[i], preferred_element_type=F32)
    out[...] = total.astype(BF16)


def finish(fine, near, near_lse, coarse, gain, w_out, w_gate, w_up, w_down):
    n_tok, width = fine.shape
    ff = w_gate.shape[1]
    chunk = 512
    vmem = pl.BlockSpec(memory_space=pltpu.VMEM)
    hbm = pl.BlockSpec(memory_space=pltpu.HBM)
    return pl.pallas_call(
        finish_kernel,
        in_specs=[vmem] * 5 + [hbm] * 4,
        out_specs=vmem,
        out_shape=jax.ShapeDtypeStruct((n_tok, width), BF16),
        scratch_shapes=[
            pltpu.VMEM((width, width), BF16),
            pltpu.VMEM((ff // chunk, width, chunk), BF16),
            pltpu.VMEM((ff // chunk, width, chunk), BF16),
            pltpu.VMEM((ff // chunk, chunk, width), BF16),
            pltpu.SemaphoreType.DMA((1 + 3 * (ff // chunk),)),
        ],
        compiler_params=pltpu.CompilerParams(vmem_limit_bytes=VMEM_LIMIT),
        cost_estimate=COST,
        name="finish",
    )(fine, near, near_lse, coarse, gain, w_out, w_gate, w_up, w_down)


def local(
    fine,
    coarse,
    block_table,
    shifts,
    attn_gain,
    w_query,
    w_key,
    w_value,
    w_out,
    coarse_key,
    coarse_value,
    mlp_gain,
    w_gate,
    w_up,
    w_down,
):
    strips = lax.axis_size("tile")
    members = lax.axis_size("narrow")
    strip = lax.axis_index("tile").astype(jnp.int32)
    member = lax.axis_index("narrow").astype(jnp.int32)
    ids = jnp.stack([strip, member])
    rows, columns, width = fine.shape
    blocks, block_tokens, cw = coarse.shape
    total = blocks * strips
    n_own = blocks * block_tokens
    flat = fine.reshape(rows * columns, width)
    table = block_table.reshape(-1)
    gain = attn_gain.reshape(1, width)

    stay = lambda x: pltpu.with_memory_space_constraint(x, pltpu.HBM)
    flat_hbm = stay(flat)
    kv, pay_o, pay_e = project(
        ids, table, stay(coarse.reshape(n_own, cw)), stay(coarse_key), stay(coarse_value), flat_hbm, total
    )
    odd_pairs = [(i, (i - 1) % strips if i % 2 == 0 else (i + 1) % strips) for i in range(strips)]
    even_pairs = [(i, i ^ 1) for i in range(strips)]
    got_o = lax.ppermute(pay_o, "tile", odd_pairs)
    far_on = lax.ppermute(kv, "tile", [(i, (i + 3) % strips) for i in range(0, strips, 2)])
    got_e = lax.ppermute(pay_e, "tile", even_pairs)
    q, q_t = queries(got_e, flat_hbm, gain, stay(w_query))
    q_head = lax.all_to_all(q_t, "narrow", 0, 0, tiled=True)
    far_even = lax.ppermute(far_on, "tile", [(i + 1, i) for i in range(0, strips, 2)])
    far_odd = lax.ppermute(got_o, "tile", [(i, i + 1) for i in range(0, strips, 2)])

    stacked = stack_rows(ids, got_o, got_e, flat, n_own)
    stacked, q_head = lax.optimization_barrier((stacked, q_head))
    right_of = lax.ppermute(stacked, "narrow", [(i, (i - 1) % members) for i in range(members)])
    left_of = lax.ppermute(stacked, "narrow", [(i, (i + 1) % members) for i in range(members)])
    mark_row = n_own + rows * columns // 2 * (width // 128)
    table_before = jnp.where(strip % 2 == 0, got_o[mark_row, :8], got_e[mark_row, :8]).astype(jnp.int32)

    far = coarse_attention(
        left_of, right_of, ids, shifts, table, table_before, q_head, kv, got_o, got_e, far_even, far_odd, total
    )
    far = lax.all_to_all(far, "narrow", 0, 0, tiled=True)
    near, near_lse = window_attention(
        ids, shifts, left_of, stacked, right_of, q, gain, stay(w_key), stay(w_value), (strips - 1, members - 1)
    )
    out = finish(
        flat,
        near,
        near_lse,
        far,
        mlp_gain.reshape(1, width),
        stay(w_out),
        stay(w_gate),
        stay(w_up),
        stay(w_down),
    )
    return out.reshape(rows, columns, width)


def solution(mesh):
    placed = (
        P("tile", "narrow", None),
        P("tile", None, None),
        P("tile", None),
    ) + (P(),) * 12
    return jax.shard_map(
        local, mesh=mesh, in_specs=placed, out_specs=P("tile", "narrow", None), check_vma=False
    )
```

time: 95 us -> 80.5 us (0.85)
  the two profiles are of different devices: /device:TPU:2 before, /device:TPU:1 now
where the time goes in v2:
time: 80.5 us; the launch traced here: 79.3 us
  starting transfers between devices  44.2 us (55%)
  Pallas kernels  20 us (25%)
  waiting for transfers between devices  14.2 us (18%)
    ppermute x1, starting transfers between devices, local(): got_o = lax.ppermute(pay_o, 'tile', odd_pairs)  16.4 us
    all_to_all x1, starting transfers between devices, local(): far = lax.all_to_all(far, 'narrow', 0, 0, tiled=True)  7.95 us
    all_to_all x1, waiting for transfers between devices, local(): q_head = lax.all_to_all(q_t, 'narrow', 0, 0, tiled=True)  7.23 us
    pallas_call x1, Pallas kernels, window_attention(): pl.pallas_call(lambda *refs: window_kernel(last, *refs), in_specs=[smem,...  5.36 us
    pallas_call x1, Pallas kernels, finish(): pl.pallas_call(finish_kernel, in_specs=[vmem] * 5 + [hbm] * 4, out_specs=...  4.62 us
    all_to_all x1, starting transfers between devices, local(): q_head = lax.all_to_all(q_t, 'narrow', 0, 0, tiled=True)  4.52 us
    pallas_call x1, Pallas kernels, coarse_attention(): pl.pallas_call(lambda *refs: coarse_kernel(total, *refs), in_specs=[pl.Bl...  4.19 us
    ppermute x1, starting transfers between devices, local(): lax.ppermute(got_o, 'tile', [(i, i + 1) for i in range(0, strips, 2)])  4 us
  transfers between devices with their start and end apart: 9, of which 5 were waited for; matrix products, arithmetic and copies ran while one was open for 0% of the time, Pallas kernels for 10%

profile of v2, /device:TPU:1, one launch (start us, length us, event | category | flops | bytes accessed | tf_op | source)
XLA Modules:
  0.0 79.3 jit_solution(7564096820384624116)
XLA Ops:
  0.0 0.0 copy-start.1
  0.0 0.1 pad_add_fusion.refs_0_.ids.refs_2_
  0.1 0.0 copy-start.2
  0.1 0.7 copy-done.2
  0.7 0.0 copy-start
  0.7 3.2 %project.1 = (bf16[512,128]{1,0:T(8,128)(2,1)S(1)}, bf16[784,128]{1,0:T(8,128)(2,1)S(1)}, bf16[784,128]{1,0:T(8,128)(2,1)S(1)}) custom-call(s32[2]{0:T(128)S(1)} %pad_add_fusion.refs_0_.ids.refs_2_, s32[8]{0:T(128)S(1)} %bitcast.19, bf16[512,1024]{1,0:T(8,128)(2,1)} %bitcast.22, bf16[1024,512]{1,0:T(8,128)(2,1)} %refs_3_.2, bf16[1024,512]{1,0:T(8,128)(2,1)} %refs_4_.1, ...), custom_call_target="tpu_custom_call" | custom-call | flops 1000 | bytes 1000 | tf_op jit(solution)/shard_map/project/pallas_call | solution.py:93
  3.9 3.9 %collective-permute-start.1 = (bf16[784,128]{1,0:T(8,128)(2,1)S(1)}, bf16[784,128]{1,0:T(8,128)(2,1)S(1)}, u32[]{:S(2)}, u32[]{:S(2)}) collective-permute-start(bf16[784,128]{1,0:T(8,128)(2,1)S(1)} %get-tuple-element.15), channel_id=1, source_target_pairs={{0,8},{8,0},{16,24},{24,16},{32,40},{40,32},{48,56},{56,48},{64,72... | collective-permute-start | bytes 602120 | tf_op jit(solution)/shard_map/ppermute | solution.py:446
  7.9 16.4 %collective-permute-start = (bf16[784,128]{1,0:T(8,128)(2,1)S(1)}, bf16[784,128]{1,0:T(8,128)(2,1)S(1)}, u32[]{:S(2)}, u32[]{:S(2)}) collective-permute-start(bf16[784,128]{1,0:T(8,128)(2,1)S(1)} %get-tuple-element.14), channel_id=1, source_target_pairs={{0,504},{8,16},{16,8},{24,32},{32,24},{40,48},{48,40},{56,64},{64,... | collective-permute-start | bytes 602120 | tf_op jit(solution)/shard_map/ppermute | solution.py:444
  24.4 1.3 %collective-permute-start.4 = (bf16[512,128]{1,0:T(8,128)(2,1)S(1)}, bf16[512,128]{1,0:T(8,128)(2,1)S(1)}, u32[]{:S(2)}, u32[]{:S(2)}) collective-permute-start(bf16[512,128]{1,0:T(8,128)(2,1)S(1)} %get-tuple-element.22.refs_7_), channel_id=1, source_target_pairs={{0,24},{16,40},{32,56},{48,72},{64,88},{80,104},{96,120},{112,136}... | collective-permute-start | bytes 393224 | tf_op jit(solution)/shard_map/ppermute | solution.py:445
  25.7 0.0 collective-permute-done.1.b.after.refs_9_
  25.7 0.0 copy-done.1
  25.7 2.1 %queries.1 = (bf16[128,512]{1,0:T(8,128)(2,1)S(1)}, bf16[8,64,128]{2,1,0:T(8,128)(2,1)}) custom-call(bf16[784,128]{1,0:T(8,128)(2,1)S(1)} %collective-permute-done.1.b.after.refs_9_, bf16[128,512]{1,0:T(8,128)(2,1)} %bitcast.14, f32[1,512]{1,0:T(1,128)S(1)} %bitcast.17, bf16[512,512]{1,0:T(8,128)(2,1)} %w_q.1), custom_call_target="tpu_custom_call" | custom-call | flops 1000 | bytes 1000 | tf_op jit(solution)/shard_map/queries/pallas_call | solution.py:132
  27.8 4.5 %all-to-all-start = ((bf16[8,64,128]{2,1,0:T(8,128)(2,1)}), bf16[8,64,128]{2,1,0:T(8,128)(2,1)S(1)}, u32[]{:S(2)}, u32[]{:S(2)}) async-start(bf16[8,64,128]{2,1,0:T(8,128)(2,1)} %get-tuple-element.16), calls=%async_computation | async-start | bytes 262144 | tf_op jit(solution)/shard_map/all_to_all | solution.py:448
  32.3 0.0 copy-start.3
  32.3 0.0 copy-start.5
  32.3 3.6 %collective-permute-done.a.refs_8_ = bf16[784,128]{1,0:T(8,128)(2,1)S(1)} collective-permute-done((bf16[784,128]{1,0:T(8,128)(2,1)S(1)}, bf16[784,128]{1,0:T(8,128)(2,1)S(1)}, u32[]{:S(2)}, u32[]{:S(2)}) %collective-permute-start) | collective-permute-done | bytes 200736 | tf_op jit(solution)/shard_map/ppermute | solution.py:444
  36.0 0.0 copy-done
  36.0 0.6 stack_rows.1.refs_3_
  36.5 0.0 copy-start.4
  36.5 7.2 %all-to-all-done.refs_6_ = bf16[8,64,128]{2,1,0:T(8,128)(2,1)S(1)} async-done(((bf16[8,64,128]{2,1,0:T(8,128)(2,1)}), bf16[8,64,128]{2,1,0:T(8,128)(2,1)S(1)}, u32[]{:S(2)}, u32[]{:S(2)}) %all-to-all-start) | async-done | bytes 131104 | tf_op jit(solution)/shard_map/all_to_all | solution.py:448
  43.8 2.5 %collective-permute-start.2 = (bf16[256,512]{1,0:T(8,128)(2,1)S(1)}, bf16[256,512]{1,0:T(8,128)(2,1)S(1)}, u32[]{:S(2)}, u32[]{:S(2)}) collective-permute-start(bf16[256,512]{1,0:T(8,128)(2,1)S(1)} %stack_rows.1.refs_3_), channel_id=1, source_target_pairs={{0,1},{1,2},{2,3},{3,4},{4,5},{5,6},{6,7},{7,0},{8,9},{9,10},{10,1... | collective-permute-start | bytes 786440 | tf_op jit(solution)/shard_map/ppermute | solution.py:455
  46.3 2.3 %collective-permute-start.3 = (bf16[256,512]{1,0:T(8,128)(2,1)S(1)}, bf16[256,512]{1,0:T(8,128)(2,1)S(1)}, u32[]{:S(2)}, u32[]{:S(2)}) collective-permute-start(bf16[256,512]{1,0:T(8,128)(2,1)S(1)} %stack_rows.1.refs_3_), channel_id=1, source_target_pairs={{0,7},{1,0},{2,1},{3,2},{4,3},{5,4},{6,5},{7,6},{8,15},{9,8},{10,9... | collective-permute-start | bytes 786440 | tf_op jit(solution)/shard_map/ppermute | solution.py:454
  48.5 0.0 collective-permute-done.4
  48.6 1.3 %collective-permute-start.5 = (bf16[512,128]{1,0:T(8,128)(2,1)S(1)}, bf16[512,128]{1,0:T(8,128)(2,1)S(1)}, u32[]{:S(2)}, u32[]{:S(2)}) collective-permute-start(bf16[512,128]{1,0:T(8,128)(2,1)S(1)} %collective-permute-done.4), channel_id=1, source_target_pairs={{8,0},{24,16},{40,32},{56,48},{72,64},{88,80},{104,96},{120,112},{... | collective-permute-start | bytes 393224 | tf_op jit(solution)/shard_map/ppermute | solution.py:449
  49.9 4.0 %collective-permute-start.6 = (bf16[784,128]{1,0:T(8,128)(2,1)S(1)}, bf16[784,128]{1,0:T(8,128)(2,1)S(1)}, u32[]{:S(2)}, u32[]{:S(2)}) collective-permute-start(bf16[784,128]{1,0:T(8,128)(2,1)S(1)} %collective-permute-done.a.refs_8_), channel_id=1, source_target_pairs={{0,8},{16,24},{32,40},{48,56},{64,72},{80,88},{96,104},{112,120},{... | collective-permute-start | bytes 602120 | tf_op jit(solution)/shard_map/ppermute | solution.py:450
  53.9 0.7 collective-permute-done.5.refs_10_
  54.6 1.9 %collective-permute-done.6.refs_11_ = bf16[784,128]{1,0:T(8,128)(2,1)S(1)} collective-permute-done((bf16[784,128]{1,0:T(8,128)(2,1)S(1)}, bf16[784,128]{1,0:T(8,128)(2,1)S(1)}, u32[]{:S(2)}, u32[]{:S(2)}) %collective-permute-start.6) | collective-permute-done | bytes 200736 | tf_op jit(solution)/shard_map/ppermute | solution.py:450
  56.5 0.0 collective-permute-done.2.refs_2_.refs_0_
  56.5 0.0 collective-permute-done.3.refs_4_.refs_1_
  56.5 0.0 copy-done.3
  56.5 0.0 copy-done.5
  56.5 4.2 %coarse_attention.1 = bf16[8,80,128]{2,1,0:T(8,128)(2,1)} custom-call(bf16[256,512]{1,0:T(8,128)(2,1)S(1)} %collective-permute-done.2.refs_2_.refs_0_, bf16[256,512]{1,0:T(8,128)(2,1)S(1)} %collective-permute-done.3.refs_4_.refs_1_, s32[2]{0:T(128)S(1)} %pad_add_fusion.refs_0_.ids.refs_2_, s32[2]{0:T(128)S(1)} %copy-done.5, s32[8]{0:T(128)S(1)} %bitcast.20, ...), custom_call_target="tpu_custom_call" | custom-call | flops 1000 | bytes 1000 | tf_op jit(solution)/shard_map/coarse_attention/pallas_call | solution.py:328
  60.7 7.9 %all-to-all-start.1 = ((bf16[8,80,128]{2,1,0:T(8,128)(2,1)}), bf16[8,80,128]{2,1,0:T(8,128)(2,1)S(1)}, u32[]{:S(2)}, u32[]{:S(2)}) async-start(bf16[8,80,128]{2,1,0:T(8,128)(2,1)} %coarse_attention.1), calls=%async_computation.1 | async-start | bytes 327680 | tf_op jit(solution)/shard_map/all_to_all | solution.py:462
  68.7 5.4 %window_attention.1 = (f32[128,512]{1,0:T(8,128)S(1)}, f32[128,128]{1,0:T(8,128)S(1)}) custom-call(s32[2]{0:T(128)S(1)} %pad_add_fusion.refs_0_.ids.refs_2_, s32[2]{0:T(128)S(1)} %copy-done.5, bf16[256,512]{1,0:T(8,128)(2,1)S(1)} %collective-permute-done.2.refs_2_.refs_0_, bf16[256,512]{1,0:T(8,128)(2,1)S(1)} %stack_rows.1.refs_3_, ...), custom_call_target="tpu_custom_call" | custom-call | flops 1000 | bytes 1000 | tf_op jit(solution)/shard_map/window_attention/pallas_call | solution.py:246
  74.0 0.7 all-to-all-done.1.coarse
  74.7 0.0 copy-done.4
  74.7 4.6 %finish.1 = bf16[128,512]{1,0:T(8,128)(2,1)} custom-call(bf16[128,512]{1,0:T(8,128)(2,1)S(1)} %bitcast.16, f32[128,512]{1,0:T(8,128)S(1)} %get-tuple-element.19.near, f32[128,128]{1,0:T(8,128)S(1)} %get-tuple-element.20.near_lse, bf16[8,80,128]{2,1,0:T(8,128)(2,1)S(1)} %all-to-all-done.1.coarse, f32[1,512]{1,0:T(1,128)S(1)} %bitcast.21, ...), custom_call_target="tpu_custom_call" | custom-call | flops 1000 | bytes 1000 | tf_op jit(solution)/shard_map/finish/pallas_call | solution.py:389
  (1 shorter events, 0.0 us)
Async XLA Ops:
  0.0 25.7 %copy-start.1 = (f32[512]{0:T(512)S(1)}, f32[512]{0:T(512)}, u32[]{:S(2)}) copy-start(f32[512]{0:T(512)} %param.19) | copy-start | bytes 6148
  0.1 0.7 copy-start.2
  0.7 35.2 %copy-start = (bf16[16,8,512]{2,1,0:T(8,128)(2,1)S(1)}, bf16[16,8,512]{2,1,0:T(8,128)(2,1)}, u32[]{:S(2)}) copy-start(bf16[16,8,512]{2,1,0:T(8,128)(2,1)} %param.15) | copy-start | bytes 393220
  3.9 21.7 %collective-permute-start.1 = (bf16[784,128]{1,0:T(8,128)(2,1)S(1)}, bf16[784,128]{1,0:T(8,128)(2,1)S(1)}, u32[]{:S(2)}, u32[]{:S(2)}) collective-permute-start(bf16[784,128]{1,0:T(8,128)(2,1)S(1)} %get-tuple-element.15), channel_id=1, source_target_pairs={{0,8},{8,0},{16,24},{24,16},{32,40},{40,32},{48,56},{56,48},{64,72... | collective-permute-start | bytes 602120 | tf_op jit(solution)/shard_map/ppermute | solution.py:446
  7.9 28.0 %collective-permute-start = (bf16[784,128]{1,0:T(8,128)(2,1)S(1)}, bf16[784,128]{1,0:T(8,128)(2,1)S(1)}, u32[]{:S(2)}, u32[]{:S(2)}) collective-permute-start(bf16[784,128]{1,0:T(8,128)(2,1)S(1)} %get-tuple-element.14), channel_id=1, source_target_pairs={{0,504},{8,16},{16,8},{24,32},{32,24},{40,48},{48,40},{56,64},{64,... | collective-permute-start | bytes 602120 | tf_op jit(solution)/shard_map/ppermute | solution.py:444
  24.4 24.2 %collective-permute-start.4 = (bf16[512,128]{1,0:T(8,128)(2,1)S(1)}, bf16[512,128]{1,0:T(8,128)(2,1)S(1)}, u32[]{:S(2)}, u32[]{:S(2)}) collective-permute-start(bf16[512,128]{1,0:T(8,128)(2,1)S(1)} %get-tuple-element.22.refs_7_), channel_id=1, source_target_pairs={{0,24},{16,40},{32,56},{48,72},{64,88},{80,104},{96,120},{112,136}... | collective-permute-start | bytes 393224 | tf_op jit(solution)/shard_map/ppermute | solution.py:445
  27.8 16.0 %all-to-all-start = ((bf16[8,64,128]{2,1,0:T(8,128)(2,1)}), bf16[8,64,128]{2,1,0:T(8,128)(2,1)S(1)}, u32[]{:S(2)}, u32[]{:S(2)}) async-start(bf16[8,64,128]{2,1,0:T(8,128)(2,1)} %get-tuple-element.16), calls=%async_computation | async-start | bytes 262144 | tf_op jit(solution)/shard_map/all_to_all | solution.py:448
  32.3 24.2 %copy-start.3 = (s32[1,8]{1,0:T(1,128)S(1)}, s32[1,8]{1,0:T(1,128)}, u32[]{:S(2)}) copy-start(s32[1,8]{1,0:T(1,128)} %param.17) | copy-start | bytes 100
  32.3 24.2 %copy-start.5 = (s32[2]{0:T(128)S(1)}, s32[2]{0:T(128)}, u32[]{:S(2)}) copy-start(s32[2]{0:T(128)} %refs_3_.3) | copy-start | bytes 28
  36.5 38.1 %copy-start.4 = (f32[512]{0:T(512)S(1)}, f32[512]{0:T(512)}, u32[]{:S(2)}) copy-start(f32[512]{0:T(512)} %param.26) | copy-start | bytes 6148
  43.8 12.7 %collective-permute-start.2 = (bf16[256,512]{1,0:T(8,128)(2,1)S(1)}, bf16[256,512]{1,0:T(8,128)(2,1)S(1)}, u32[]{:S(2)}, u32[]{:S(2)}) collective-permute-start(bf16[256,512]{1,0:T(8,128)(2,1)S(1)} %stack_rows.1.refs_3_), channel_id=1, source_target_pairs={{0,1},{1,2},{2,3},{3,4},{4,5},{5,6},{6,7},{7,0},{8,9},{9,10},{10,1... | collective-permute-start | bytes 786440 | tf_op jit(solution)/shard_map/ppermute | solution.py:455
  46.3 10.2 %collective-permute-start.3 = (bf16[256,512]{1,0:T(8,128)(2,1)S(1)}, bf16[256,512]{1,0:T(8,128)(2,1)S(1)}, u32[]{:S(2)}, u32[]{:S(2)}) collective-permute-start(bf16[256,512]{1,0:T(8,128)(2,1)S(1)} %stack_rows.1.refs_3_), channel_id=1, source_target_pairs={{0,7},{1,0},{2,1},{3,2},{4,3},{5,4},{6,5},{7,6},{8,15},{9,8},{10,9... | collective-permute-start | bytes 786440 | tf_op jit(solution)/shard_map/ppermute | solution.py:454
  48.6 6.0 %collective-permute-start.5 = (bf16[512,128]{1,0:T(8,128)(2,1)S(1)}, bf16[512,128]{1,0:T(8,128)(2,1)S(1)}, u32[]{:S(2)}, u32[]{:S(2)}) collective-permute-start(bf16[512,128]{1,0:T(8,128)(2,1)S(1)} %collective-permute-done.4), channel_id=1, source_target_pairs={{8,0},{24,16},{40,32},{56,48},{72,64},{88,80},{104,96},{120,112},{... | collective-permute-start | bytes 393224 | tf_op jit(solution)/shard_map/ppermute | solution.py:449
  49.9 6.6 %collective-permute-start.6 = (bf16[784,128]{1,0:T(8,128)(2,1)S(1)}, bf16[784,128]{1,0:T(8,128)(2,1)S(1)}, u32[]{:S(2)}, u32[]{:S(2)}) collective-permute-start(bf16[784,128]{1,0:T(8,128)(2,1)S(1)} %collective-permute-done.a.refs_8_), channel_id=1, source_target_pairs={{0,8},{16,24},{32,40},{48,56},{64,72},{80,88},{96,104},{112,120},{... | collective-permute-start | bytes 602120 | tf_op jit(solution)/shard_map/ppermute | solution.py:450
  60.7 14.0 %all-to-all-start.1 = ((bf16[8,80,128]{2,1,0:T(8,128)(2,1)}), bf16[8,80,128]{2,1,0:T(8,128)(2,1)S(1)}, u32[]{:S(2)}, u32[]{:S(2)}) async-start(bf16[8,80,128]{2,1,0:T(8,128)(2,1)} %coarse_attention.1), calls=%async_computation.1 | async-start | bytes 327680 | tf_op jit(solution)/shard_map/all_to_all | solution.py:462

commit v3 on v2

--- a/solution.py
+++ b/solution.py
@@ -14,6 +14,10 @@
 LOW = -1e30
 VMEM_LIMIT = 24 * 1024 * 1024
 COST = pl.CostEstimate(flops=1000, bytes_accessed=1000, transcendentals=0)
+COST_ONWARD = pl.CostEstimate(flops=1000000000, bytes_accessed=1000, transcendentals=0)
+COST_STACK = pl.CostEstimate(flops=10000000000, bytes_accessed=1000, transcendentals=0)
+COST_CHOOSE = pl.CostEstimate(flops=10000000000, bytes_accessed=1000, transcendentals=0)
+COST_COARSE = pl.CostEstimate(flops=1000, bytes_accessed=1000, transcendentals=0)
 
 
 def iota(shape, dim):
@@ -30,13 +34,13 @@
     return [lax.rem(table[i] - first + 2 * total, total) for i in range(table.shape[0])]
 
 
-def project_kernel(total, ids, table, coarse, w_k, w_v, fine, kv, pay_o, pay_e, c_buf, k_buf, v_buf, x_buf, sems):
+def project_kernel(total, ids, table, coarse, w_k, w_v, fine, kv, pay_o, c_buf, w_buf, x_buf, sems):
     chunks = c_buf.shape[0]
     rows = c_buf.shape[1]
     cols = pl.ds(pl.multiple_of(ids[1] // 2 * 128, 128), 128)
     loads = [
-        pltpu.make_async_copy(w_k.at[:, cols], k_buf, sems.at[0]),
-        pltpu.make_async_copy(w_v.at[:, cols], v_buf, sems.at[1]),
+        pltpu.make_async_copy(w_k.at[:, cols], w_buf.at[:, 0:128], sems.at[0]),
+        pltpu.make_async_copy(w_v.at[:, cols], w_buf.at[:, 128:256], sems.at[1]),
         pltpu.make_async_copy(fine, x_buf, sems.at[2]),
     ]
     parts = [
@@ -58,28 +62,25 @@
         marks = jnp.where(lane == i, b.astype(F32), marks)
     end = base + half * (width // 128)
     pay_o[end : end + 16, :] = marks.astype(BF16)
-    pay_e[end : end + 16, :] = marks.astype(BF16)
     loads[0].wait()
     loads[1].wait()
     for i in range(chunks):
         parts[i].wait()
         tokens = c_buf[i]
-        key = jnp.dot(tokens, k_buf[...], preferred_element_type=F32)
-        value = jnp.dot(tokens, v_buf[...], preferred_element_type=F32)
+        product = jnp.dot(tokens, w_buf[...], preferred_element_type=F32)
+        key, value = product[:, 0:128], product[:, 128:256]
         key = jnp.where(odd_head, pltpu.roll(key, HD, 1), key)
         value = jnp.where(odd_head, value, pltpu.roll(value, HD, 1))
         both = jnp.where(low, key, value).astype(BF16)
         at = slice(rows * i, rows * i + rows)
         kv[at, :] = both
         pay_o[at, :] = both
-        pay_e[at, :] = both
     loads[2].wait()
     for c in range(width // 128):
         lanes = slice(128 * c, 128 * c + 128)
         at = slice(base + half * c, base + half * (c + 1))
         top, bottom = x_buf[0:half, lanes], x_buf[half:, lanes]
         pay_o[at, :] = jnp.where(even, top, bottom)
-        pay_e[at, :] = jnp.where(even, bottom, top)
 
 
 def project(ids, table, coarse, w_k, w_v, fine, total):
@@ -93,16 +94,14 @@
     return pl.pallas_call(
         lambda *refs: project_kernel(total, *refs),
         in_specs=[smem, smem] + [hbm] * 4,
-        out_specs=[vmem] * 3,
+        out_specs=[vmem] * 2,
         out_shape=[
             jax.ShapeDtypeStruct((n_coarse, 128), BF16),
             jax.ShapeDtypeStruct((pay_rows, 128), BF16),
-            jax.ShapeDtypeStruct((pay_rows, 128), BF16),
         ],
         scratch_shapes=[
             pltpu.VMEM((chunks, n_coarse // chunks, cw), BF16),
-            pltpu.VMEM((cw, 128), BF16),
-            pltpu.VMEM((cw, 128), BF16),
+            pltpu.VMEM((cw, 256), BF16),
             pltpu.VMEM((n_tok, width), BF16),
             pltpu.SemaphoreType.DMA((3 + chunks,)),
         ],
@@ -112,12 +111,23 @@
     )(ids, table, coarse, w_k, w_v, fine)
 
 
-def query_kernel(after, fine, gain, w_q, q_nat, q_t, x_buf, q_buf, sems):
+def query_kernel(ids, kv, pay_o, fine, gain, w_q, pay_e, q_nat, q_t, x_buf, q_buf, sems):
     first = pltpu.make_async_copy(fine, x_buf, sems.at[0])
     second = pltpu.make_async_copy(w_q, q_buf, sems.at[1])
     first.start()
     second.start()
+    base = kv.shape[0]
+    n_tok, width = x_buf.shape
+    half = n_tok // 2
+    end = base + half * (width // 128)
+    pay_e[0:base, :] = kv[...]
+    pay_e[end:, :] = pay_o[end:, :]
+    even = lax.rem(ids[0], 2) == 0
     first.wait()
+    for c in range(width // 128):
+        lanes = slice(128 * c, 128 * c + 128)
+        top, bottom = x_buf[0:half, lanes], x_buf[half:, lanes]
+        pay_e[base + half * c : base + half * (c + 1), :] = jnp.where(even, bottom, top)
     normed = rms(x_buf[...].astype(F32), gain[...]).astype(BF16)
     second.wait()
     q = jnp.dot(normed, q_buf[...], preferred_element_type=F32) * (1.0 / HD**0.5)
@@ -125,15 +135,16 @@
     q_t[...] = q.T.astype(BF16).reshape(q_t.shape)
 
 
-def queries(after, fine, gain, w_q):
+def queries(ids, kv, pay_o, fine, gain, w_q):
     n_tok, width = fine.shape
     hbm = pl.BlockSpec(memory_space=pltpu.HBM)
     vmem = pl.BlockSpec(memory_space=pltpu.VMEM)
     return pl.pallas_call(
         query_kernel,
-        in_specs=[pl.BlockSpec(memory_space=pl.ANY), hbm, vmem, hbm],
-        out_specs=[vmem] * 2,
+        in_specs=[pl.BlockSpec(memory_space=pltpu.SMEM), vmem, vmem, hbm, vmem, hbm],
+        out_specs=[vmem] * 3,
         out_shape=[
+            jax.ShapeDtypeStruct(pay_o.shape, BF16),
             jax.ShapeDtypeStruct((n_tok, width), BF16),
             jax.ShapeDtypeStruct((HEADS, HD, n_tok), BF16),
         ],
@@ -145,77 +156,95 @@
         compiler_params=pltpu.CompilerParams(vmem_limit_bytes=VMEM_LIMIT),
         cost_estimate=COST,
         name="queries",
-    )(after, fine, gain, w_q)
-
-
-def stack_kernel(ids, base, got_o, got_e, fine, out):
+    )(ids, kv, pay_o, fine, gain, w_q)
+
+
+def onward_kernel(ids, got_o, far_on, out):
+    out[...] = jnp.where(lax.rem(ids[0], 2) == 0, got_o[0 : out.shape[0], :], far_on[...])
+
+
+def pass_on(ids, got_o, far_on):
+    vmem = pl.BlockSpec(memory_space=pltpu.VMEM)
+    return pl.pallas_call(
+        onward_kernel,
+        in_specs=[pl.BlockSpec(memory_space=pltpu.SMEM), vmem, vmem],
+        out_specs=vmem,
+        out_shape=jax.ShapeDtypeStruct(far_on.shape, BF16),
+        compiler_params=pltpu.CompilerParams(vmem_limit_bytes=VMEM_LIMIT),
+        cost_estimate=COST_ONWARD,
+        name="pass_on",
+    )(ids, got_o, far_on)
+
+
+def stack_kernel(ids, shifts, base, got_o, got_e, fine, out, rows):
     n_tok, width = fine.shape
     half = n_tok // 2
-    out[half : half + n_tok, :] = fine[...]
     even = lax.rem(ids[0], 2) == 0
+    rows[half : half + n_tok, :] = fine[...].astype(F32)
     for c in range(width // 128):
         lanes = slice(128 * c, 128 * c + 128)
         at = slice(base + half * c, base + half * (c + 1))
-        a, b = got_o[at, :], got_e[at, :]
-        out[0:half, lanes] = jnp.where(even, a, b)
-        out[half + n_tok :, lanes] = jnp.where(even, b, a)
-
-
-def stack_rows(ids, got_o, got_e, fine, base):
+        a, b = got_o[at, :].astype(F32), got_e[at, :].astype(F32)
+        rows[0:half, lanes] = jnp.where(even, a, b)
+        rows[half + n_tok :, lanes] = jnp.where(even, b, a)
+    out[...] = rows[pl.ds(pl.multiple_of(shifts[0] * WS, WS), out.shape[0]), :].astype(BF16)
+
+
+def stack_rows(ids, shifts, got_o, got_e, fine, base):
     n_tok, width = fine.shape
     vmem = pl.BlockSpec(memory_space=pltpu.VMEM)
-    return pl.pallas_call(
-        lambda ids, a, b, x, out: stack_kernel(ids, base, a, b, x, out),
-        in_specs=[pl.BlockSpec(memory_space=pltpu.SMEM), vmem, vmem, vmem],
+    smem = pl.BlockSpec(memory_space=pltpu.SMEM)
+    return pl.pallas_call(
+        lambda ids, shifts, *refs: stack_kernel(ids, shifts, base, *refs),
+        in_specs=[smem, smem] + [vmem] * 3,
         out_specs=vmem,
-        out_shape=jax.ShapeDtypeStruct((2 * n_tok, width), BF16),
-        compiler_params=pltpu.CompilerParams(vmem_limit_bytes=VMEM_LIMIT),
-        cost_estimate=pl.CostEstimate(flops=10000000000, bytes_accessed=33333333, transcendentals=0),
+        out_shape=jax.ShapeDtypeStruct((n_tok + n_tok // 2, width), BF16),
+        scratch_shapes=[pltpu.VMEM((2 * n_tok, width), F32)],
+        compiler_params=pltpu.CompilerParams(vmem_limit_bytes=VMEM_LIMIT),
+        cost_estimate=COST_STACK,
         name="stack_rows",
-    )(ids, got_o, got_e, fine)
+    )(ids, shifts, got_o, got_e, fine)
 
 
 def window_kernel(last, ids, shifts, left, mid, right, q, gain, w_k, w_v, out, lse, k_buf, v_buf, sems):
     loads = [pltpu.make_async_copy(w_k, k_buf, sems.at[0]), pltpu.make_async_copy(w_v, v_buf, sems.at[1])]
     for copy in loads:
         copy.start()
-    span = left.shape[0]
-    side = span - 64
+    span, width = left.shape
     strip, member = ids[0], ids[1]
     shift_row, shift_col = shifts[0], shifts[1]
-    fine = jnp.concatenate([left[...], mid[...], right[...]], axis=0).astype(F32)
+    turn = lambda ref: pltpu.roll(ref[...].astype(F32).reshape(span // WS, WS, width), WS - shift_col, 1)
+    a, b, c = turn(left), turn(mid), turn(right)
+    stays = iota((1, WS, width), 1) < WS - shift_col
+    fine = jnp.concatenate([jnp.where(stays, a, b), jnp.where(stays, b, c)], axis=0).reshape(2 * span, width)
     normed = rms(fine, gain[...]).astype(BF16)
     loads[0].wait()
     keys = jnp.dot(normed, k_buf[...], preferred_element_type=F32).astype(BF16)
     loads[1].wait()
     values = jnp.dot(normed, v_buf[...], preferred_element_type=F32).astype(BF16)
-    shape = (128, 3 * side)
+    per = 2 * WS * WS
+    shape = (128, 2 * per)
     query = lax.rem(iota(shape, 0), 64)
-    column_q = lax.rem(query, 8)
+    column_q = lax.rem(query, WS)
     key = iota(shape, 1)
-    part = (key >= side).astype(jnp.int32) + (key >= 2 * side).astype(jnp.int32)
-    within = key - part * side
-    column_k = (part - 1) * 8 + lax.rem(within, 8)
-    same_col = lax.shift_right_arithmetic(column_q - shift_col + 16, 3) == lax.shift_right_arithmetic(
-        column_k - shift_col + 16, 3
-    )
-    wrap_col = ((column_k < 0) & (member == 0)) | ((column_k > 7) & (member == last[1]))
+    block = lax.shift_right_arithmetic(key, 7)
+    within = lax.bitwise_and(key, per - 1)
+    column_k = block * WS - WS + shift_col + lax.bitwise_and(within, WS - 1)
+    same_col = (column_q >= shift_col) == (block == 1)
+    wrap_col = ((column_k < 0) & (member == 0)) | ((column_k >= WS) & (member == last[1]))
+    low = iota((64, 128), 1) < HD
     lane = iota((64, 128), 1)
-    low = lane < HD
-    low_rows = iota((128, 128), 0) < 64
-    low_lanes = iota((128, 128), 1) < HD
-    own = low_rows == low_lanes
+    own = (iota((128, 128), 0) < 64) == (iota((128, 128), 1) < HD)
     for half in range(2):
-        row_q = 8 * half + lax.shift_right_arithmetic(query, 3)
-        row_k = 8 * half - 8 + lax.shift_right_arithmetic(within, 3)
-        same_row = lax.shift_right_arithmetic(row_q - shift_row + 16, 3) == lax.shift_right_arithmetic(
-            row_k - shift_row + 16, 3
-        )
-        wrap_row = ((row_k < 0) & (strip == 0)) | ((row_k > 15) & (strip == last[0]))
+        row_q = WS * half + lax.shift_right_arithmetic(query, 3)
+        line_k = WS * half + lax.shift_right_arithmetic(within, 3)
+        row_k = line_k + shift_row - WS
+        same_row = lax.shift_right_arithmetic(row_q - shift_row + WS, 3) == lax.shift_right_arithmetic(line_k, 3)
+        wrap_row = ((row_k < 0) & (strip == 0)) | ((row_k >= 2 * WS) & (strip == last[0]))
         seen = same_row & same_col & jnp.logical_not(wrap_row | wrap_col)
         rows = slice(64 * half, 64 * half + 64)
-        pick = lambda a: jnp.concatenate(
-            [a[span * b + 64 * half : span * b + 64 * half + side] for b in range(3)], axis=0
+        pick = lambda x: jnp.concatenate(
+            [x[span * i + 64 * half : span * i + 64 * half + per] for i in range(2)], axis=0
         )
         keys_h, values_h = pick(keys), pick(values)
         marks = jnp.zeros((64, 128), F32)
@@ -262,79 +291,104 @@
     )(ids, shifts, left, mid, right, q, gain, w_k, w_v)
 
 
-def coarse_kernel(total, after, after_too, ids, shifts, table, table_before, q_t, own, got_o, got_e, far_even, far_odd, out, store):
+def choose_kernel(total, ids, table, table_before, own, got_o, got_e, far, here_out, before_out, here_t, before_t, store):
     n_own = own.shape[0]
     per_strip = n_own // 128
     even = lax.rem(ids[0], 2) == 0
-    store[2 * per_strip : 3 * per_strip] = own[...].reshape(per_strip, 128, 128)
+    blocked = lambda ref: ref[0:n_own, :].reshape(per_strip, 128, 128)
+    store[0:per_strip] = blocked(far)
+    store[2 * per_strip : 3 * per_strip] = blocked(own)
 
     @pl.when(even)
     def _():
-        store[0:per_strip] = far_even[...].reshape(per_strip, 128, 128)
-        store[per_strip : 2 * per_strip] = got_o[0:n_own, :].reshape(per_strip, 128, 128)
-        store[3 * per_strip :] = got_e[0:n_own, :].reshape(per_strip, 128, 128)
+        store[per_strip : 2 * per_strip] = blocked(got_o)
+        store[3 * per_strip :] = blocked(got_e)
 
     @pl.when(jnp.logical_not(even))
     def _():
-        store[0:per_strip] = far_odd[0:n_own, :].reshape(per_strip, 128, 128)
-        store[per_strip : 2 * per_strip] = got_e[0:n_own, :].reshape(per_strip, 128, 128)
-        store[3 * per_strip :] = got_o[0:n_own, :].reshape(per_strip, 128, 128)
+        store[per_strip : 2 * per_strip] = blocked(got_e)
+        store[3 * per_strip :] = blocked(got_o)
 
     here = [b + per_strip for b in local_blocks(ids, table, per_strip, total)]
     before = [table_before[i] for i in range(table_before.shape[0])]
-    kv_here = jnp.concatenate([store[b] for b in here], axis=0)
-    kv_before = jnp.concatenate([store[b] for b in before], axis=0)
-    kv_here_t = kv_here.astype(F32).T.astype(BF16)
-    kv_before_t = kv_before.astype(F32).T.astype(BF16)
-    shift_row = shifts[0]
-    lane = lax.rem(iota((1, 256), 1), 128)
-    earlier = lane < WS * shift_row
+    for chosen, out, turned in ((here, here_out, here_t), (before, before_out, before_t)):
+        for i, b in enumerate(chosen):
+            block = store[b]
+            at = slice(128 * i, 128 * i + 128)
+            out[at, :] = block
+            turned[:, at] = block.astype(F32).T.astype(BF16)
+
+
+def choose_blocks(ids, table, table_before, own, got_o, got_e, far, total):
+    vmem = pl.BlockSpec(memory_space=pltpu.VMEM)
+    smem = pl.BlockSpec(memory_space=pltpu.SMEM)
+    keys = 128 * table.shape[0]
+    return pl.pallas_call(
+        lambda *refs: choose_kernel(total, *refs),
+        in_specs=[smem] * 3 + [vmem] * 4,
+        out_specs=[vmem] * 4,
+        out_shape=[jax.ShapeDtypeStruct((keys, 128), BF16)] * 2 + [jax.ShapeDtypeStruct((128, keys), BF16)] * 2,
+        scratch_shapes=[pltpu.VMEM((4 * own.shape[0] // 128, 128, 128), BF16)],
+        compiler_params=pltpu.CompilerParams(vmem_limit_bytes=VMEM_LIMIT),
+        cost_estimate=COST_CHOOSE,
+        name="choose_blocks",
+    )(ids, table, table_before, own, got_o, got_e, far)
+
+
+def coarse_kernel(after, after_too, shifts, q_t, here_ref, before_ref, here_t_ref, before_t_ref, out):
+    kv_here, kv_before, kv_here_t, kv_before_t = here_ref[...], before_ref[...], here_t_ref[...], before_t_ref[...]
+    low = iota((1, 128), 1) < 64
+    earlier = lax.rem(iota((1, 256), 1), 64) < WS * shifts[0]
     line = iota((16, 256), 0)
-    members = q_t.shape[0]
-    for p in range(members // 2):
-        q = jnp.concatenate([q_t[2 * p], q_t[2 * p + 1]], axis=1)
+    swap = lambda x: pltpu.roll(x, 64, 1)
+
+    def attend(q, mixed_rows):
         q = jnp.concatenate([q, jnp.zeros_like(q)], axis=0)
-        score = jnp.where(
-            earlier,
-            jnp.dot(kv_before, q, preferred_element_type=F32),
-            jnp.dot(kv_here, q, preferred_element_type=F32),
-        )
+        score = jnp.dot(kv_here, q, preferred_element_type=F32)
+        if mixed_rows:
+            score = jnp.where(earlier, jnp.dot(kv_before, q, preferred_element_type=F32), score)
         peak = jnp.max(score, axis=0, keepdims=True)
         weight = jnp.exp(score - peak)
         sums = jnp.sum(weight, axis=0, keepdims=True)
         weight = weight.astype(BF16)
-        mixed = jnp.where(
-            earlier,
-            jnp.dot(kv_before_t, weight, preferred_element_type=F32),
-            jnp.dot(kv_here_t, weight, preferred_element_type=F32),
-        )
-        mixed = (mixed[HD:] / sums).astype(BF16)
+        mixed = jnp.dot(kv_here_t, weight, preferred_element_type=F32)
+        if mixed_rows:
+            mixed = jnp.where(earlier, jnp.dot(kv_before_t, weight, preferred_element_type=F32), mixed)
         level = peak + jnp.log(sums)
         first = level.astype(BF16).astype(F32)
         second = (level - first).astype(BF16).astype(F32)
         third = level - first - second
         marks = jnp.where(line == 0, first, jnp.where(line == 1, second, jnp.where(line == 2, third, 0.0)))
-        marks = marks.astype(BF16)
-        for k in range(2):
-            lanes = slice(128 * k, 128 * k + 128)
-            out[2 * p + k, 0:HD, :] = mixed[:, lanes]
-            out[2 * p + k, HD : HD + 16, :] = marks[:, lanes]
-
-
-def coarse_attention(after, after_too, ids, shifts, table, table_before, q_t, own, got_o, got_e, far_even, far_odd, total):
-    vmem = pl.BlockSpec(memory_space=pltpu.VMEM)
-    smem = pl.BlockSpec(memory_space=pltpu.SMEM)
+        return jnp.concatenate([mixed[HD:] / sums, marks], axis=0)
+
+    for group in range(q_t.shape[0] // 4):
+        tops, bottoms = [], []
+        for pair in range(2):
+            a = q_t[4 * group + 2 * pair].astype(F32)
+            b = q_t[4 * group + 2 * pair + 1].astype(F32)
+            tops.append(jnp.where(low, a, swap(b)).astype(BF16))
+            bottoms.append(jnp.where(low, swap(a), b).astype(BF16))
+        top = attend(jnp.concatenate(tops, axis=1), True)
+        bottom = attend(jnp.concatenate(bottoms, axis=1), False)
+        for pair in range(2):
+            lanes = slice(128 * pair, 128 * pair + 128)
+            t, u = top[:, lanes], bottom[:, lanes]
+            out[4 * group + 2 * pair] = jnp.where(low, t, swap(u)).astype(BF16)
+            out[4 * group + 2 * pair + 1] = jnp.where(low, swap(t), u).astype(BF16)
+
+
+def coarse_attention(after, after_too, shifts, q_t, blocks):
+    vmem = pl.BlockSpec(memory_space=pltpu.VMEM)
     members, _, n_tok = q_t.shape
     return pl.pallas_call(
-        lambda *refs: coarse_kernel(total, *refs),
-        in_specs=[pl.BlockSpec(memory_space=pl.ANY)] * 2 + [smem] * 4 + [vmem] * 6,
+        coarse_kernel,
+        in_specs=[pl.BlockSpec(memory_space=pl.ANY)] * 2 + [pl.BlockSpec(memory_space=pltpu.SMEM)] + [vmem] * 5,
         out_specs=vmem,
         out_shape=jax.ShapeDtypeStruct((members, HD + 16, n_tok), BF16),
-        scratch_shapes=[pltpu.VMEM((4 * own.shape[0] // 128, 128, 128), BF16)],
-        compiler_params=pltpu.CompilerParams(vmem_limit_bytes=VMEM_LIMIT),
-        cost_estimate=COST,
+        compiler_params=pltpu.CompilerParams(vmem_limit_bytes=VMEM_LIMIT),
+        cost_estimate=COST_COARSE,
         name="coarse_attention",
-    )(after, after_too, ids, shifts, table, table_before, q_t, own, got_o, got_e, far_even, far_odd)
+    )(after, after_too, shifts, q_t, *blocks)
 
 
 def finish_kernel(
@@ -436,30 +490,30 @@
 
     stay = lambda x: pltpu.with_memory_space_constraint(x, pltpu.HBM)
     flat_hbm = stay(flat)
-    kv, pay_o, pay_e = project(
+    kv, pay_o = project(
         ids, table, stay(coarse.reshape(n_own, cw)), stay(coarse_key), stay(coarse_value), flat_hbm, total
     )
     odd_pairs = [(i, (i - 1) % strips if i % 2 == 0 else (i + 1) % strips) for i in range(strips)]
     even_pairs = [(i, i ^ 1) for i in range(strips)]
     got_o = lax.ppermute(pay_o, "tile", odd_pairs)
     far_on = lax.ppermute(kv, "tile", [(i, (i + 3) % strips) for i in range(0, strips, 2)])
+    pay_e, q, q_t = queries(ids, kv, pay_o, flat_hbm, gain, stay(w_query))
     got_e = lax.ppermute(pay_e, "tile", even_pairs)
-    q, q_t = queries(got_e, flat_hbm, gain, stay(w_query))
     q_head = lax.all_to_all(q_t, "narrow", 0, 0, tiled=True)
-    far_even = lax.ppermute(far_on, "tile", [(i + 1, i) for i in range(0, strips, 2)])
-    far_odd = lax.ppermute(got_o, "tile", [(i, i + 1) for i in range(0, strips, 2)])
-
-    stacked = stack_rows(ids, got_o, got_e, flat, n_own)
+
+    onward = pass_on(ids, got_o, far_on)
+    onward, got_o, got_e = lax.optimization_barrier((onward, got_o, got_e))
+    stacked = stack_rows(ids, shifts, got_o, got_e, flat, n_own)
     stacked, q_head = lax.optimization_barrier((stacked, q_head))
-    right_of = lax.ppermute(stacked, "narrow", [(i, (i - 1) % members) for i in range(members)])
-    left_of = lax.ppermute(stacked, "narrow", [(i, (i + 1) % members) for i in range(members)])
+    far = lax.ppermute(onward, "tile", even_pairs)
+    right_of = lax.ppermute(stacked, "narrow", [(i, i - 1) for i in range(1, members)])
+    left_of = lax.ppermute(stacked, "narrow", [(i, i + 1) for i in range(members - 1)])
     mark_row = n_own + rows * columns // 2 * (width // 128)
     table_before = jnp.where(strip % 2 == 0, got_o[mark_row, :8], got_e[mark_row, :8]).astype(jnp.int32)
 
-    far = coarse_attention(
-        left_of, right_of, ids, shifts, table, table_before, q_head, kv, got_o, got_e, far_even, far_odd, total
-    )
-    far = lax.all_to_all(far, "narrow", 0, 0, tiled=True)
+    blocks = choose_blocks(ids, table, table_before, kv, got_o, got_e, far, total)
+    from_coarse = coarse_attention(left_of, right_of, shifts, q_head, blocks)
+    from_coarse = lax.all_to_all(from_coarse, "narrow", 0, 0, tiled=True)
     near, near_lse = window_attention(
         ids, shifts, left_of, stacked, right_of, q, gain, stay(w_key), stay(w_value), (strips - 1, members - 1)
     )
@@ -467,7 +521,7 @@
         flat,
         near,
         near_lse,
-        far,
+        from_coarse,
         mlp_gain.reshape(1, width),
         stay(w_out),
         stay(w_gate),

time: 80.5 us -> 72 us (0.89)
  starting transfers between devices: 44.2 us -> 37.3 us
    all_to_all x1, waiting for transfers between devices: 7.23 us -> 0.71 us  [local(): q_head = lax.all_to_all(q_t, 'narrow', 0, 0, tiled=True)]
    all_to_all x1, starting transfers between devices: 7.95 us -> 3.92 us  [local(): from_coarse = lax.all_to_all(from_coarse, 'narrow', 0, 0, tiled=True)]
    pallas_call x1, Pallas kernels: 5.36 us -> 2.87 us  [window_attention(): pl.pallas_call(lambda *refs: window_kernel(last, *refs), in_specs=[smem,...]
    all_to_all x1, waiting for transfers between devices: 0.65 us -> 3.11 us  [local(): from_coarse = lax.all_to_all(from_coarse, 'narrow', 0, 0, tiled=True)]
    ppermute x4 -> x3, starting transfers between devices: 10 us -> 7.84 us  [the longest x1 4 us: local(): lax.ppermute(stacked, 'narrow', [(i, i + 1) for i in range(members - 1)])]
    pallas_call x3 -> x5, Pallas kernels: 6.86 us -> 8.86 us  [the longest x1 4.18 us: coarse_attention(): pl.pallas_call(coarse_kernel, in_specs=[pl.BlockSpec(memory_space=pl.ANY)...]
    ppermute x1, starting transfers between devices: 3.95 us -> 2.05 us  [local(): got_e = lax.ppermute(pay_e, 'tile', even_pairs)]
    ppermute x1, waiting for transfers between devices: 3.64 us -> 5.53 us  [local(): got_o = lax.ppermute(pay_o, 'tile', odd_pairs)]
  transfers between devices with their start and end apart: 9 -> 8, of which waited for: 5 -> 4; matrix products, arithmetic and copies ran while one was open for 0% -> 0% of each run, Pallas kernels for 10% -> 11%
where the time goes in v3:
time: 72 us; the launch traced here: 71.3 us
  starting transfers between devices  37.3 us (52%)
  Pallas kernels  19.5 us (27%)
  waiting for transfers between devices  13.5 us (19%)
    ppermute x1, starting transfers between devices, local(): got_o = lax.ppermute(pay_o, 'tile', odd_pairs)  17.9 us
    ppermute x1, waiting for transfers between devices, local(): got_o = lax.ppermute(pay_o, 'tile', odd_pairs)  5.53 us
    pallas_call x1, Pallas kernels, finish(): pl.pallas_call(finish_kernel, in_specs=[vmem] * 5 + [hbm] * 4, out_specs=...  4.62 us
    all_to_all x1, starting transfers between devices, local(): q_head = lax.all_to_all(q_t, 'narrow', 0, 0, tiled=True)  4.24 us
    pallas_call x1, Pallas kernels, coarse_attention(): pl.pallas_call(coarse_kernel, in_specs=[pl.BlockSpec(memory_space=pl.ANY)...  4.18 us
    ppermute x1, waiting for transfers between devices, local(): lax.ppermute(stacked, 'narrow', [(i, i - 1) for i in range(1, members)])  4.17 us
    ppermute x1, starting transfers between devices, local(): lax.ppermute(stacked, 'narrow', [(i, i + 1) for i in range(members - 1)])  4 us
    all_to_all x1, starting transfers between devices, local(): from_coarse = lax.all_to_all(from_coarse, 'narrow', 0, 0, tiled=True)  3.92 us
  transfers between devices with their start and end apart: 8, of which 4 were waited for; matrix products, arithmetic and copies ran while one was open for 0% of the time, Pallas kernels for 11%

profile of v3, /device:TPU:1, one launch (start us, length us, event | category | flops | bytes accessed | tf_op | source)
XLA Modules:
  0.0 71.3 jit_solution(13973943307285691207)
XLA Ops:
  0.0 0.0 copy-start.1
  0.0 0.1 pad_add_fusion.refs_0_.ids
  0.1 0.0 copy-start.4
  0.1 0.7 copy-done.4
  0.7 3.2 %project.1 = (bf16[512,128]{1,0:T(8,128)(2,1)S(1)}, bf16[784,128]{1,0:T(8,128)(2,1)S(1)}) custom-call(s32[2]{0:T(128)S(1)} %pad_add_fusion.refs_0_.ids, s32[8]{0:T(128)S(1)} %bitcast.20, bf16[512,1024]{1,0:T(8,128)(2,1)} %bitcast.22, bf16[1024,512]{1,0:T(8,128)(2,1)} %refs_3_.1, bf16[1024,512]{1,0:T(8,128)(2,1)} %refs_4_.1, bf16[128,512]{1,0:T(8,128)(2,1)} %bitcast.13), custom_call_target="tpu_custom_call" | custom-call | flops 1000 | bytes 1000 | tf_op jit(solution)/shard_map/project/pallas_call | solution.py:94
  3.9 17.9 %collective-permute-start = (bf16[784,128]{1,0:T(8,128)(2,1)S(1)}, bf16[784,128]{1,0:T(8,128)(2,1)S(1)}, u32[]{:S(2)}, u32[]{:S(2)}) collective-permute-start(bf16[784,128]{1,0:T(8,128)(2,1)S(1)} %get-tuple-element.21.pay_o), channel_id=1, source_target_pairs={{0,504},{8,16},{16,8},{24,32},{32,24},{40,48},{48,40},{56,64},{64,... | collective-permute-start | bytes 602120 | tf_op jit(solution)/shard_map/ppermute | solution.py:498
  21.9 1.3 %collective-permute-start.1 = (bf16[512,128]{1,0:T(8,128)(2,1)S(1)}, bf16[512,128]{1,0:T(8,128)(2,1)S(1)}, u32[]{:S(2)}, u32[]{:S(2)}) collective-permute-start(bf16[512,128]{1,0:T(8,128)(2,1)S(1)} %get-tuple-element.22.kv.refs_3_), channel_id=1, source_target_pairs={{0,24},{16,40},{32,56},{48,72},{64,88},{80,104},{96,120},{112,136}... | collective-permute-start | bytes 393224 | tf_op jit(solution)/shard_map/ppermute | solution.py:499
  23.2 0.0 copy-done.1
  23.2 2.6 %queries.1 = (bf16[784,128]{1,0:T(8,128)(2,1)S(1)}, bf16[128,512]{1,0:T(8,128)(2,1)S(1)}, bf16[8,64,128]{2,1,0:T(8,128)(2,1)}) custom-call(s32[2]{0:T(128)S(1)} %pad_add_fusion.refs_0_.ids, bf16[512,128]{1,0:T(8,128)(2,1)S(1)} %get-tuple-element.22.kv.refs_3_, bf16[784,128]{1,0:T(8,128)(2,1)S(1)} %get-tuple-element.21.pay_o, bf16[128,512]{1,0:T(8,128)(2,1)} %bitcast.14, ...), custom_call_target="tpu_custom_call" | custom-call | flops 1000 | bytes 1000 | tf_op jit(solution)/shard_map/queries/pallas_call | solution.py:142
  25.8 0.0 copy-start
  25.8 0.0 copy-start.3
  25.9 2.1 %collective-permute-start.2 = (bf16[784,128]{1,0:T(8,128)(2,1)S(1)}, bf16[784,128]{1,0:T(8,128)(2,1)S(1)}, u32[]{:S(2)}, u32[]{:S(2)}) collective-permute-start(bf16[784,128]{1,0:T(8,128)(2,1)S(1)} %get-tuple-element.23), channel_id=1, source_target_pairs={{0,8},{8,0},{16,24},{24,16},{32,40},{40,32},{48,56},{56,48},{64,72... | collective-permute-start | bytes 602120 | tf_op jit(solution)/shard_map/ppermute | solution.py:501
  27.9 4.2 %all-to-all-start = ((bf16[8,64,128]{2,1,0:T(8,128)(2,1)}), bf16[8,64,128]{2,1,0:T(8,128)(2,1)S(1)}, u32[]{:S(2)}, u32[]{:S(2)}) async-start(bf16[8,64,128]{2,1,0:T(8,128)(2,1)} %get-tuple-element.26), calls=%async_computation | async-start | bytes 262144 | tf_op jit(solution)/shard_map/all_to_all | solution.py:502
  32.2 0.0 collective-permute-done.1.far_on
  32.2 5.5 %collective-permute-done.got_o.refs_0_.refs_4_ = bf16[784,128]{1,0:T(8,128)(2,1)S(1)} collective-permute-done((bf16[784,128]{1,0:T(8,128)(2,1)S(1)}, bf16[784,128]{1,0:T(8,128)(2,1)S(1)}, u32[]{:S(2)}, u32[]{:S(2)}) %collective-permute-start) | collective-permute-done | bytes 200736 | tf_op jit(solution)/shard_map/ppermute | solution.py:498
  37.7 0.6 pass_on.1
  38.3 0.0 copy-start.5
  38.3 0.0 collective-permute-done.2.refs_1_.refs_5_
  38.3 1.9 %collective-permute-start.5 = (bf16[512,128]{1,0:T(8,128)(2,1)S(1)}, bf16[512,128]{1,0:T(8,128)(2,1)S(1)}, u32[]{:S(2)}, u32[]{:S(2)}) collective-permute-start(bf16[512,128]{1,0:T(8,128)(2,1)S(1)} %pass_on.1), channel_id=1, source_target_pairs={{0,8},{8,0},{16,24},{24,16},{32,40},{40,32},{48,56},{56,48},{64,72... | collective-permute-start | bytes 393224 | tf_op jit(solution)/shard_map/ppermute | solution.py:508
  40.2 0.0 copy-done
  40.2 0.0 copy-done.3
  40.2 0.6 stack_rows.1.refs_3_
  40.9 0.7 all-to-all-done.q_t
  41.6 4.0 %collective-permute-start.3 = (bf16[192,512]{1,0:T(8,128)(2,1)S(1)}, bf16[192,512]{1,0:T(8,128)(2,1)S(1)}, u32[]{:S(2)}, u32[]{:S(2)}) collective-permute-start(bf16[192,512]{1,0:T(8,128)(2,1)S(1)} %stack_rows.1.refs_3_), channel_id=1, source_target_pairs={{0,1},{1,2},{2,3},{3,4},{4,5},{5,6},{6,7},{8,9},{9,10},{10,11},{11... | collective-permute-start | bytes 589832 | tf_op jit(solution)/shard_map/ppermute | solution.py:510
  45.6 1.9 %collective-permute-start.4 = (bf16[192,512]{1,0:T(8,128)(2,1)S(1)}, bf16[192,512]{1,0:T(8,128)(2,1)S(1)}, u32[]{:S(2)}, u32[]{:S(2)}) collective-permute-start(bf16[192,512]{1,0:T(8,128)(2,1)S(1)} %stack_rows.1.refs_3_), channel_id=1, source_target_pairs={{1,0},{2,1},{3,2},{4,3},{5,4},{6,5},{7,6},{9,8},{10,9},{11,10},{12... | collective-permute-start | bytes 589832 | tf_op jit(solution)/shard_map/ppermute | solution.py:509
  47.5 0.0 collective-permute-done.5.refs_6_
  47.5 0.0 copy-done.5
  47.5 0.8 %choose_blocks.1 = (bf16[1024,128]{1,0:T(8,128)(2,1)S(1)}, bf16[1024,128]{1,0:T(8,128)(2,1)S(1)}, bf16[128,1024]{1,0:T(8,128)(2,1)S(1)}, bf16[128,1024]{1,0:T(8,128)(2,1)S(1)}) custom-call(s32[2]{0:T(128)S(1)} %pad_add_fusion.refs_0_.ids, s32[8]{0:T(128)S(1)} %bitcast.21, s32[8]{0:T(128)S(1)} %fusion.1.refs_2_, ...), custom_call_target="tpu_custom_call" | custom-call | flops 10000000000 | bytes 1000 | tf_op jit(solution)/shard_map/choose_blocks/pallas_call | solution.py:326
  48.4 0.0 copy-start.2
  48.4 0.0 collective-permute-done.3.refs_2_.after
  48.4 4.2 %collective-permute-done.4.refs_4_.after_too = bf16[192,512]{1,0:T(8,128)(2,1)S(1)} collective-permute-done((bf16[192,512]{1,0:T(8,128)(2,1)S(1)}, bf16[192,512]{1,0:T(8,128)(2,1)S(1)}, u32[]{:S(2)}, u32[]{:S(2)}) %collective-permute-start.4) | collective-permute-done | bytes 196640 | tf_op jit(solution)/shard_map/ppermute | solution.py:509
  52.6 4.2 %coarse_attention.1 = bf16[8,80,128]{2,1,0:T(8,128)(2,1)} custom-call(bf16[192,512]{1,0:T(8,128)(2,1)S(1)} %collective-permute-done.3.refs_2_.after, bf16[192,512]{1,0:T(8,128)(2,1)S(1)} %collective-permute-done.4.refs_4_.after_too, s32[2]{0:T(128)S(1)} %copy-done.3, bf16[8,64,128]{2,1,0:T(8,128)(2,1)S(1)} %all-to-all-done.q_t, ...), custom_call_target="tpu_custom_call" | custom-call | flops 1000 | bytes 1000 | tf_op jit(solution)/shard_map/coarse_attention/pallas_call | solution.py:383
  56.8 3.9 %all-to-all-start.1 = ((bf16[8,80,128]{2,1,0:T(8,128)(2,1)}), bf16[8,80,128]{2,1,0:T(8,128)(2,1)S(1)}, u32[]{:S(2)}, u32[]{:S(2)}) async-start(bf16[8,80,128]{2,1,0:T(8,128)(2,1)} %coarse_attention.1), calls=%async_computation.1 | async-start | bytes 327680 | tf_op jit(solution)/shard_map/all_to_all | solution.py:516
  60.7 2.9 %window_attention.1 = (f32[128,512]{1,0:T(8,128)S(1)}, f32[128,128]{1,0:T(8,128)S(1)}) custom-call(s32[2]{0:T(128)S(1)} %pad_add_fusion.refs_0_.ids, s32[2]{0:T(128)S(1)} %copy-done.3, bf16[192,512]{1,0:T(8,128)(2,1)S(1)} %collective-permute-done.3.refs_2_.after, bf16[192,512]{1,0:T(8,128)(2,1)S(1)} %stack_rows.1.refs_3_, ...), custom_call_target="tpu_custom_call" | custom-call | flops 1000 | bytes 1000 | tf_op jit(solution)/shard_map/window_attention/pallas_call | solution.py:275
  63.6 3.1 %all-to-all-done.1.coarse = bf16[8,80,128]{2,1,0:T(8,128)(2,1)S(1)} async-done(((bf16[8,80,128]{2,1,0:T(8,128)(2,1)}), bf16[8,80,128]{2,1,0:T(8,128)(2,1)S(1)}, u32[]{:S(2)}, u32[]{:S(2)}) %all-to-all-start.1) | async-done | bytes 163872 | tf_op jit(solution)/shard_map/all_to_all | solution.py:516
  66.7 0.0 copy-done.2
  66.7 4.6 %finish.1 = bf16[128,512]{1,0:T(8,128)(2,1)} custom-call(bf16[128,512]{1,0:T(8,128)(2,1)S(1)} %bitcast.16, f32[128,512]{1,0:T(8,128)S(1)} %get-tuple-element.29.near, f32[128,128]{1,0:T(8,128)S(1)} %get-tuple-element.30.near_lse, bf16[8,80,128]{2,1,0:T(8,128)(2,1)S(1)} %all-to-all-done.1.coarse, f32[1,512]{1,0:T(1,128)S(1)} %bitcast.19, ...), custom_call_target="tpu_custom_call" | custom-call | flops 1000 | bytes 1000 | tf_op jit(solution)/shard_map/finish/pallas_call | solution.py:443
  (1 shorter events, 0.0 us)
Async XLA Ops:
  0.0 23.2 %copy-start.1 = (f32[512]{0:T(512)S(1)}, f32[512]{0:T(512)}, u32[]{:S(2)}) copy-start(f32[512]{0:T(512)} %param.19) | copy-start | bytes 6148
  0.1 0.7 copy-start.4
  3.9 33.8 %collective-permute-start = (bf16[784,128]{1,0:T(8,128)(2,1)S(1)}, bf16[784,128]{1,0:T(8,128)(2,1)S(1)}, u32[]{:S(2)}, u32[]{:S(2)}) collective-permute-start(bf16[784,128]{1,0:T(8,128)(2,1)S(1)} %get-tuple-element.21.pay_o), channel_id=1, source_target_pairs={{0,504},{8,16},{16,8},{24,32},{32,24},{40,48},{48,40},{56,64},{64,... | collective-permute-start | bytes 602120 | tf_op jit(solution)/shard_map/ppermute | solution.py:498
  21.9 10.3 %collective-permute-start.1 = (bf16[512,128]{1,0:T(8,128)(2,1)S(1)}, bf16[512,128]{1,0:T(8,128)(2,1)S(1)}, u32[]{:S(2)}, u32[]{:S(2)}) collective-permute-start(bf16[512,128]{1,0:T(8,128)(2,1)S(1)} %get-tuple-element.22.kv.refs_3_), channel_id=1, source_target_pairs={{0,24},{16,40},{32,56},{48,72},{64,88},{80,104},{96,120},{112,136}... | collective-permute-start | bytes 393224 | tf_op jit(solution)/shard_map/ppermute | solution.py:499
  25.8 14.4 %copy-start = (bf16[16,8,512]{2,1,0:T(8,128)(2,1)S(1)}, bf16[16,8,512]{2,1,0:T(8,128)(2,1)}, u32[]{:S(2)}) copy-start(bf16[16,8,512]{2,1,0:T(8,128)(2,1)} %param.15) | copy-start | bytes 393220
  25.8 14.4 %copy-start.3 = (s32[2]{0:T(128)S(1)}, s32[2]{0:T(128)}, u32[]{:S(2)}) copy-start(s32[2]{0:T(128)} %shifts.3) | copy-start | bytes 28
  25.9 12.4 %collective-permute-start.2 = (bf16[784,128]{1,0:T(8,128)(2,1)S(1)}, bf16[784,128]{1,0:T(8,128)(2,1)S(1)}, u32[]{:S(2)}, u32[]{:S(2)}) collective-permute-start(bf16[784,128]{1,0:T(8,128)(2,1)S(1)} %get-tuple-element.23), channel_id=1, source_target_pairs={{0,8},{8,0},{16,24},{24,16},{32,40},{40,32},{48,56},{56,48},{64,72... | collective-permute-start | bytes 602120 | tf_op jit(solution)/shard_map/ppermute | solution.py:501
  27.9 13.7 %all-to-all-start = ((bf16[8,64,128]{2,1,0:T(8,128)(2,1)}), bf16[8,64,128]{2,1,0:T(8,128)(2,1)S(1)}, u32[]{:S(2)}, u32[]{:S(2)}) async-start(bf16[8,64,128]{2,1,0:T(8,128)(2,1)} %get-tuple-element.26), calls=%async_computation | async-start | bytes 262144 | tf_op jit(solution)/shard_map/all_to_all | solution.py:502
  38.3 9.3 %copy-start.5 = (s32[1,8]{1,0:T(1,128)S(1)}, s32[1,8]{1,0:T(1,128)}, u32[]{:S(2)}) copy-start(s32[1,8]{1,0:T(1,128)} %param.17) | copy-start | bytes 100
  38.3 9.2 %collective-permute-start.5 = (bf16[512,128]{1,0:T(8,128)(2,1)S(1)}, bf16[512,128]{1,0:T(8,128)(2,1)S(1)}, u32[]{:S(2)}, u32[]{:S(2)}) collective-permute-start(bf16[512,128]{1,0:T(8,128)(2,1)S(1)} %pass_on.1), channel_id=1, source_target_pairs={{0,8},{8,0},{16,24},{24,16},{32,40},{40,32},{48,56},{56,48},{64,72... | collective-permute-start | bytes 393224 | tf_op jit(solution)/shard_map/ppermute | solution.py:508
  41.6 6.8 %collective-permute-start.3 = (bf16[192,512]{1,0:T(8,128)(2,1)S(1)}, bf16[192,512]{1,0:T(8,128)(2,1)S(1)}, u32[]{:S(2)}, u32[]{:S(2)}) collective-permute-start(bf16[192,512]{1,0:T(8,128)(2,1)S(1)} %stack_rows.1.refs_3_), channel_id=1, source_target_pairs={{0,1},{1,2},{2,3},{3,4},{4,5},{5,6},{6,7},{8,9},{9,10},{10,11},{11... | collective-permute-start | bytes 589832 | tf_op jit(solution)/shard_map/ppermute | solution.py:510
  45.6 7.0 %collective-permute-start.4 = (bf16[192,512]{1,0:T(8,128)(2,1)S(1)}, bf16[192,512]{1,0:T(8,128)(2,1)S(1)}, u32[]{:S(2)}, u32[]{:S(2)}) collective-permute-start(bf16[192,512]{1,0:T(8,128)(2,1)S(1)} %stack_rows.1.refs_3_), channel_id=1, source_target_pairs={{1,0},{2,1},{3,2},{4,3},{5,4},{6,5},{7,6},{9,8},{10,9},{11,10},{12... | collective-permute-start | bytes 589832 | tf_op jit(solution)/shard_map/ppermute | solution.py:509
  48.4 18.3 %copy-start.2 = (f32[512]{0:T(512)S(1)}, f32[512]{0:T(512)}, u32[]{:S(2)}) copy-start(f32[512]{0:T(512)} %param.26) | copy-start | bytes 6148
  56.8 9.9 %all-to-all-start.1 = ((bf16[8,80,128]{2,1,0:T(8,128)(2,1)}), bf16[8,80,128]{2,1,0:T(8,128)(2,1)S(1)}, u32[]{:S(2)}, u32[]{:S(2)}) async-start(bf16[8,80,128]{2,1,0:T(8,128)(2,1)} %coarse_attention.1), calls=%async_computation.1 | async-start | bytes 327680 | tf_op jit(solution)/shard_map/all_to_all | solution.py:516

commit v4 on v3

v4 whole, which is shorter than its diff:
```python
import jax
import jax.numpy as jnp
from jax import lax
from jax.experimental import pallas as pl
from jax.experimental.pallas import tpu as pltpu
from jax.sharding import PartitionSpec as P

HEADS = 8
HD = 64
WS = 8
HALO = WS - 1
CHUNK = 512
EPS = 1e-06
F32 = jnp.float32
BF16 = jnp.bfloat16
LOW = -1e30
VMEM_LIMIT = 24 * 1024 * 1024
COST = pl.CostEstimate(flops=1000, bytes_accessed=1000, transcendentals=0)
COST_ONWARD = pl.CostEstimate(flops=1000000000, bytes_accessed=1000, transcendentals=0)
COST_STACK = pl.CostEstimate(flops=10000000000, bytes_accessed=1000, transcendentals=0)
COST_HERE = pl.CostEstimate(flops=1000, bytes_accessed=1000, transcendentals=0)
COST_CHOOSE = pl.CostEstimate(flops=10000000000, bytes_accessed=1000, transcendentals=0)


def iota(shape, dim):
    return lax.broadcasted_iota(jnp.int32, shape, dim)


def rms(x, gain):
    mean_square = jnp.mean(x * x, axis=-1, keepdims=True)
    return x * lax.rsqrt(mean_square + EPS) * gain


def local_blocks(ids, table, per_strip, total):
    first = (ids[0] - 1) * per_strip
    return [lax.rem(table[0, i] - first + 2 * total, total) for i in range(table.shape[1])]


def edge_rows(x, top):
    n_tok, width = x.shape
    halo = HALO * WS
    parts = []
    for c in range(width // 128):
        lanes = slice(128 * c, 128 * c + 128)
        first, last = x[0:64, lanes].astype(F32), x[n_tok - 64 :, lanes].astype(F32)
        parts.append(jnp.where(top, first[0:halo], last[64 - halo :]))
    return jnp.concatenate(parts, axis=0).astype(BF16)


def project_kernel(total, ids, table_in, coarse, w_k, w_v, fine, kv, pay_o, table, c_buf, w_buf, x_buf, sems):
    chunks = c_buf.shape[0]
    rows = c_buf.shape[1]
    cols = pl.ds(pl.multiple_of(ids[1] // 2 * 128, 128), 128)
    loads = [
        pltpu.make_async_copy(w_k.at[:, cols], w_buf.at[:, 0:128], sems.at[0]),
        pltpu.make_async_copy(w_v.at[:, cols], w_buf.at[:, 128:256], sems.at[1]),
        pltpu.make_async_copy(fine, x_buf, sems.at[2]),
        pltpu.make_async_copy(table_in, table, sems.at[3 + chunks]),
    ]
    parts = [
        pltpu.make_async_copy(coarse.at[pl.ds(rows * i, rows)], c_buf.at[i], sems.at[3 + i])
        for i in range(chunks)
    ]
    for copy in (loads[0], loads[1], *parts, loads[2], loads[3]):
        copy.start()
    odd_head = lax.rem(ids[1], 2) == 1
    even = lax.rem(ids[0], 2) == 0
    low = iota((rows, 128), 1) < HD
    base = kv.shape[0]
    n_tok, width = x_buf.shape
    half = n_tok // 2
    loads[0].wait()
    loads[1].wait()
    for i in range(chunks):
        parts[i].wait()
        tokens = c_buf[i]
        product = jnp.dot(tokens, w_buf[...], preferred_element_type=F32)
        key, value = product[:, 0:128], product[:, 128:256]
        key = jnp.where(odd_head, pltpu.roll(key, HD, 1), key)
        value = jnp.where(odd_head, value, pltpu.roll(value, HD, 1))
        both = jnp.where(low, key, value).astype(BF16)
        at = slice(rows * i, rows * i + rows)
        kv[at, :] = both
        pay_o[at, :] = both
    loads[3].wait()
    chosen = local_blocks(ids, table, base // 128, total)
    lane = iota((16, 128), 1)
    marks = jnp.zeros((16, 128), F32)
    for i, b in enumerate(chosen):
        marks = jnp.where(lane == i, b.astype(F32), marks)
    end = base + HALO * WS * (width // 128)
    pay_o[end : end + 16, :] = marks.astype(BF16)
    loads[2].wait()
    pay_o[base:end, :] = edge_rows(x_buf, even)


def project(ids, table, coarse, w_k, w_v, fine, total):
    n_coarse, cw = coarse.shape
    n_tok, width = fine.shape
    chunks = 2
    pay_rows = n_coarse + HALO * WS * (width // 128) + 16
    smem = pl.BlockSpec(memory_space=pltpu.SMEM)
    hbm = pl.BlockSpec(memory_space=pltpu.HBM)
    vmem = pl.BlockSpec(memory_space=pltpu.VMEM)
    return pl.pallas_call(
        lambda *refs: project_kernel(total, *refs),
        in_specs=[smem] + [hbm] * 5,
        out_specs=[vmem] * 2,
        out_shape=[
            jax.ShapeDtypeStruct((n_coarse, 128), BF16),
            jax.ShapeDtypeStruct((pay_rows, 128), BF16),
        ],
        scratch_shapes=[
            pltpu.SMEM(table.shape, jnp.int32),
            pltpu.VMEM((chunks, n_coarse // chunks, cw), BF16),
            pltpu.VMEM((cw, 256), BF16),
            pltpu.VMEM((n_tok, width), BF16),
            pltpu.SemaphoreType.DMA((4 + chunks,)),
        ],
        compiler_params=pltpu.CompilerParams(vmem_limit_bytes=VMEM_LIMIT),
        cost_estimate=COST,
        name="project",
    )(ids, table, coarse, w_k, w_v, fine)


def query_kernel(ids, kv, pay_o, fine, gain, w_q, pay_e, q_nat, q_t, x_buf, q_buf, sems):
    first = pltpu.make_async_copy(fine, x_buf, sems.at[0])
    second = pltpu.make_async_copy(w_q, q_buf, sems.at[1])
    first.start()
    second.start()
    base = kv.shape[0]
    n_tok, width = x_buf.shape
    halo = HALO * WS
    end = base + halo * (width // 128)
    pay_e[0:base, :] = kv[...]
    pay_e[end:, :] = pay_o[end:, :]
    even = lax.rem(ids[0], 2) == 0
    first.wait()
    pay_e[base:end, :] = edge_rows(x_buf, jnp.logical_not(even))
    normed = rms(x_buf[...].astype(F32), gain[...]).astype(BF16)
    second.wait()
    q = jnp.dot(normed, q_buf[...], preferred_element_type=F32) * (1.0 / HD**0.5)
    q_nat[...] = q.astype(BF16)
    q_t[...] = q.T.astype(BF16).reshape(q_t.shape)


def queries(ids, kv, pay_o, fine, gain, w_q):
    n_tok, width = fine.shape
    hbm = pl.BlockSpec(memory_space=pltpu.HBM)
    vmem = pl.BlockSpec(memory_space=pltpu.VMEM)
    return pl.pallas_call(
        query_kernel,
        in_specs=[pl.BlockSpec(memory_space=pltpu.SMEM), vmem, vmem, hbm, vmem, hbm],
        out_specs=[vmem] * 3,
        out_shape=[
            jax.ShapeDtypeStruct(pay_o.shape, BF16),
            jax.ShapeDtypeStruct((n_tok, width), BF16),
            jax.ShapeDtypeStruct((HEADS, HD, n_tok), BF16),
        ],
        scratch_shapes=[
            pltpu.VMEM((n_tok, width), BF16),
            pltpu.VMEM((width, width), BF16),
            pltpu.SemaphoreType.DMA((2,)),
        ],
        compiler_params=pltpu.CompilerParams(vmem_limit_bytes=VMEM_LIMIT),
        cost_estimate=COST,
        name="queries",
    )(ids, kv, pay_o, fine, gain, w_q)


def onward_kernel(ids, got_o, far_on, out):
    out[...] = jnp.where(lax.rem(ids[0], 2) == 0, got_o[0 : out.shape[0], :], far_on[...])


def pass_on(ids, got_o, far_on):
    vmem = pl.BlockSpec(memory_space=pltpu.VMEM)
    return pl.pallas_call(
        onward_kernel,
        in_specs=[pl.BlockSpec(memory_space=pltpu.SMEM), vmem, vmem],
        out_specs=vmem,
        out_shape=jax.ShapeDtypeStruct(far_on.shape, BF16),
        compiler_params=pltpu.CompilerParams(vmem_limit_bytes=VMEM_LIMIT),
        cost_estimate=COST_ONWARD,
        name="pass_on",
    )(ids, got_o, far_on)


def stack_kernel(ids, shifts, base, got_o, got_e, fine, out, rows):
    n_tok, width = fine.shape
    half = n_tok // 2
    even = lax.rem(ids[0], 2) == 0
    rows[half : half + n_tok, :] = fine[...].astype(F32)
    halo = HALO * WS
    end = base + halo * (width // 128)
    a, b = got_o[base:end, :].astype(F32), got_e[base:end, :].astype(F32)
    above, below = jnp.where(even, a, b), jnp.where(even, b, a)
    for c in range(width // 128):
        lanes = slice(128 * c, 128 * c + 128)
        at = slice(halo * c, halo * c + halo)
        rows[half - halo : half, lanes] = above[at]
        rows[half + n_tok : half + n_tok + halo, lanes] = below[at]
    out[...] = rows[pl.ds(pl.multiple_of(shifts[0] * WS, WS), out.shape[0]), :].astype(BF16)


def stack_rows(ids, shifts, got_o, got_e, fine, base):
    n_tok, width = fine.shape
    vmem = pl.BlockSpec(memory_space=pltpu.VMEM)
    smem = pl.BlockSpec(memory_space=pltpu.SMEM)
    return pl.pallas_call(
        lambda ids, shifts, *refs: stack_kernel(ids, shifts, base, *refs),
        in_specs=[smem, smem] + [vmem] * 3,
        out_specs=vmem,
        out_shape=jax.ShapeDtypeStruct((n_tok + n_tok // 2, width), BF16),
        scratch_shapes=[pltpu.VMEM((2 * n_tok, width), F32)],
        compiler_params=pltpu.CompilerParams(vmem_limit_bytes=VMEM_LIMIT),
        cost_estimate=COST_STACK,
        name="stack_rows",
    )(ids, shifts, got_o, got_e, fine)


def window_kernel(last, count, ids, shifts, left, mid, right, q, gain, w_k, w_v, *refs):
    weights, (out, lse), held = refs[:count], refs[count : count + 2], refs[count + 2 : 2 * count + 2]
    k_buf, v_buf, sems = refs[2 * count + 2 :]
    loads = [pltpu.make_async_copy(w_k, k_buf, sems.at[0]), pltpu.make_async_copy(w_v, v_buf, sems.at[1])]
    for copy in loads:
        copy.start()
    early = [
        pltpu.make_async_copy(w.at[0 : h.shape[0], 0 : h.shape[1]], h, sems.at[2 + i])
        for i, (w, h) in enumerate(zip(weights, held))
    ]
    span, width = left.shape
    strip, member = ids[0], ids[1]
    shift_row, shift_col = shifts[0], shifts[1]
    turn = lambda ref: pltpu.roll(ref[...].astype(F32).reshape(span // WS, WS, width), WS - shift_col, 1)
    a, b, c = turn(left), turn(mid), turn(right)
    stays = iota((1, WS, width), 1) < WS - shift_col
    fine = jnp.concatenate([jnp.where(stays, a, b), jnp.where(stays, b, c)], axis=0).reshape(2 * span, width)
    normed = rms(fine, gain[...]).astype(BF16)
    loads[0].wait()
    keys = jnp.dot(normed, k_buf[...], preferred_element_type=F32).astype(BF16)
    loads[1].wait()
    for copy in early:
        copy.start()
    values = jnp.dot(normed, v_buf[...], preferred_element_type=F32).astype(BF16)
    per = 2 * WS * WS
    shape = (128, 2 * per)
    query = lax.rem(iota(shape, 0), 64)
    column_q = lax.rem(query, WS)
    key = iota(shape, 1)
    block = lax.shift_right_arithmetic(key, 7)
    within = lax.bitwise_and(key, per - 1)
    column_k = block * WS - WS + shift_col + lax.bitwise_and(within, WS - 1)
    same_col = (column_q >= shift_col) == (block == 1)
    wrap_col = ((column_k < 0) & (member == 0)) | ((column_k >= WS) & (member == last[1]))
    low = iota((64, 128), 1) < HD
    lane = iota((64, 128), 1)
    own = (iota((128, 128), 0) < 64) == (iota((128, 128), 1) < HD)
    for half in range(2):
        row_q = WS * half + lax.shift_right_arithmetic(query, 3)
        line_k = WS * half + lax.shift_right_arithmetic(within, 3)
        row_k = line_k + shift_row - WS
        same_row = lax.shift_right_arithmetic(row_q - shift_row + WS, 3) == lax.shift_right_arithmetic(line_k, 3)
        wrap_row = ((row_k < 0) & (strip == 0)) | ((row_k >= 2 * WS) & (strip == last[0]))
        seen = same_row & same_col & jnp.logical_not(wrap_row | wrap_col)
        rows = slice(64 * half, 64 * half + 64)
        pick = lambda x: jnp.concatenate(
            [x[span * i + 64 * half : span * i + 64 * half + per] for i in range(2)], axis=0
        )
        keys_h, values_h = pick(keys), pick(values)
        marks = jnp.zeros((64, 128), F32)
        for pair in range(HEADS // 2):
            lanes = slice(128 * pair, 128 * pair + 128)
            q_pair = q[rows, lanes]
            q_both = jnp.concatenate([q_pair, q_pair], axis=0)
            q_both = jnp.where(own, q_both, jnp.zeros_like(q_both))
            score = lax.dot_general(
                q_both, keys_h[:, lanes], (((1,), (1,)), ((), ())), preferred_element_type=F32
            )
            score = jnp.where(seen, score, LOW)
            peak = jnp.max(score, axis=-1, keepdims=True)
            weight = jnp.exp(score - peak)
            total = jnp.sum(weight, axis=-1, keepdims=True)
            mixed = jnp.dot(weight.astype(BF16), values_h[:, lanes], preferred_element_type=F32) / total
            out[rows, lanes] = jnp.where(low, mixed[:64], mixed[64:])
            level = peak + jnp.log(total)
            marks = jnp.where(lane == 2 * pair, level[:64], marks)
            marks = jnp.where(lane == 2 * pair + 1, level[64:], marks)
        lse[rows, :] = marks
    for copy in early:
        copy.wait()


def window_attention(ids, shifts, left, mid, right, q, gain, w_k, w_v, weights, last):
    n_tok, width = q.shape
    count = len(weights)
    vmem = pl.BlockSpec(memory_space=pltpu.VMEM)
    smem = pl.BlockSpec(memory_space=pltpu.SMEM)
    return pl.pallas_call(
        lambda *refs: window_kernel(last, count, *refs),
        in_specs=[smem, smem] + [vmem] * 5 + [pl.BlockSpec(memory_space=pltpu.HBM)] * (2 + count),
        out_specs=[vmem] * (2 + count),
        out_shape=[
            jax.ShapeDtypeStruct((n_tok, width), F32),
            jax.ShapeDtypeStruct((n_tok, 128), F32),
        ]
        + [jax.ShapeDtypeStruct((min(w.shape[0], CHUNK), min(w.shape[1], CHUNK)), w.dtype) for w in weights],
        scratch_shapes=[
            pltpu.VMEM((width, width), BF16),
            pltpu.VMEM((width, width), BF16),
            pltpu.SemaphoreType.DMA((2 + count,)),
        ],
        compiler_params=pltpu.CompilerParams(vmem_limit_bytes=VMEM_LIMIT),
        cost_estimate=COST,
        name="window_attention",
    )(ids, shifts, left, mid, right, q, gain, w_k, w_v, *weights)


def attend(q, kv, kv_t):
    score = jnp.dot(kv, jnp.concatenate([q, jnp.zeros_like(q)], axis=0), preferred_element_type=F32)
    peak = jnp.max(score, axis=0, keepdims=True)
    weight = jnp.exp(score - peak)
    sums = jnp.sum(weight, axis=0, keepdims=True)
    mixed = jnp.dot(kv_t, weight.astype(BF16), preferred_element_type=F32)
    level = peak + jnp.log(sums)
    first = level.astype(BF16).astype(F32)
    second = (level - first).astype(BF16).astype(F32)
    third = level - first - second
    line = iota((16, q.shape[1]), 0)
    marks = jnp.where(line == 0, first, jnp.where(line == 1, second, jnp.where(line == 2, third, 0.0)))
    return jnp.concatenate([mixed[HD:] / sums, marks], axis=0)


def swap_halves(x):
    return pltpu.roll(x, 64, 1)


def top_rows(q_t, group):
    low = iota((1, 128), 1) < 64
    tiles = []
    for pair in range(2):
        a, b = (q_t[4 * group + 2 * pair + k].astype(F32) for k in range(2))
        tiles.append(jnp.where(low, a, swap_halves(b)).astype(BF16))
    return jnp.concatenate(tiles, axis=1)


def bottom_rows(q_t, group):
    low = iota((1, 128), 1) < 64
    tiles = []
    for pair in range(2):
        a, b = (q_t[4 * group + 2 * pair + k].astype(F32) for k in range(2))
        tiles.append(jnp.where(low, swap_halves(a), b).astype(BF16))
    return jnp.concatenate(tiles, axis=1)


def here_kernel(total, ids, table, q_t, own, got_o, got_e, out, store, turned):
    n_own = own.shape[0]
    per_strip = n_own // 128
    even = lax.rem(ids[0], 2) == 0
    blocked = lambda ref: ref[0:n_own, :].reshape(per_strip, 128, 128)
    above, below = blocked(got_o), blocked(got_e)
    store[0:per_strip] = jnp.where(even, above, below)
    store[per_strip : 2 * per_strip] = blocked(own)
    store[2 * per_strip :] = jnp.where(even, below, above)
    chosen = local_blocks(ids, table, per_strip, total)
    kv = jnp.concatenate([store[b] for b in chosen], axis=0)
    turned[...] = kv.astype(F32).T.astype(BF16)
    kv_t = turned[...]
    low = iota((1, 128), 1) < 64
    for group in range(q_t.shape[0] // 4):
        top = attend(top_rows(q_t, group), kv, kv_t)
        bottom = attend(bottom_rows(q_t, group), kv, kv_t)
        for pair in range(2):
            lanes = slice(128 * pair, 128 * pair + 128)
            t, u = top[:, lanes], bottom[:, lanes]
            out[4 * group + 2 * pair] = jnp.where(low, t, swap_halves(u)).astype(BF16)
            out[4 * group + 2 * pair + 1] = jnp.where(low, swap_halves(t), u).astype(BF16)


def here_attention(ids, table, q_t, own, got_o, got_e, total):
    vmem = pl.BlockSpec(memory_space=pltpu.VMEM)
    smem = pl.BlockSpec(memory_space=pltpu.SMEM)
    members, _, n_tok = q_t.shape
    return pl.pallas_call(
        lambda *refs: here_kernel(total, *refs),
        in_specs=[smem, smem] + [vmem] * 4,
        out_specs=vmem,
        out_shape=jax.ShapeDtypeStruct((members, HD + 16, n_tok), BF16),
        scratch_shapes=[
            pltpu.VMEM((3 * own.shape[0] // 128, 128, 128), BF16),
            pltpu.VMEM((128, 128 * table.shape[1]), BF16),
        ],
        compiler_params=pltpu.CompilerParams(vmem_limit_bytes=VMEM_LIMIT),
        cost_estimate=COST_HERE,
        name="here_attention",
    )(ids, table, q_t, own, got_o, got_e)


def choose_kernel(after, ids, table, far, got_o, got_e, own, kv, kv_t, store):
    n_own = own.shape[0]
    per_strip = n_own // 128
    even = lax.rem(ids[0], 2) == 0
    blocked = lambda ref: ref[0:n_own, :].reshape(per_strip, 128, 128)
    store[0:per_strip] = blocked(far)
    store[per_strip : 2 * per_strip] = jnp.where(even, blocked(got_o), blocked(got_e))
    store[2 * per_strip :] = blocked(own)
    for i in range(table.shape[0]):
        block = store[table[i]]
        at = slice(128 * i, 128 * i + 128)
        kv[at, :] = block
        kv_t[:, at] = block.astype(F32).T.astype(BF16)


def choose_blocks(after, ids, table, far, got_o, got_e, own):
    vmem = pl.BlockSpec(memory_space=pltpu.VMEM)
    smem = pl.BlockSpec(memory_space=pltpu.SMEM)
    keys = 128 * table.shape[0]
    return pl.pallas_call(
        choose_kernel,
        in_specs=[pl.BlockSpec(memory_space=pl.ANY), smem, smem] + [vmem] * 4,
        out_specs=[vmem] * 2,
        out_shape=[jax.ShapeDtypeStruct((keys, 128), BF16), jax.ShapeDtypeStruct((128, keys), BF16)],
        scratch_shapes=[pltpu.VMEM((3 * own.shape[0] // 128, 128, 128), BF16)],
        compiler_params=pltpu.CompilerParams(vmem_limit_bytes=VMEM_LIMIT),
        cost_estimate=COST_CHOOSE,
        name="choose_blocks",
    )(after, ids, table, far, got_o, got_e, own)


def before_kernel(after, after_too, shifts, q_t, kv, kv_t, here, out):
    lane = iota((1, 128), 1)
    earlier = lane < WS * shifts[0]
    for group in range(q_t.shape[0] // 4):
        top = attend(top_rows(q_t, group), kv[...], kv_t[...])
        for pair in range(2):
            t = top[:, 128 * pair : 128 * pair + 128]
            for k in range(2):
                m = 4 * group + 2 * pair + k
                mine = t if k == 0 else swap_halves(t)
                out[m] = jnp.where(earlier, mine, here[m].astype(F32)).astype(BF16)


def before_attention(after, after_too, shifts, q_t, kv, kv_t, here):
    vmem = pl.BlockSpec(memory_space=pltpu.VMEM)
    return pl.pallas_call(
        before_kernel,
        in_specs=[pl.BlockSpec(memory_space=pl.ANY)] * 2 + [pl.BlockSpec(memory_space=pltpu.SMEM)] + [vmem] * 4,
        out_specs=vmem,
        out_shape=jax.ShapeDtypeStruct(here.shape, BF16),
        compiler_params=pltpu.CompilerParams(vmem_limit_bytes=VMEM_LIMIT),
        cost_estimate=COST,
        name="before_attention",
    )(after, after_too, shifts, q_t, kv, kv_t, here)


def finish_kernel(
    fine, near, near_lse, coarse, gain, w_out, gate_0, up_0, down_0, w_gate, w_up, w_down, out, g_buf, u_buf, d_buf, sems
):
    steps = w_gate.shape[1] // CHUNK
    loads = []
    for i in range(1, steps):
        at = pl.ds(CHUNK * i, CHUNK)
        loads.append(
            [
                pltpu.make_async_copy(w_gate.at[:, at], g_buf.at[i - 1], sems.at[3 * i - 3]),
                pltpu.make_async_copy(w_up.at[:, at], u_buf.at[i - 1], sems.at[3 * i - 2]),
                pltpu.make_async_copy(w_down.at[at], d_buf.at[i - 1], sems.at[3 * i - 1]),
            ]
        )
    for group in loads:
        for copy in group:
            copy.start()
    heads = coarse.shape[0]
    far = jnp.concatenate([coarse[h, 0:HD, :].astype(F32) for h in range(heads)], axis=0).T
    marks = [coarse[h, HD : HD + 16, :].astype(F32) for h in range(heads)]
    level = jnp.concatenate([m[0:1] + m[1:2] + m[2:3] for m in marks], axis=0).T
    diff = near_lse[:, 0:heads] - level
    share = 1.0 / (1.0 + jnp.exp(diff))
    share = jnp.concatenate(
        [jnp.broadcast_to(share[:, h : h + 1], (share.shape[0], HD)) for h in range(heads)], axis=1
    )
    head_out = (near[...] * (1.0 - share) + far * share).astype(BF16)
    mid = fine[...].astype(F32) + jnp.dot(head_out, w_out[...], preferred_element_type=F32)
    normed = rms(mid, gain[...]).astype(BF16)
    total = mid
    for i in range(steps):
        if i == 0:
            parts = (gate_0, up_0, down_0)
        else:
            for copy in loads[i - 1]:
                copy.wait()
            parts = (g_buf.at[i - 1], u_buf.at[i - 1], d_buf.at[i - 1])
        gate = jnp.dot(normed, parts[0][...], preferred_element_type=F32)
        up = jnp.dot(normed, parts[1][...], preferred_element_type=F32)
        hidden = (gate * (1.0 / (1.0 + jnp.exp(-gate))) * up).astype(BF16)
        total = total + jnp.dot(hidden, parts[2][...], preferred_element_type=F32)
    out[...] = total.astype(BF16)


def finish(fine, near, near_lse, coarse, gain, w_out, gate_0, up_0, down_0, w_gate, w_up, w_down):
    n_tok, width = fine.shape
    rest = w_gate.shape[1] // CHUNK - 1
    vmem = pl.BlockSpec(memory_space=pltpu.VMEM)
    hbm = pl.BlockSpec(memory_space=pltpu.HBM)
    return pl.pallas_call(
        finish_kernel,
        in_specs=[vmem] * 9 + [hbm] * 3,
        out_specs=vmem,
        out_shape=jax.ShapeDtypeStruct((n_tok, width), BF16),
        scratch_shapes=[
            pltpu.VMEM((rest, width, CHUNK), BF16),
            pltpu.VMEM((rest, width, CHUNK), BF16),
            pltpu.VMEM((rest, CHUNK, width), BF16),
            pltpu.SemaphoreType.DMA((3 * rest,)),
        ],
        compiler_params=pltpu.CompilerParams(vmem_limit_bytes=VMEM_LIMIT),
        cost_estimate=COST,
        name="finish",
    )(fine, near, near_lse, coarse, gain, w_out, gate_0, up_0, down_0, w_gate, w_up, w_down)


def local(
    fine,
    coarse,
    block_table,
    shifts,
    attn_gain,
    w_query,
    w_key,
    w_value,
    w_out,
    coarse_key,
    coarse_value,
    mlp_gain,
    w_gate,
    w_up,
    w_down,
):
    strips = lax.axis_size("tile")
    members = lax.axis_size("narrow")
    strip = lax.axis_index("tile").astype(jnp.int32)
    member = lax.axis_index("narrow").astype(jnp.int32)
    ids = jnp.stack([strip, member])
    rows, columns, width = fine.shape
    blocks, block_tokens, cw = coarse.shape
    total = blocks * strips
    n_own = blocks * block_tokens
    flat = fine.reshape(rows * columns, width)
    table = block_table
    gain = attn_gain.reshape(1, width)

    stay = lambda x: pltpu.with_memory_space_constraint(x, pltpu.HBM)
    flat_hbm = stay(flat)
    kv, pay_o = project(
        ids, stay(table), stay(coarse.reshape(n_own, cw)), stay(coarse_key), stay(coarse_value), flat_hbm, total
    )
    odd_pairs = [(i, (i - 1) % strips if i % 2 == 0 else (i + 1) % strips) for i in range(strips)]
    even_pairs = [(i, i ^ 1) for i in range(strips)]
    got_o = lax.ppermute(pay_o, "tile", odd_pairs)
    far_on = lax.ppermute(kv, "tile", [(i, (i + 3) % strips) for i in range(0, strips, 2)])
    pay_e, q, q_t = queries(ids, kv, pay_o, flat_hbm, gain, stay(w_query))
    got_e = lax.ppermute(pay_e, "tile", even_pairs)
    q_head = lax.all_to_all(q_t, "narrow", 0, 0, tiled=True)

    onward = pass_on(ids, got_o, far_on)
    onward, got_o, got_e = lax.optimization_barrier((onward, got_o, got_e))
    stacked = stack_rows(ids, shifts, got_o, got_e, flat, n_own)
    stacked, q_head = lax.optimization_barrier((stacked, q_head))
    far = lax.ppermute(onward, "tile", even_pairs)
    right_of = lax.ppermute(stacked, "narrow", [(i, i - 1) for i in range(1, members)])
    left_of = lax.ppermute(stacked, "narrow", [(i, i + 1) for i in range(members - 1)])
    mark_row = n_own + HALO * WS * (width // 128)
    table_before = jnp.where(strip % 2 == 0, got_o[mark_row, :8], got_e[mark_row, :8]).astype(jnp.int32)

    here = here_attention(ids, table, q_head, kv, got_o, got_e, total)
    kv_before, kv_before_t = choose_blocks(here, ids, table_before, far, got_o, got_e, kv)
    from_coarse = before_attention(left_of, right_of, shifts, q_head, kv_before, kv_before_t, here)
    from_coarse = lax.all_to_all(from_coarse, "narrow", 0, 0, tiled=True)
    near, near_lse, *held = window_attention(
        ids,
        shifts,
        left_of,
        stacked,
        right_of,
        q,
        gain,
        stay(w_key),
        stay(w_value),
        (stay(w_out), stay(w_gate), stay(w_up), stay(w_down)),
        (strips - 1, members - 1),
    )
    out = finish(
        flat,
        near,
        near_lse,
        from_coarse,
        mlp_gain.reshape(1, width),
        *held,
        stay(w_gate),
        stay(w_up),
        stay(w_down),
    )
    return out.reshape(rows, columns, width)


def solution(mesh):
    placed = (
        P("tile", "narrow", None),
        P("tile", None, None),
        P("tile", None),
    ) + (P(),) * 12
    return jax.shard_map(
        local, mesh=mesh, in_specs=placed, out_specs=P("tile", "narrow", None), check_vma=False
    )
```

time: 72 us -> 68.2 us (0.947)
  waiting for transfers between devices: 13.5 us -> 7.67 us
  Pallas kernels: 19.5 us -> 21.8 us
    ppermute x1, waiting for transfers between devices: 4.17 us -> 0.01 us  [local(): lax.ppermute(stacked, 'narrow', [(i, i - 1) for i in range(1, members)])]
    pallas_call x4 -> x5, Pallas kernels: 12.5 us -> 15.1 us  [the longest x1 4.14 us: finish(): pl.pallas_call(finish_kernel, in_specs=[vmem] * 9 + [hbm] * 3, out_specs=...]
    all_to_all x1, waiting for transfers between devices: 3.11 us -> 2.11 us  [local(): from_coarse = lax.all_to_all(from_coarse, 'narrow', 0, 0, tiled=True)]
    ppermute x1, waiting for transfers between devices: 5.53 us -> 4.72 us  [local(): got_o = lax.ppermute(pay_o, 'tile', odd_pairs)]
  transfers between devices with their start and end apart: 8 -> 8, of which waited for: 4 -> 3; matrix products, arithmetic and copies ran while one was open for 0% -> 0% of each run, Pallas kernels for 11% -> 18%
where the time goes in v4:
time: 68.2 us; the launch traced here: 67.5 us
  starting transfers between devices  37.7 us (55%)
  Pallas kernels  21.8 us (32%)
  waiting for transfers between devices  7.67 us (11%)
    ppermute x1, starting transfers between devices, local(): got_o = lax.ppermute(pay_o, 'tile', odd_pairs)  17.9 us
    ppermute x1, waiting for transfers between devices, local(): got_o = lax.ppermute(pay_o, 'tile', odd_pairs)  4.72 us
    all_to_all x1, starting transfers between devices, local(): from_coarse = lax.all_to_all(from_coarse, 'narrow', 0, 0, tiled=True)  4.35 us
    all_to_all x1, starting transfers between devices, local(): q_head = lax.all_to_all(q_t, 'narrow', 0, 0, tiled=True)  4.24 us
    pallas_call x1, Pallas kernels, finish(): pl.pallas_call(finish_kernel, in_specs=[vmem] * 9 + [hbm] * 3, out_specs=...  4.14 us
    pallas_call x1, Pallas kernels, window_attention(): pl.pallas_call(lambda *refs: window_kernel(last, count, *refs), in_specs=...  3.87 us
    pallas_call x1, Pallas kernels, here_attention(): pl.pallas_call(lambda *refs: here_kernel(total, *refs), in_specs=[smem, s...  3.53 us
    ppermute x1, starting transfers between devices, local(): lax.ppermute(stacked, 'narrow', [(i, i + 1) for i in range(members - 1)])  3.39 us
  transfers between devices with their start and end apart: 8, of which 3 were waited for; matrix products, arithmetic and copies ran while one was open for 0% of the time, Pallas kernels for 18%

profile of v4, /device:TPU:1, one launch (start us, length us, event | category | flops | bytes accessed | tf_op | source)
XLA Modules:
  0.0 67.5 jit_solution(15641963358582805644)
XLA Ops:
  0.0 0.0 copy-start.1
  0.0 0.1 pad_add_fusion.refs_0_.ids
  0.1 2.9 %project.1 = (bf16[512,128]{1,0:T(8,128)(2,1)S(1)}, bf16[752,128]{1,0:T(8,128)(2,1)S(1)}) custom-call(s32[2]{0:T(128)S(1)} %pad_add_fusion.refs_0_.ids, s32[1,8]{1,0:T(1,128)} %refs_1_.5, bf16[512,1024]{1,0:T(8,128)(2,1)} %bitcast.19, bf16[1024,512]{1,0:T(8,128)(2,1)} %refs_3_.1, bf16[1024,512]{1,0:T(8,128)(2,1)} %refs_4_.1, bf16[128,512]{1,0:T(8,128)(2,1)} %bitcast.12), custom_call_target="tpu_custom_call" | custom-call | flops 1000 | bytes 1000 | tf_op jit(solution)/shard_map/project/pallas_call | solution.py:105
  2.9 17.9 %collective-permute-start = (bf16[752,128]{1,0:T(8,128)(2,1)S(1)}, bf16[752,128]{1,0:T(8,128)(2,1)S(1)}, u32[]{:S(2)}, u32[]{:S(2)}) collective-permute-start(bf16[752,128]{1,0:T(8,128)(2,1)S(1)} %get-tuple-element.23.pay_o), channel_id=1, source_target_pairs={{0,504},{8,16},{16,8},{24,32},{32,24},{40,48},{48,40},{56,64},{64,... | collective-permute-start | bytes 577544 | tf_op jit(solution)/shard_map/ppermute | solution.py:558
  20.9 1.3 %collective-permute-start.1 = (bf16[512,128]{1,0:T(8,128)(2,1)S(1)}, bf16[512,128]{1,0:T(8,128)(2,1)S(1)}, u32[]{:S(2)}, u32[]{:S(2)}) collective-permute-start(bf16[512,128]{1,0:T(8,128)(2,1)S(1)} %get-tuple-element.24.kv.refs_3_.own), channel_id=1, source_target_pairs={{0,24},{16,40},{32,56},{48,72},{64,88},{80,104},{96,120},{112,136}... | collective-permute-start | bytes 393224 | tf_op jit(solution)/shard_map/ppermute | solution.py:559
  22.2 0.0 copy-done.1
  22.2 2.6 %queries.1 = (bf16[752,128]{1,0:T(8,128)(2,1)S(1)}, bf16[128,512]{1,0:T(8,128)(2,1)S(1)}, bf16[8,64,128]{2,1,0:T(8,128)(2,1)}) custom-call(s32[2]{0:T(128)S(1)} %pad_add_fusion.refs_0_.ids, bf16[512,128]{1,0:T(8,128)(2,1)S(1)} %get-tuple-element.24.kv.refs_3_.own, bf16[752,128]{1,0:T(8,128)(2,1)S(1)} %get-tuple-element.23.pay_o, bf16[128,512]{1,0:T(8,128)(2,1)} %bitcast.13, ...), custom_call_target="tpu_custom_call" | custom-call | flops 1000 | bytes 1000 | tf_op jit(solution)/shard_map/queries/pallas_call | solution.py:151
  24.8 0.0 copy-start
  24.9 0.0 copy-start.2
  24.9 2.1 %collective-permute-start.2 = (bf16[752,128]{1,0:T(8,128)(2,1)S(1)}, bf16[752,128]{1,0:T(8,128)(2,1)S(1)}, u32[]{:S(2)}, u32[]{:S(2)}) collective-permute-start(bf16[752,128]{1,0:T(8,128)(2,1)S(1)} %get-tuple-element.25), channel_id=1, source_target_pairs={{0,8},{8,0},{16,24},{24,16},{32,40},{40,32},{48,56},{56,48},{64,72... | collective-permute-start | bytes 577544 | tf_op jit(solution)/shard_map/ppermute | solution.py:561
  26.9 4.2 %all-to-all-start = ((bf16[8,64,128]{2,1,0:T(8,128)(2,1)}), bf16[8,64,128]{2,1,0:T(8,128)(2,1)S(1)}, u32[]{:S(2)}, u32[]{:S(2)}) async-start(bf16[8,64,128]{2,1,0:T(8,128)(2,1)} %get-tuple-element.28), calls=%async_computation | async-start | bytes 262144 | tf_op jit(solution)/shard_map/all_to_all | solution.py:562
  31.2 0.0 collective-permute-done.1.far_on
  31.2 4.7 %collective-permute-done.got_o.refs_0_.refs_4_ = bf16[752,128]{1,0:T(8,128)(2,1)S(1)} collective-permute-done((bf16[752,128]{1,0:T(8,128)(2,1)S(1)}, bf16[752,128]{1,0:T(8,128)(2,1)S(1)}, u32[]{:S(2)}, u32[]{:S(2)}) %collective-permute-start) | collective-permute-done | bytes 192544 | tf_op jit(solution)/shard_map/ppermute | solution.py:558
  35.9 0.6 pass_on.1
  36.5 0.0 copy-start.4
  36.5 0.0 collective-permute-done.2.refs_1_.refs_5_.got_e
  36.5 1.9 %collective-permute-start.5 = (bf16[512,128]{1,0:T(8,128)(2,1)S(1)}, bf16[512,128]{1,0:T(8,128)(2,1)S(1)}, u32[]{:S(2)}, u32[]{:S(2)}) collective-permute-start(bf16[512,128]{1,0:T(8,128)(2,1)S(1)} %pass_on.1), channel_id=1, source_target_pairs={{0,8},{8,0},{16,24},{24,16},{32,40},{40,32},{48,56},{56,48},{64,72... | collective-permute-start | bytes 393224 | tf_op jit(solution)/shard_map/ppermute | solution.py:568
  38.4 0.0 copy-done
  38.4 0.0 copy-done.2
  38.4 0.6 stack_rows.1.refs_3_
  39.1 0.8 %all-to-all-done.refs_2_.q_t = bf16[8,64,128]{2,1,0:T(8,128)(2,1)S(1)} async-done(((bf16[8,64,128]{2,1,0:T(8,128)(2,1)}), bf16[8,64,128]{2,1,0:T(8,128)(2,1)S(1)}, u32[]{:S(2)}, u32[]{:S(2)}) %all-to-all-start) | async-done | bytes 131104 | tf_op jit(solution)/shard_map/all_to_all | solution.py:562
  39.9 2.5 %collective-permute-start.4 = (bf16[192,512]{1,0:T(8,128)(2,1)S(1)}, bf16[192,512]{1,0:T(8,128)(2,1)S(1)}, u32[]{:S(2)}, u32[]{:S(2)}) collective-permute-start(bf16[192,512]{1,0:T(8,128)(2,1)S(1)} %stack_rows.1.refs_3_), channel_id=1, source_target_pairs={{1,0},{2,1},{3,2},{4,3},{5,4},{6,5},{7,6},{9,8},{10,9},{11,10},{12... | collective-permute-start | bytes 589832 | tf_op jit(solution)/shard_map/ppermute | solution.py:569
  42.4 3.4 %collective-permute-start.3 = (bf16[192,512]{1,0:T(8,128)(2,1)S(1)}, bf16[192,512]{1,0:T(8,128)(2,1)S(1)}, u32[]{:S(2)}, u32[]{:S(2)}) collective-permute-start(bf16[192,512]{1,0:T(8,128)(2,1)S(1)} %stack_rows.1.refs_3_), channel_id=1, source_target_pairs={{0,1},{1,2},{2,3},{3,4},{4,5},{5,6},{6,7},{8,9},{9,10},{10,11},{11... | collective-permute-start | bytes 589832 | tf_op jit(solution)/shard_map/ppermute | solution.py:570
  45.8 0.0 copy-done.4
  45.8 3.5 %here_attention.1.after.here = bf16[8,80,128]{2,1,0:T(8,128)(2,1)S(1)} custom-call(s32[2]{0:T(128)S(1)} %pad_add_fusion.refs_0_.ids, s32[1,8]{1,0:T(1,128)S(1)} %copy-done.4, bf16[8,64,128]{2,1,0:T(8,128)(2,1)S(1)} %all-to-all-done.refs_2_.q_t, bf16[512,128]{1,0:T(8,128)(2,1)S(1)} %get-tuple-element.24.kv.refs_3_.own, ...), custom_call_target="tpu_custom_call" | custom-call | flops 1000 | bytes 1000 | tf_op jit(solution)/shard_map/here_attention/pallas_call | solution.py:383
  49.4 0.0 collective-permute-done.5.far
  49.4 0.8 %choose_blocks.1 = (bf16[1024,128]{1,0:T(8,128)(2,1)S(1)}, bf16[128,1024]{1,0:T(8,128)(2,1)S(1)}) custom-call(bf16[8,80,128]{2,1,0:T(8,128)(2,1)S(1)} %here_attention.1.after.here, s32[2]{0:T(128)S(1)} %pad_add_fusion.refs_0_.ids, s32[8]{0:T(128)S(1)} %fusion.1.table, bf16[512,128]{1,0:T(8,128)(2,1)S(1)} %collective-permute-done.5.far, ...), custom_call_target="tpu_custom_call" | custom-call | flops 10000000000 | bytes 1000 | tf_op jit(solution)/shard_map/choose_blocks/pallas_call | solution.py:417
  50.1 0.0 collective-permute-done.4.refs_4_.after_too
  50.2 0.0 collective-permute-done.3.refs_2_.after
  50.2 2.8 %before_attention.1 = bf16[8,80,128]{2,1,0:T(8,128)(2,1)} custom-call(bf16[192,512]{1,0:T(8,128)(2,1)S(1)} %collective-permute-done.3.refs_2_.after, bf16[192,512]{1,0:T(8,128)(2,1)S(1)} %collective-permute-done.4.refs_4_.after_too, s32[2]{0:T(128)S(1)} %copy-done.2, bf16[8,64,128]{2,1,0:T(8,128)(2,1)S(1)} %all-to-all-done.refs_2_.q_t, ...), custom_call_target="tpu_custom_call" | custom-call | flops 1000 | bytes 1000 | tf_op jit(solution)/shard_map/before_attention/pallas_call | solution.py:444
  53.0 4.3 %all-to-all-start.1 = ((bf16[8,80,128]{2,1,0:T(8,128)(2,1)}), bf16[8,80,128]{2,1,0:T(8,128)(2,1)S(1)}, u32[]{:S(2)}, u32[]{:S(2)}) async-start(bf16[8,80,128]{2,1,0:T(8,128)(2,1)} %before_attention.1), calls=%async_computation.1 | async-start | bytes 327680 | tf_op jit(solution)/shard_map/all_to_all | solution.py:577
  57.3 0.0 copy-start.3
  57.3 3.9 %window_attention.1 = (f32[128,512]{1,0:T(8,128)S(1)}, f32[128,128]{1,0:T(8,128)S(1)}, bf16[512,512]{1,0:T(8,128)(2,1)S(1)}, bf16[512,512]{1,0:T(8,128)(2,1)S(1)...) custom-call(s32[2]{0:T(128)S(1)} %pad_add_fusion.refs_0_.ids, s32[2]{0:T(128)S(1)} %copy-done.2, ...), custom_call_target="tpu_custom_call" | custom-call | flops 1000 | bytes 1000 | tf_op jit(solution)/shard_map/window_attention/pallas_call | solution.py:298
  61.2 2.1 %all-to-all-done.1.coarse = bf16[8,80,128]{2,1,0:T(8,128)(2,1)S(1)} async-done(((bf16[8,80,128]{2,1,0:T(8,128)(2,1)}), bf16[8,80,128]{2,1,0:T(8,128)(2,1)S(1)}, u32[]{:S(2)}, u32[]{:S(2)}) %all-to-all-start.1) | async-done | bytes 163872 | tf_op jit(solution)/shard_map/all_to_all | solution.py:577
  63.3 0.0 copy-done.3
  63.3 4.1 %finish.1 = bf16[128,512]{1,0:T(8,128)(2,1)} custom-call(bf16[128,512]{1,0:T(8,128)(2,1)S(1)} %bitcast.15, f32[128,512]{1,0:T(8,128)S(1)} %get-tuple-element.31.near, f32[128,128]{1,0:T(8,128)S(1)} %get-tuple-element.32.near_lse, bf16[8,80,128]{2,1,0:T(8,128)(2,1)S(1)} %all-to-all-done.1.coarse, f32[1,512]{1,0:T(1,128)S(1)} %bitcast.18, ...), custom_call_target="tpu_custom_call" | custom-call | flops 1000 | bytes 1000 | tf_op jit(solution)/shard_map/finish/pallas_call | solution.py:504
  (1 shorter events, 0.0 us)
Async XLA Ops:
  0.0 22.2 %copy-start.1 = (f32[512]{0:T(512)S(1)}, f32[512]{0:T(512)}, u32[]{:S(2)}) copy-start(f32[512]{0:T(512)} %param.19) | copy-start | bytes 6148
  2.9 32.9 %collective-permute-start = (bf16[752,128]{1,0:T(8,128)(2,1)S(1)}, bf16[752,128]{1,0:T(8,128)(2,1)S(1)}, u32[]{:S(2)}, u32[]{:S(2)}) collective-permute-start(bf16[752,128]{1,0:T(8,128)(2,1)S(1)} %get-tuple-element.23.pay_o), channel_id=1, source_target_pairs={{0,504},{8,16},{16,8},{24,32},{32,24},{40,48},{48,40},{56,64},{64,... | collective-permute-start | bytes 577544 | tf_op jit(solution)/shard_map/ppermute | solution.py:558
  20.9 10.3 %collective-permute-start.1 = (bf16[512,128]{1,0:T(8,128)(2,1)S(1)}, bf16[512,128]{1,0:T(8,128)(2,1)S(1)}, u32[]{:S(2)}, u32[]{:S(2)}) collective-permute-start(bf16[512,128]{1,0:T(8,128)(2,1)S(1)} %get-tuple-element.24.kv.refs_3_.own), channel_id=1, source_target_pairs={{0,24},{16,40},{32,56},{48,72},{64,88},{80,104},{96,120},{112,136}... | collective-permute-start | bytes 393224 | tf_op jit(solution)/shard_map/ppermute | solution.py:559
  24.8 13.6 %copy-start = (bf16[16,8,512]{2,1,0:T(8,128)(2,1)S(1)}, bf16[16,8,512]{2,1,0:T(8,128)(2,1)}, u32[]{:S(2)}) copy-start(bf16[16,8,512]{2,1,0:T(8,128)(2,1)} %param.15) | copy-start | bytes 393220
  24.9 13.6 %copy-start.2 = (s32[2]{0:T(128)S(1)}, s32[2]{0:T(128)}, u32[]{:S(2)}) copy-start(s32[2]{0:T(128)} %shifts.3) | copy-start | bytes 28
  24.9 11.6 %collective-permute-start.2 = (bf16[752,128]{1,0:T(8,128)(2,1)S(1)}, bf16[752,128]{1,0:T(8,128)(2,1)S(1)}, u32[]{:S(2)}, u32[]{:S(2)}) collective-permute-start(bf16[752,128]{1,0:T(8,128)(2,1)S(1)} %get-tuple-element.25), channel_id=1, source_target_pairs={{0,8},{8,0},{16,24},{24,16},{32,40},{40,32},{48,56},{56,48},{64,72... | collective-permute-start | bytes 577544 | tf_op jit(solution)/shard_map/ppermute | solution.py:561
  26.9 13.0 %all-to-all-start = ((bf16[8,64,128]{2,1,0:T(8,128)(2,1)}), bf16[8,64,128]{2,1,0:T(8,128)(2,1)S(1)}, u32[]{:S(2)}, u32[]{:S(2)}) async-start(bf16[8,64,128]{2,1,0:T(8,128)(2,1)} %get-tuple-element.28), calls=%async_computation | async-start | bytes 262144 | tf_op jit(solution)/shard_map/all_to_all | solution.py:562
  36.5 9.4 %copy-start.4 = (s32[1,8]{1,0:T(1,128)S(1)}, s32[1,8]{1,0:T(1,128)}, u32[]{:S(2)}) copy-start(s32[1,8]{1,0:T(1,128)} %refs_1_.5) | copy-start | bytes 100
  36.5 12.9 %collective-permute-start.5 = (bf16[512,128]{1,0:T(8,128)(2,1)S(1)}, bf16[512,128]{1,0:T(8,128)(2,1)S(1)}, u32[]{:S(2)}, u32[]{:S(2)}) collective-permute-start(bf16[512,128]{1,0:T(8,128)(2,1)S(1)} %pass_on.1), channel_id=1, source_target_pairs={{0,8},{8,0},{16,24},{24,16},{32,40},{40,32},{48,56},{56,48},{64,72... | collective-permute-start | bytes 393224 | tf_op jit(solution)/shard_map/ppermute | solution.py:568
  39.9 10.2 %collective-permute-start.4 = (bf16[192,512]{1,0:T(8,128)(2,1)S(1)}, bf16[192,512]{1,0:T(8,128)(2,1)S(1)}, u32[]{:S(2)}, u32[]{:S(2)}) collective-permute-start(bf16[192,512]{1,0:T(8,128)(2,1)S(1)} %stack_rows.1.refs_3_), channel_id=1, source_target_pairs={{1,0},{2,1},{3,2},{4,3},{5,4},{6,5},{7,6},{9,8},{10,9},{11,10},{12... | collective-permute-start | bytes 589832 | tf_op jit(solution)/shard_map/ppermute | solution.py:569
  42.4 7.7 %collective-permute-start.3 = (bf16[192,512]{1,0:T(8,128)(2,1)S(1)}, bf16[192,512]{1,0:T(8,128)(2,1)S(1)}, u32[]{:S(2)}, u32[]{:S(2)}) collective-permute-start(bf16[192,512]{1,0:T(8,128)(2,1)S(1)} %stack_rows.1.refs_3_), channel_id=1, source_target_pairs={{0,1},{1,2},{2,3},{3,4},{4,5},{5,6},{6,7},{8,9},{9,10},{10,11},{11... | collective-permute-start | bytes 589832 | tf_op jit(solution)/shard_map/ppermute | solution.py:570
  53.0 10.3 %all-to-all-start.1 = ((bf16[8,80,128]{2,1,0:T(8,128)(2,1)}), bf16[8,80,128]{2,1,0:T(8,128)(2,1)S(1)}, u32[]{:S(2)}, u32[]{:S(2)}) async-start(bf16[8,80,128]{2,1,0:T(8,128)(2,1)} %before_attention.1), calls=%async_computation.1 | async-start | bytes 327680 | tf_op jit(solution)/shard_map/all_to_all | solution.py:577
  57.3 6.0 %copy-start.3 = (f32[512]{0:T(512)S(1)}, f32[512]{0:T(512)}, u32[]{:S(2)}) copy-start(f32[512]{0:T(512)} %param.26) | copy-start | bytes 6148

commit v5 on v4

--- a/solution.py
+++ b/solution.py
@@ -9,6 +9,7 @@
 HD = 64
 WS = 8
 HALO = WS - 1
+PLANE = 16
 CHUNK = 512
 EPS = 1e-06
 F32 = jnp.float32
@@ -16,7 +17,6 @@
 LOW = -1e30
 VMEM_LIMIT = 24 * 1024 * 1024
 COST = pl.CostEstimate(flops=1000, bytes_accessed=1000, transcendentals=0)
-COST_ONWARD = pl.CostEstimate(flops=1000000000, bytes_accessed=1000, transcendentals=0)
 COST_STACK = pl.CostEstimate(flops=10000000000, bytes_accessed=1000, transcendentals=0)
 COST_HERE = pl.CostEstimate(flops=1000, bytes_accessed=1000, transcendentals=0)
 COST_CHOOSE = pl.CostEstimate(flops=10000000000, bytes_accessed=1000, transcendentals=0)
@@ -47,7 +47,7 @@
     return jnp.concatenate(parts, axis=0).astype(BF16)
 
 
-def project_kernel(total, ids, table_in, coarse, w_k, w_v, fine, kv, pay_o, table, c_buf, w_buf, x_buf, sems):
+def project_kernel(total, ids, table_in, coarse, w_k, w_v, fine, kv, pay_o, pay_e, table, c_buf, w_buf, x_buf, sems):
     chunks = c_buf.shape[0]
     rows = c_buf.shape[1]
     cols = pl.ds(pl.multiple_of(ids[1] // 2 * 128, 128), 128)
@@ -82,6 +82,7 @@
         at = slice(rows * i, rows * i + rows)
         kv[at, :] = both
         pay_o[at, :] = both
+        pay_e[at, :] = both
     loads[3].wait()
     chosen = local_blocks(ids, table, base // 128, total)
     lane = iota((16, 128), 1)
@@ -90,8 +91,10 @@
         marks = jnp.where(lane == i, b.astype(F32), marks)
     end = base + HALO * WS * (width // 128)
     pay_o[end : end + 16, :] = marks.astype(BF16)
+    pay_e[end : end + 16, :] = marks.astype(BF16)
     loads[2].wait()
     pay_o[base:end, :] = edge_rows(x_buf, even)
+    pay_e[base:end, :] = edge_rows(x_buf, jnp.logical_not(even))
 
 
 def project(ids, table, coarse, w_k, w_v, fine, total):
@@ -105,9 +108,10 @@
     return pl.pallas_call(
         lambda *refs: project_kernel(total, *refs),
         in_specs=[smem] + [hbm] * 5,
-        out_specs=[vmem] * 2,
+        out_specs=[vmem] * 3,
         out_shape=[
             jax.ShapeDtypeStruct((n_coarse, 128), BF16),
+            jax.ShapeDtypeStruct((pay_rows, 128), BF16),
             jax.ShapeDtypeStruct((pay_rows, 128), BF16),
         ],
         scratch_shapes=[
@@ -123,20 +127,12 @@
     )(ids, table, coarse, w_k, w_v, fine)
 
 
-def query_kernel(ids, kv, pay_o, fine, gain, w_q, pay_e, q_nat, q_t, x_buf, q_buf, sems):
+def query_kernel(after, fine, gain, w_q, q_nat, q_t, x_buf, q_buf, sems):
     first = pltpu.make_async_copy(fine, x_buf, sems.at[0])
     second = pltpu.make_async_copy(w_q, q_buf, sems.at[1])
     first.start()
     second.start()
-    base = kv.shape[0]
-    n_tok, width = x_buf.shape
-    halo = HALO * WS
-    end = base + halo * (width // 128)
-    pay_e[0:base, :] = kv[...]
-    pay_e[end:, :] = pay_o[end:, :]
-    even = lax.rem(ids[0], 2) == 0
     first.wait()
-    pay_e[base:end, :] = edge_rows(x_buf, jnp.logical_not(even))
     normed = rms(x_buf[...].astype(F32), gain[...]).astype(BF16)
     second.wait()
     q = jnp.dot(normed, q_buf[...], preferred_element_type=F32) * (1.0 / HD**0.5)
@@ -144,16 +140,15 @@
     q_t[...] = q.T.astype(BF16).reshape(q_t.shape)
 
 
-def queries(ids, kv, pay_o, fine, gain, w_q):
+def queries(after, fine, gain, w_q):
     n_tok, width = fine.shape
     hbm = pl.BlockSpec(memory_space=pltpu.HBM)
     vmem = pl.BlockSpec(memory_space=pltpu.VMEM)
     return pl.pallas_call(
         query_kernel,
-        in_specs=[pl.BlockSpec(memory_space=pltpu.SMEM), vmem, vmem, hbm, vmem, hbm],
-        out_specs=[vmem] * 3,
+        in_specs=[pl.BlockSpec(memory_space=pl.ANY), hbm, vmem, hbm],
+        out_specs=[vmem] * 2,
         out_shape=[
-            jax.ShapeDtypeStruct(pay_o.shape, BF16),
             jax.ShapeDtypeStruct((n_tok, width), BF16),
             jax.ShapeDtypeStruct((HEADS, HD, n_tok), BF16),
         ],
@@ -165,24 +160,7 @@
         compiler_params=pltpu.CompilerParams(vmem_limit_bytes=VMEM_LIMIT),
         cost_estimate=COST,
         name="queries",
-    )(ids, kv, pay_o, fine, gain, w_q)
-
-
-def onward_kernel(ids, got_o, far_on, out):
-    out[...] = jnp.where(lax.rem(ids[0], 2) == 0, got_o[0 : out.shape[0], :], far_on[...])
-
-
-def pass_on(ids, got_o, far_on):
-    vmem = pl.BlockSpec(memory_space=pltpu.VMEM)
-    return pl.pallas_call(
-        onward_kernel,
-        in_specs=[pl.BlockSpec(memory_space=pltpu.SMEM), vmem, vmem],
-        out_specs=vmem,
-        out_shape=jax.ShapeDtypeStruct(far_on.shape, BF16),
-        compiler_params=pltpu.CompilerParams(vmem_limit_bytes=VMEM_LIMIT),
-        cost_estimate=COST_ONWARD,
-        name="pass_on",
-    )(ids, got_o, far_on)
+    )(after, fine, gain, w_q)
 
 
 def stack_kernel(ids, shifts, base, got_o, got_e, fine, out, rows):
@@ -395,12 +373,13 @@
     )(ids, table, q_t, own, got_o, got_e)
 
 
-def choose_kernel(after, ids, table, far, got_o, got_e, own, kv, kv_t, store):
+def choose_kernel(after, ids, table, far_straight, far_handed, got_o, got_e, own, kv, kv_t, store):
     n_own = own.shape[0]
     per_strip = n_own // 128
     even = lax.rem(ids[0], 2) == 0
     blocked = lambda ref: ref[0:n_own, :].reshape(per_strip, 128, 128)
-    store[0:per_strip] = blocked(far)
+    handed = lax.rem(ids[0], PLANE) == 1
+    store[0:per_strip] = jnp.where(handed, blocked(far_handed), blocked(far_straight))
     store[per_strip : 2 * per_strip] = jnp.where(even, blocked(got_o), blocked(got_e))
     store[2 * per_strip :] = blocked(own)
     for i in range(table.shape[0]):
@@ -410,20 +389,20 @@
         kv_t[:, at] = block.astype(F32).T.astype(BF16)
 
 
-def choose_blocks(after, ids, table, far, got_o, got_e, own):
+def choose_blocks(after, ids, table, far_straight, far_handed, got_o, got_e, own):
     vmem = pl.BlockSpec(memory_space=pltpu.VMEM)
     smem = pl.BlockSpec(memory_space=pltpu.SMEM)
     keys = 128 * table.shape[0]
     return pl.pallas_call(
         choose_kernel,
-        in_specs=[pl.BlockSpec(memory_space=pl.ANY), smem, smem] + [vmem] * 4,
+        in_specs=[pl.BlockSpec(memory_space=pl.ANY), smem, smem] + [vmem] * 5,
         out_specs=[vmem] * 2,
         out_shape=[jax.ShapeDtypeStruct((keys, 128), BF16), jax.ShapeDtypeStruct((128, keys), BF16)],
         scratch_shapes=[pltpu.VMEM((3 * own.shape[0] // 128, 128, 128), BF16)],
         compiler_params=pltpu.CompilerParams(vmem_limit_bytes=VMEM_LIMIT),
         cost_estimate=COST_CHOOSE,
         name="choose_blocks",
-    )(after, ids, table, far, got_o, got_e, own)
+    )(after, ids, table, far_straight, far_handed, got_o, got_e, own)
 
 
 def before_kernel(after, after_too, shifts, q_t, kv, kv_t, here, out):
@@ -550,29 +529,29 @@
 
     stay = lambda x: pltpu.with_memory_space_constraint(x, pltpu.HBM)
     flat_hbm = stay(flat)
-    kv, pay_o = project(
+    kv, pay_o, pay_e = project(
         ids, stay(table), stay(coarse.reshape(n_own, cw)), stay(coarse_key), stay(coarse_value), flat_hbm, total
     )
     odd_pairs = [(i, (i - 1) % strips if i % 2 == 0 else (i + 1) % strips) for i in range(strips)]
     even_pairs = [(i, i ^ 1) for i in range(strips)]
     got_o = lax.ppermute(pay_o, "tile", odd_pairs)
-    far_on = lax.ppermute(kv, "tile", [(i, (i + 3) % strips) for i in range(0, strips, 2)])
-    pay_e, q, q_t = queries(ids, kv, pay_o, flat_hbm, gain, stay(w_query))
     got_e = lax.ppermute(pay_e, "tile", even_pairs)
+    far_straight = lax.ppermute(
+        kv, "tile", [(i, (i + 2) % strips) for i in range(strips) if i % PLANE != PLANE - 1]
+    )
+    q, q_t = queries(kv, flat_hbm, gain, stay(w_query))
     q_head = lax.all_to_all(q_t, "narrow", 0, 0, tiled=True)
 
-    onward = pass_on(ids, got_o, far_on)
-    onward, got_o, got_e = lax.optimization_barrier((onward, got_o, got_e))
+    far_handed = lax.ppermute(got_o, "tile", [(i, i + 1) for i in range(0, strips, PLANE)])
+    mark_row = n_own + HALO * WS * (width // 128)
+    table_before = jnp.where(strip % 2 == 0, got_o[mark_row, :8], got_e[mark_row, :8]).astype(jnp.int32)
+
     stacked = stack_rows(ids, shifts, got_o, got_e, flat, n_own)
-    stacked, q_head = lax.optimization_barrier((stacked, q_head))
-    far = lax.ppermute(onward, "tile", even_pairs)
+    stacked, table_before = lax.optimization_barrier((stacked, table_before))
     right_of = lax.ppermute(stacked, "narrow", [(i, i - 1) for i in range(1, members)])
     left_of = lax.ppermute(stacked, "narrow", [(i, i + 1) for i in range(members - 1)])
-    mark_row = n_own + HALO * WS * (width // 128)
-    table_before = jnp.where(strip % 2 == 0, got_o[mark_row, :8], got_e[mark_row, :8]).astype(jnp.int32)
-
     here = here_attention(ids, table, q_head, kv, got_o, got_e, total)
-    kv_before, kv_before_t = choose_blocks(here, ids, table_before, far, got_o, got_e, kv)
+    kv_before, kv_before_t = choose_blocks(here, ids, table_before, far_straight, far_handed, got_o, got_e, kv)
     from_coarse = before_attention(left_of, right_of, shifts, q_head, kv_before, kv_before_t, here)
     from_coarse = lax.all_to_all(from_coarse, "narrow", 0, 0, tiled=True)
     near, near_lse, *held = window_attention(

time: 68.2 us -> 66.5 us (0.975)
  Pallas kernels: 21.8 us -> 20.7 us
    pallas_call x2 -> x1, Pallas kernels: 3.21 us -> 2.1 us  [queries(): pl.pallas_call(query_kernel, in_specs=[pl.BlockSpec(memory_space=pl.ANY),...]
    all_to_all x1, waiting for transfers between devices: 0.83 us -> 0.01 us  [local(): q_head = lax.all_to_all(q_t, 'narrow', 0, 0, tiled=True)]
    ppermute x1, starting transfers between devices: 2.52 us -> 3.27 us  [local(): lax.ppermute(stacked, 'narrow', [(i, i - 1) for i in range(1, members)])]
  transfers between devices with their start and end apart: 8 -> 8, of which waited for: 3 -> 2; matrix products, arithmetic and copies ran while one was open for 0% -> 0% of each run, Pallas kernels for 18% -> 16%
where the time goes in v5:
time: 66.5 us; the launch traced here: 66 us
  starting transfers between devices  38 us (57%)
  Pallas kernels  20.7 us (31%)
  waiting for transfers between devices  7.01 us (11%)
    ppermute x1, starting transfers between devices, local(): got_o = lax.ppermute(pay_o, 'tile', odd_pairs)  17.9 us
    ppermute x1, waiting for transfers between devices, local(): got_o = lax.ppermute(pay_o, 'tile', odd_pairs)  4.89 us
    all_to_all x1, starting transfers between devices, local(): q_head = lax.all_to_all(q_t, 'narrow', 0, 0, tiled=True)  4.24 us
    all_to_all x1, starting transfers between devices, local(): from_coarse = lax.all_to_all(from_coarse, 'narrow', 0, 0, tiled=True)  4.15 us
    pallas_call x1, Pallas kernels, finish(): pl.pallas_call(finish_kernel, in_specs=[vmem] * 9 + [hbm] * 3, out_specs=...  4.14 us
    pallas_call x1, Pallas kernels, window_attention(): pl.pallas_call(lambda *refs: window_kernel(last, count, *refs), in_specs=...  3.87 us
    pallas_call x1, Pallas kernels, here_attention(): pl.pallas_call(lambda *refs: here_kernel(total, *refs), in_specs=[smem, s...  3.53 us
    ppermute x1, starting transfers between devices, local(): lax.ppermute(stacked, 'narrow', [(i, i + 1) for i in range(members - 1)])  3.28 us
  transfers between devices with their start and end apart: 8, of which 2 were waited for; matrix products, arithmetic and copies ran while one was open for 0% of the time, Pallas kernels for 16%

profile of v5, /device:TPU:1, one launch (start us, length us, event | category | flops | bytes accessed | tf_op | source)
XLA Modules:
  0.0 66.0 jit_solution(5844496865121011567)
XLA Ops:
  0.0 0.0 copy-start.1
  0.0 0.1 pad_add_fusion.refs_0_.ids
  0.1 0.0 copy-start
  0.1 0.0 copy-start.2
  0.1 2.9 %project.1 = (bf16[512,128]{1,0:T(8,128)(2,1)S(1)}, bf16[752,128]{1,0:T(8,128)(2,1)S(1)}, bf16[752,128]{1,0:T(8,128)(2,1)S(1)}) custom-call(s32[2]{0:T(128)S(1)} %pad_add_fusion.refs_0_.ids, s32[1,8]{1,0:T(1,128)} %refs_1_.5, bf16[512,1024]{1,0:T(8,128)(2,1)} %bitcast.19, bf16[1024,512]{1,0:T(8,128)(2,1)} %refs_3_.1, bf16[1024,512]{1,0:T(8,128)(2,1)} %refs_4_.1, ...), custom_call_target="tpu_custom_call" | custom-call | flops 1000 | bytes 1000 | tf_op jit(solution)/shard_map/project/pallas_call | solution.py:108
  3.0 17.9 %collective-permute-start = (bf16[752,128]{1,0:T(8,128)(2,1)S(1)}, bf16[752,128]{1,0:T(8,128)(2,1)S(1)}, u32[]{:S(2)}, u32[]{:S(2)}) collective-permute-start(bf16[752,128]{1,0:T(8,128)(2,1)S(1)} %get-tuple-element.20), channel_id=1, source_target_pairs={{0,504},{8,16},{16,8},{24,32},{32,24},{40,48},{48,40},{56,64},{64,... | collective-permute-start | bytes 577544 | tf_op jit(solution)/shard_map/ppermute | solution.py:537
  20.9 1.9 %collective-permute-start.1 = (bf16[752,128]{1,0:T(8,128)(2,1)S(1)}, bf16[752,128]{1,0:T(8,128)(2,1)S(1)}, u32[]{:S(2)}, u32[]{:S(2)}) collective-permute-start(bf16[752,128]{1,0:T(8,128)(2,1)S(1)} %get-tuple-element.21), channel_id=1, source_target_pairs={{0,8},{8,0},{16,24},{24,16},{32,40},{40,32},{48,56},{56,48},{64,72... | collective-permute-start | bytes 577544 | tf_op jit(solution)/shard_map/ppermute | solution.py:538
  22.8 1.9 %collective-permute-start.4 = (bf16[512,128]{1,0:T(8,128)(2,1)S(1)}, bf16[512,128]{1,0:T(8,128)(2,1)S(1)}, u32[]{:S(2)}, u32[]{:S(2)}) collective-permute-start(bf16[512,128]{1,0:T(8,128)(2,1)S(1)} %get-tuple-element.23.after.refs_3_.own), channel_id=1, source_target_pairs={{0,16},{8,24},{16,32},{24,40},{32,48},{40,56},{48,64},{56,72},{64,... | collective-permute-start | bytes 393224 | tf_op jit(solution)/shard_map/ppermute | solution.py:539
  24.8 0.0 copy-done.1
  24.8 2.1 %queries.1 = (bf16[128,512]{1,0:T(8,128)(2,1)S(1)}, bf16[8,64,128]{2,1,0:T(8,128)(2,1)}) custom-call(bf16[512,128]{1,0:T(8,128)(2,1)S(1)} %get-tuple-element.23.after.refs_3_.own, bf16[128,512]{1,0:T(8,128)(2,1)} %bitcast.13, f32[1,512]{1,0:T(1,128)S(1)} %bitcast.16, bf16[512,512]{1,0:T(8,128)(2,1)} %w_q.1), custom_call_target="tpu_custom_call" | custom-call | flops 1000 | bytes 1000 | tf_op jit(solution)/shard_map/queries/pallas_call | solution.py:147
  26.9 4.2 %all-to-all-start = ((bf16[8,64,128]{2,1,0:T(8,128)(2,1)}), bf16[8,64,128]{2,1,0:T(8,128)(2,1)S(1)}, u32[]{:S(2)}, u32[]{:S(2)}) async-start(bf16[8,64,128]{2,1,0:T(8,128)(2,1)} %get-tuple-element.27), calls=%async_computation | async-start | bytes 262144 | tf_op jit(solution)/shard_map/all_to_all | solution.py:543
  31.1 0.0 copy-start.4
  31.1 4.9 %collective-permute-done.refs_0_.refs_4_.got_o = bf16[752,128]{1,0:T(8,128)(2,1)S(1)} collective-permute-done((bf16[752,128]{1,0:T(8,128)(2,1)S(1)}, bf16[752,128]{1,0:T(8,128)(2,1)S(1)}, u32[]{:S(2)}, u32[]{:S(2)}) %collective-permute-start) | collective-permute-done | bytes 192544 | tf_op jit(solution)/shard_map/ppermute | solution.py:537
  36.0 1.3 %collective-permute-start.5 = (bf16[752,128]{1,0:T(8,128)(2,1)S(1)}, bf16[752,128]{1,0:T(8,128)(2,1)S(1)}, u32[]{:S(2)}, u32[]{:S(2)}) collective-permute-start(bf16[752,128]{1,0:T(8,128)(2,1)S(1)} %collective-permute-done.refs_0_.refs_4_.got_o), channel_id=1, source_target_pairs={{0,8},{128,136},{256,264},{384,392},{1,9},{129,137},{257,265},{385... | collective-permute-start | bytes 577544 | tf_op jit(solution)/shard_map/ppermute | solution.py:545
  37.3 0.0 collective-permute-done.1.refs_1_.refs_5_.got_e
  37.3 0.0 copy-done
  37.3 0.0 copy-done.2
  37.3 0.6 stack_rows.1.refs_3_
  37.9 3.3 %collective-permute-start.3 = (bf16[192,512]{1,0:T(8,128)(2,1)S(1)}, bf16[192,512]{1,0:T(8,128)(2,1)S(1)}, u32[]{:S(2)}, u32[]{:S(2)}) collective-permute-start(bf16[192,512]{1,0:T(8,128)(2,1)S(1)} %stack_rows.1.refs_3_), channel_id=1, source_target_pairs={{1,0},{2,1},{3,2},{4,3},{5,4},{6,5},{7,6},{9,8},{10,9},{11,10},{12... | collective-permute-start | bytes 589832 | tf_op jit(solution)/shard_map/ppermute | solution.py:551
  41.2 3.3 %collective-permute-start.2 = (bf16[192,512]{1,0:T(8,128)(2,1)S(1)}, bf16[192,512]{1,0:T(8,128)(2,1)S(1)}, u32[]{:S(2)}, u32[]{:S(2)}) collective-permute-start(bf16[192,512]{1,0:T(8,128)(2,1)S(1)} %stack_rows.1.refs_3_), channel_id=1, source_target_pairs={{0,1},{1,2},{2,3},{3,4},{4,5},{5,6},{6,7},{8,9},{9,10},{10,11},{11... | collective-permute-start | bytes 589832 | tf_op jit(solution)/shard_map/ppermute | solution.py:552
  44.5 0.0 all-to-all-done.refs_2_.q_t
  44.5 0.0 copy-done.4
  44.5 3.5 %here_attention.1.after.here = bf16[8,80,128]{2,1,0:T(8,128)(2,1)S(1)} custom-call(s32[2]{0:T(128)S(1)} %pad_add_fusion.refs_0_.ids, s32[1,8]{1,0:T(1,128)S(1)} %copy-done.4, bf16[8,64,128]{2,1,0:T(8,128)(2,1)S(1)} %all-to-all-done.refs_2_.q_t, bf16[512,128]{1,0:T(8,128)(2,1)S(1)} %get-tuple-element.23.after.refs_3_.own, ...), custom_call_target="tpu_custom_call" | custom-call | flops 1000 | bytes 1000 | tf_op jit(solution)/shard_map/here_attention/pallas_call | solution.py:361
  48.1 0.0 collective-permute-done.4.far_straight
  48.1 0.0 collective-permute-done.5.far_handed
  48.1 0.8 %choose_blocks.1 = (bf16[1024,128]{1,0:T(8,128)(2,1)S(1)}, bf16[128,1024]{1,0:T(8,128)(2,1)S(1)}) custom-call(bf16[8,80,128]{2,1,0:T(8,128)(2,1)S(1)} %here_attention.1.after.here, s32[2]{0:T(128)S(1)} %pad_add_fusion.refs_0_.ids, s32[8]{0:T(128)S(1)} %fusion.1.table, bf16[512,128]{1,0:T(8,128)(2,1)S(1)} %collective-permute-done.4.far_straight, ...), custom_call_target="tpu_custom_call" | custom-call | flops 10000000000 | bytes 1000 | tf_op jit(solution)/shard_map/choose_blocks/pallas_call | solution.py:396
  48.9 0.0 collective-permute-done.3.refs_4_.after_too
  48.9 0.0 collective-permute-done.2.refs_2_.after
  48.9 2.8 %before_attention.1 = bf16[8,80,128]{2,1,0:T(8,128)(2,1)} custom-call(bf16[192,512]{1,0:T(8,128)(2,1)S(1)} %collective-permute-done.2.refs_2_.after, bf16[192,512]{1,0:T(8,128)(2,1)S(1)} %collective-permute-done.3.refs_4_.after_too, s32[2]{0:T(128)S(1)} %copy-done.2, bf16[8,64,128]{2,1,0:T(8,128)(2,1)S(1)} %all-to-all-done.refs_2_.q_t, ...), custom_call_target="tpu_custom_call" | custom-call | flops 1000 | bytes 1000 | tf_op jit(solution)/shard_map/before_attention/pallas_call | solution.py:423
  51.7 4.1 %all-to-all-start.1 = ((bf16[8,80,128]{2,1,0:T(8,128)(2,1)}), bf16[8,80,128]{2,1,0:T(8,128)(2,1)S(1)}, u32[]{:S(2)}, u32[]{:S(2)}) async-start(bf16[8,80,128]{2,1,0:T(8,128)(2,1)} %before_attention.1), calls=%async_computation.1 | async-start | bytes 327680 | tf_op jit(solution)/shard_map/all_to_all | solution.py:556
  55.9 0.0 copy-start.3
  55.9 3.9 %window_attention.1 = (f32[128,512]{1,0:T(8,128)S(1)}, f32[128,128]{1,0:T(8,128)S(1)}, bf16[512,512]{1,0:T(8,128)(2,1)S(1)}, bf16[512,512]{1,0:T(8,128)(2,1)S(1)...) custom-call(s32[2]{0:T(128)S(1)} %pad_add_fusion.refs_0_.ids, s32[2]{0:T(128)S(1)} %copy-done.2, ...), custom_call_target="tpu_custom_call" | custom-call | flops 1000 | bytes 1000 | tf_op jit(solution)/shard_map/window_attention/pallas_call | solution.py:276
  59.8 2.1 %all-to-all-done.1.coarse = bf16[8,80,128]{2,1,0:T(8,128)(2,1)S(1)} async-done(((bf16[8,80,128]{2,1,0:T(8,128)(2,1)}), bf16[8,80,128]{2,1,0:T(8,128)(2,1)S(1)}, u32[]{:S(2)}, u32[]{:S(2)}) %all-to-all-start.1) | async-done | bytes 163872 | tf_op jit(solution)/shard_map/all_to_all | solution.py:556
  61.9 0.0 copy-done.3
  61.9 4.1 %finish.1 = bf16[128,512]{1,0:T(8,128)(2,1)} custom-call(bf16[128,512]{1,0:T(8,128)(2,1)S(1)} %bitcast.15, f32[128,512]{1,0:T(8,128)S(1)} %get-tuple-element.25.near, f32[128,128]{1,0:T(8,128)S(1)} %get-tuple-element.26.near_lse, bf16[8,80,128]{2,1,0:T(8,128)(2,1)S(1)} %all-to-all-done.1.coarse, f32[1,512]{1,0:T(1,128)S(1)} %bitcast.18, ...), custom_call_target="tpu_custom_call" | custom-call | flops 1000 | bytes 1000 | tf_op jit(solution)/shard_map/finish/pallas_call | solution.py:483
  (1 shorter events, 0.0 us)
Async XLA Ops:
  0.0 24.8 %copy-start.1 = (f32[512]{0:T(512)S(1)}, f32[512]{0:T(512)}, u32[]{:S(2)}) copy-start(f32[512]{0:T(512)} %param.19) | copy-start | bytes 6148
  0.1 37.2 %copy-start = (bf16[16,8,512]{2,1,0:T(8,128)(2,1)S(1)}, bf16[16,8,512]{2,1,0:T(8,128)(2,1)}, u32[]{:S(2)}) copy-start(bf16[16,8,512]{2,1,0:T(8,128)(2,1)} %param.15) | copy-start | bytes 393220
  0.1 37.2 %copy-start.2 = (s32[2]{0:T(128)S(1)}, s32[2]{0:T(128)}, u32[]{:S(2)}) copy-start(s32[2]{0:T(128)} %shifts.3) | copy-start | bytes 28
  3.0 33.0 %collective-permute-start = (bf16[752,128]{1,0:T(8,128)(2,1)S(1)}, bf16[752,128]{1,0:T(8,128)(2,1)S(1)}, u32[]{:S(2)}, u32[]{:S(2)}) collective-permute-start(bf16[752,128]{1,0:T(8,128)(2,1)S(1)} %get-tuple-element.20), channel_id=1, source_target_pairs={{0,504},{8,16},{16,8},{24,32},{32,24},{40,48},{48,40},{56,64},{64,... | collective-permute-start | bytes 577544 | tf_op jit(solution)/shard_map/ppermute | solution.py:537
  20.9 16.4 %collective-permute-start.1 = (bf16[752,128]{1,0:T(8,128)(2,1)S(1)}, bf16[752,128]{1,0:T(8,128)(2,1)S(1)}, u32[]{:S(2)}, u32[]{:S(2)}) collective-permute-start(bf16[752,128]{1,0:T(8,128)(2,1)S(1)} %get-tuple-element.21), channel_id=1, source_target_pairs={{0,8},{8,0},{16,24},{24,16},{32,40},{40,32},{48,56},{56,48},{64,72... | collective-permute-start | bytes 577544 | tf_op jit(solution)/shard_map/ppermute | solution.py:538
  22.8 25.2 %collective-permute-start.4 = (bf16[512,128]{1,0:T(8,128)(2,1)S(1)}, bf16[512,128]{1,0:T(8,128)(2,1)S(1)}, u32[]{:S(2)}, u32[]{:S(2)}) collective-permute-start(bf16[512,128]{1,0:T(8,128)(2,1)S(1)} %get-tuple-element.23.after.refs_3_.own), channel_id=1, source_target_pairs={{0,16},{8,24},{16,32},{24,40},{32,48},{40,56},{48,64},{56,72},{64,... | collective-permute-start | bytes 393224 | tf_op jit(solution)/shard_map/ppermute | solution.py:539
  26.9 17.6 %all-to-all-start = ((bf16[8,64,128]{2,1,0:T(8,128)(2,1)}), bf16[8,64,128]{2,1,0:T(8,128)(2,1)S(1)}, u32[]{:S(2)}, u32[]{:S(2)}) async-start(bf16[8,64,128]{2,1,0:T(8,128)(2,1)} %get-tuple-element.27), calls=%async_computation | async-start | bytes 262144 | tf_op jit(solution)/shard_map/all_to_all | solution.py:543
  31.1 13.4 %copy-start.4 = (s32[1,8]{1,0:T(1,128)S(1)}, s32[1,8]{1,0:T(1,128)}, u32[]{:S(2)}) copy-start(s32[1,8]{1,0:T(1,128)} %refs_1_.5) | copy-start | bytes 100
  36.0 12.1 %collective-permute-start.5 = (bf16[752,128]{1,0:T(8,128)(2,1)S(1)}, bf16[752,128]{1,0:T(8,128)(2,1)S(1)}, u32[]{:S(2)}, u32[]{:S(2)}) collective-permute-start(bf16[752,128]{1,0:T(8,128)(2,1)S(1)} %collective-permute-done.refs_0_.refs_4_.got_o), channel_id=1, source_target_pairs={{0,8},{128,136},{256,264},{384,392},{1,9},{129,137},{257,265},{385... | collective-permute-start | bytes 577544 | tf_op jit(solution)/shard_map/ppermute | solution.py:545
  37.9 10.9 %collective-permute-start.3 = (bf16[192,512]{1,0:T(8,128)(2,1)S(1)}, bf16[192,512]{1,0:T(8,128)(2,1)S(1)}, u32[]{:S(2)}, u32[]{:S(2)}) collective-permute-start(bf16[192,512]{1,0:T(8,128)(2,1)S(1)} %stack_rows.1.refs_3_), channel_id=1, source_target_pairs={{1,0},{2,1},{3,2},{4,3},{5,4},{6,5},{7,6},{9,8},{10,9},{11,10},{12... | collective-permute-start | bytes 589832 | tf_op jit(solution)/shard_map/ppermute | solution.py:551
  41.2 7.7 %collective-permute-start.2 = (bf16[192,512]{1,0:T(8,128)(2,1)S(1)}, bf16[192,512]{1,0:T(8,128)(2,1)S(1)}, u32[]{:S(2)}, u32[]{:S(2)}) collective-permute-start(bf16[192,512]{1,0:T(8,128)(2,1)S(1)} %stack_rows.1.refs_3_), channel_id=1, source_target_pairs={{0,1},{1,2},{2,3},{3,4},{4,5},{5,6},{6,7},{8,9},{9,10},{10,11},{11... | collective-permute-start | bytes 589832 | tf_op jit(solution)/shard_map/ppermute | solution.py:552
  51.7 10.1 %all-to-all-start.1 = ((bf16[8,80,128]{2,1,0:T(8,128)(2,1)}), bf16[8,80,128]{2,1,0:T(8,128)(2,1)S(1)}, u32[]{:S(2)}, u32[]{:S(2)}) async-start(bf16[8,80,128]{2,1,0:T(8,128)(2,1)} %before_attention.1), calls=%async_computation.1 | async-start | bytes 327680 | tf_op jit(solution)/shard_map/all_to_all | solution.py:556
  55.9 6.0 %copy-start.3 = (f32[512]{0:T(512)S(1)}, f32[512]{0:T(512)}, u32[]{:S(2)}) copy-start(f32[512]{0:T(512)} %param.26) | copy-start | bytes 6148

commit v6 on v5

--- a/solution.py
+++ b/solution.py
@@ -100,7 +100,7 @@
 def project(ids, table, coarse, w_k, w_v, fine, total):
     n_coarse, cw = coarse.shape
     n_tok, width = fine.shape
-    chunks = 2
+    chunks = 1
     pay_rows = n_coarse + HALO * WS * (width // 128) + 16
     smem = pl.BlockSpec(memory_space=pltpu.SMEM)
     hbm = pl.BlockSpec(memory_space=pltpu.HBM)
@@ -315,8 +315,8 @@
 def top_rows(q_t, group):
     low = iota((1, 128), 1) < 64
     tiles = []
-    for pair in range(2):
-        a, b = (q_t[4 * group + 2 * pair + k].astype(F32) for k in range(2))
+    for pair in range(4):
+        a, b = (q_t[8 * group + 2 * pair + k].astype(F32) for k in range(2))
         tiles.append(jnp.where(low, a, swap_halves(b)).astype(BF16))
     return jnp.concatenate(tiles, axis=1)
 
@@ -324,8 +324,8 @@
 def bottom_rows(q_t, group):
     low = iota((1, 128), 1) < 64
     tiles = []
-    for pair in range(2):
-        a, b = (q_t[4 * group + 2 * pair + k].astype(F32) for k in range(2))
+    for pair in range(4):
+        a, b = (q_t[8 * group + 2 * pair + k].astype(F32) for k in range(2))
         tiles.append(jnp.where(low, swap_halves(a), b).astype(BF16))
     return jnp.concatenate(tiles, axis=1)
 
@@ -344,14 +344,14 @@
     turned[...] = kv.astype(F32).T.astype(BF16)
     kv_t = turned[...]
     low = iota((1, 128), 1) < 64
-    for group in range(q_t.shape[0] // 4):
+    for group in range(q_t.shape[0] // 8):
         top = attend(top_rows(q_t, group), kv, kv_t)
         bottom = attend(bottom_rows(q_t, group), kv, kv_t)
-        for pair in range(2):
+        for pair in range(4):
             lanes = slice(128 * pair, 128 * pair + 128)
             t, u = top[:, lanes], bottom[:, lanes]
-            out[4 * group + 2 * pair] = jnp.where(low, t, swap_halves(u)).astype(BF16)
-            out[4 * group + 2 * pair + 1] = jnp.where(low, swap_halves(t), u).astype(BF16)
+            out[8 * group + 2 * pair] = jnp.where(low, t, swap_halves(u)).astype(BF16)
+            out[8 * group + 2 * pair + 1] = jnp.where(low, swap_halves(t), u).astype(BF16)
 
 
 def here_attention(ids, table, q_t, own, got_o, got_e, total):
@@ -408,12 +408,12 @@
 def before_kernel(after, after_too, shifts, q_t, kv, kv_t, here, out):
     lane = iota((1, 128), 1)
     earlier = lane < WS * shifts[0]
-    for group in range(q_t.shape[0] // 4):
+    for group in range(q_t.shape[0] // 8):
         top = attend(top_rows(q_t, group), kv[...], kv_t[...])
-        for pair in range(2):
+        for pair in range(4):
             t = top[:, 128 * pair : 128 * pair + 128]
             for k in range(2):
-                m = 4 * group + 2 * pair + k
+                m = 8 * group + 2 * pair + k
                 mine = t if k == 0 else swap_halves(t)
                 out[m] = jnp.where(earlier, mine, here[m].astype(F32)).astype(BF16)
 

time: 66.5 us -> 65.7 us (0.988)
  Pallas kernels: 20.7 us -> 19.1 us
  starting transfers between devices: 38 us -> 38.8 us
    pallas_call x1, Pallas kernels: 3.53 us -> 2.68 us  [here_attention(): pl.pallas_call(lambda *refs: here_kernel(total, *refs), in_specs=[smem, s...]
    all_to_all x1, starting transfers between devices: 4.15 us -> 4.95 us  [local(): from_coarse = lax.all_to_all(from_coarse, 'narrow', 0, 0, tiled=True)]
  transfers between devices with their start and end apart: 8 -> 8, of which waited for: 2 -> 2; matrix products, arithmetic and copies ran while one was open for 0% -> 0% of each run, Pallas kernels for 16% -> 15%
where the time goes in v6:
time: 65.7 us; the launch traced here: 65.2 us
  starting transfers between devices  38.8 us (59%)
  Pallas kernels  19.1 us (29%)
  waiting for transfers between devices  7.02 us (11%)
    ppermute x1, starting transfers between devices, local(): got_o = lax.ppermute(pay_o, 'tile', odd_pairs)  17.9 us
    all_to_all x1, starting transfers between devices, local(): from_coarse = lax.all_to_all(from_coarse, 'narrow', 0, 0, tiled=True)  4.95 us
    ppermute x1, waiting for transfers between devices, local(): got_o = lax.ppermute(pay_o, 'tile', odd_pairs)  4.89 us
    all_to_all x1, starting transfers between devices, local(): q_head = lax.all_to_all(q_t, 'narrow', 0, 0, tiled=True)  4.24 us
    pallas_call x1, Pallas kernels, finish(): pl.pallas_call(finish_kernel, in_specs=[vmem] * 9 + [hbm] * 3, out_specs=...  4.15 us
    pallas_call x1, Pallas kernels, window_attention(): pl.pallas_call(lambda *refs: window_kernel(last, count, *refs), in_specs=...  3.86 us
    ppermute x1, starting transfers between devices, local(): lax.ppermute(stacked, 'narrow', [(i, i + 1) for i in range(members - 1)])  3.28 us
    ppermute x1, starting transfers between devices, local(): lax.ppermute(stacked, 'narrow', [(i, i - 1) for i in range(1, members)])  3.27 us
  transfers between devices with their start and end apart: 8, of which 2 were waited for; matrix products, arithmetic and copies ran while one was open for 0% of the time, Pallas kernels for 15%

profile of v6, /device:TPU:1, one launch (start us, length us, event | category | flops | bytes accessed | tf_op | source)
XLA Modules:
  0.0 65.2 jit_solution(2941060361676853387)
XLA Ops:
  0.0 0.0 copy-start.1
  0.0 0.1 pad_add_fusion.refs_0_.ids
  0.1 0.0 copy-start
  0.1 0.0 copy-start.2
  0.1 2.6 %project.1 = (bf16[512,128]{1,0:T(8,128)(2,1)S(1)}, bf16[752,128]{1,0:T(8,128)(2,1)S(1)}, bf16[752,128]{1,0:T(8,128)(2,1)S(1)}) custom-call(s32[2]{0:T(128)S(1)} %pad_add_fusion.refs_0_.ids, s32[1,8]{1,0:T(1,128)} %refs_1_.5, bf16[512,1024]{1,0:T(8,128)(2,1)} %bitcast.19, bf16[1024,512]{1,0:T(8,128)(2,1)} %refs_3_.1, bf16[1024,512]{1,0:T(8,128)(2,1)} %refs_4_.1, ...), custom_call_target="tpu_custom_call" | custom-call | flops 1000 | bytes 1000 | tf_op jit(solution)/shard_map/project/pallas_call | solution.py:108
  2.7 17.9 %collective-permute-start = (bf16[752,128]{1,0:T(8,128)(2,1)S(1)}, bf16[752,128]{1,0:T(8,128)(2,1)S(1)}, u32[]{:S(2)}, u32[]{:S(2)}) collective-permute-start(bf16[752,128]{1,0:T(8,128)(2,1)S(1)} %get-tuple-element.20), channel_id=1, source_target_pairs={{0,504},{8,16},{16,8},{24,32},{32,24},{40,48},{48,40},{56,64},{64,... | collective-permute-start | bytes 577544 | tf_op jit(solution)/shard_map/ppermute | solution.py:537
  20.6 1.9 %collective-permute-start.1 = (bf16[752,128]{1,0:T(8,128)(2,1)S(1)}, bf16[752,128]{1,0:T(8,128)(2,1)S(1)}, u32[]{:S(2)}, u32[]{:S(2)}) collective-permute-start(bf16[752,128]{1,0:T(8,128)(2,1)S(1)} %get-tuple-element.21), channel_id=1, source_target_pairs={{0,8},{8,0},{16,24},{24,16},{32,40},{40,32},{48,56},{56,48},{64,72... | collective-permute-start | bytes 577544 | tf_op jit(solution)/shard_map/ppermute | solution.py:538
  22.5 1.9 %collective-permute-start.4 = (bf16[512,128]{1,0:T(8,128)(2,1)S(1)}, bf16[512,128]{1,0:T(8,128)(2,1)S(1)}, u32[]{:S(2)}, u32[]{:S(2)}) collective-permute-start(bf16[512,128]{1,0:T(8,128)(2,1)S(1)} %get-tuple-element.23.after.refs_3_.own), channel_id=1, source_target_pairs={{0,16},{8,24},{16,32},{24,40},{32,48},{40,56},{48,64},{56,72},{64,... | collective-permute-start | bytes 393224 | tf_op jit(solution)/shard_map/ppermute | solution.py:539
  24.5 0.0 copy-done.1
  24.5 2.1 %queries.1 = (bf16[128,512]{1,0:T(8,128)(2,1)S(1)}, bf16[8,64,128]{2,1,0:T(8,128)(2,1)}) custom-call(bf16[512,128]{1,0:T(8,128)(2,1)S(1)} %get-tuple-element.23.after.refs_3_.own, bf16[128,512]{1,0:T(8,128)(2,1)} %bitcast.13, f32[1,512]{1,0:T(1,128)S(1)} %bitcast.16, bf16[512,512]{1,0:T(8,128)(2,1)} %w_q.1), custom_call_target="tpu_custom_call" | custom-call | flops 1000 | bytes 1000 | tf_op jit(solution)/shard_map/queries/pallas_call | solution.py:147
  26.6 4.2 %all-to-all-start = ((bf16[8,64,128]{2,1,0:T(8,128)(2,1)}), bf16[8,64,128]{2,1,0:T(8,128)(2,1)S(1)}, u32[]{:S(2)}, u32[]{:S(2)}) async-start(bf16[8,64,128]{2,1,0:T(8,128)(2,1)} %get-tuple-element.27), calls=%async_computation | async-start | bytes 262144 | tf_op jit(solution)/shard_map/all_to_all | solution.py:543
  30.8 0.0 copy-start.4
  30.8 4.9 %collective-permute-done.refs_0_.refs_4_.got_o = bf16[752,128]{1,0:T(8,128)(2,1)S(1)} collective-permute-done((bf16[752,128]{1,0:T(8,128)(2,1)S(1)}, bf16[752,128]{1,0:T(8,128)(2,1)S(1)}, u32[]{:S(2)}, u32[]{:S(2)}) %collective-permute-start) | collective-permute-done | bytes 192544 | tf_op jit(solution)/shard_map/ppermute | solution.py:537
  35.7 1.3 %collective-permute-start.5 = (bf16[752,128]{1,0:T(8,128)(2,1)S(1)}, bf16[752,128]{1,0:T(8,128)(2,1)S(1)}, u32[]{:S(2)}, u32[]{:S(2)}) collective-permute-start(bf16[752,128]{1,0:T(8,128)(2,1)S(1)} %collective-permute-done.refs_0_.refs_4_.got_o), channel_id=1, source_target_pairs={{0,8},{128,136},{256,264},{384,392},{1,9},{129,137},{257,265},{385... | collective-permute-start | bytes 577544 | tf_op jit(solution)/shard_map/ppermute | solution.py:545
  37.0 0.0 collective-permute-done.1.refs_1_.refs_5_.got_e
  37.0 0.0 copy-done
  37.0 0.0 copy-done.2
  37.0 0.6 stack_rows.1.refs_3_
  37.7 3.3 %collective-permute-start.3 = (bf16[192,512]{1,0:T(8,128)(2,1)S(1)}, bf16[192,512]{1,0:T(8,128)(2,1)S(1)}, u32[]{:S(2)}, u32[]{:S(2)}) collective-permute-start(bf16[192,512]{1,0:T(8,128)(2,1)S(1)} %stack_rows.1.refs_3_), channel_id=1, source_target_pairs={{1,0},{2,1},{3,2},{4,3},{5,4},{6,5},{7,6},{9,8},{10,9},{11,10},{12... | collective-permute-start | bytes 589832 | tf_op jit(solution)/shard_map/ppermute | solution.py:551
  40.9 3.3 %collective-permute-start.2 = (bf16[192,512]{1,0:T(8,128)(2,1)S(1)}, bf16[192,512]{1,0:T(8,128)(2,1)S(1)}, u32[]{:S(2)}, u32[]{:S(2)}) collective-permute-start(bf16[192,512]{1,0:T(8,128)(2,1)S(1)} %stack_rows.1.refs_3_), channel_id=1, source_target_pairs={{0,1},{1,2},{2,3},{3,4},{4,5},{5,6},{6,7},{8,9},{9,10},{10,11},{11... | collective-permute-start | bytes 589832 | tf_op jit(solution)/shard_map/ppermute | solution.py:552
  44.2 0.0 all-to-all-done.refs_2_.q_t
  44.2 0.0 copy-done.4
  44.2 2.7 %here_attention.1.after.here = bf16[8,80,128]{2,1,0:T(8,128)(2,1)S(1)} custom-call(s32[2]{0:T(128)S(1)} %pad_add_fusion.refs_0_.ids, s32[1,8]{1,0:T(1,128)S(1)} %copy-done.4, bf16[8,64,128]{2,1,0:T(8,128)(2,1)S(1)} %all-to-all-done.refs_2_.q_t, bf16[512,128]{1,0:T(8,128)(2,1)S(1)} %get-tuple-element.23.after.refs_3_.own, ...), custom_call_target="tpu_custom_call" | custom-call | flops 1000 | bytes 1000 | tf_op jit(solution)/shard_map/here_attention/pallas_call | solution.py:361
  46.9 0.0 collective-permute-done.4.far_straight
  46.9 0.0 collective-permute-done.5.far_handed
  46.9 0.8 %choose_blocks.1 = (bf16[1024,128]{1,0:T(8,128)(2,1)S(1)}, bf16[128,1024]{1,0:T(8,128)(2,1)S(1)}) custom-call(bf16[8,80,128]{2,1,0:T(8,128)(2,1)S(1)} %here_attention.1.after.here, s32[2]{0:T(128)S(1)} %pad_add_fusion.refs_0_.ids, s32[8]{0:T(128)S(1)} %fusion.1.table, bf16[512,128]{1,0:T(8,128)(2,1)S(1)} %collective-permute-done.4.far_straight, ...), custom_call_target="tpu_custom_call" | custom-call | flops 10000000000 | bytes 1000 | tf_op jit(solution)/shard_map/choose_blocks/pallas_call | solution.py:396
  47.7 0.0 collective-permute-done.3.refs_4_.after_too
  47.8 0.0 collective-permute-done.2.refs_2_.after
  47.8 2.4 %before_attention.1 = bf16[8,80,128]{2,1,0:T(8,128)(2,1)} custom-call(bf16[192,512]{1,0:T(8,128)(2,1)S(1)} %collective-permute-done.2.refs_2_.after, bf16[192,512]{1,0:T(8,128)(2,1)S(1)} %collective-permute-done.3.refs_4_.after_too, s32[2]{0:T(128)S(1)} %copy-done.2, bf16[8,64,128]{2,1,0:T(8,128)(2,1)S(1)} %all-to-all-done.refs_2_.q_t, ...), custom_call_target="tpu_custom_call" | custom-call | flops 1000 | bytes 1000 | tf_op jit(solution)/shard_map/before_attention/pallas_call | solution.py:423
  50.1 4.9 %all-to-all-start.1 = ((bf16[8,80,128]{2,1,0:T(8,128)(2,1)}), bf16[8,80,128]{2,1,0:T(8,128)(2,1)S(1)}, u32[]{:S(2)}, u32[]{:S(2)}) async-start(bf16[8,80,128]{2,1,0:T(8,128)(2,1)} %before_attention.1), calls=%async_computation.1 | async-start | bytes 327680 | tf_op jit(solution)/shard_map/all_to_all | solution.py:556
  55.1 0.0 copy-start.3
  55.1 3.9 %window_attention.1 = (f32[128,512]{1,0:T(8,128)S(1)}, f32[128,128]{1,0:T(8,128)S(1)}, bf16[512,512]{1,0:T(8,128)(2,1)S(1)}, bf16[512,512]{1,0:T(8,128)(2,1)S(1)...) custom-call(s32[2]{0:T(128)S(1)} %pad_add_fusion.refs_0_.ids, s32[2]{0:T(128)S(1)} %copy-done.2, ...), custom_call_target="tpu_custom_call" | custom-call | flops 1000 | bytes 1000 | tf_op jit(solution)/shard_map/window_attention/pallas_call | solution.py:276
  59.0 2.1 %all-to-all-done.1.coarse = bf16[8,80,128]{2,1,0:T(8,128)(2,1)S(1)} async-done(((bf16[8,80,128]{2,1,0:T(8,128)(2,1)}), bf16[8,80,128]{2,1,0:T(8,128)(2,1)S(1)}, u32[]{:S(2)}, u32[]{:S(2)}) %all-to-all-start.1) | async-done | bytes 163872 | tf_op jit(solution)/shard_map/all_to_all | solution.py:556
  61.1 0.0 copy-done.3
  61.1 4.1 %finish.1 = bf16[128,512]{1,0:T(8,128)(2,1)} custom-call(bf16[128,512]{1,0:T(8,128)(2,1)S(1)} %bitcast.15, f32[128,512]{1,0:T(8,128)S(1)} %get-tuple-element.25.near, f32[128,128]{1,0:T(8,128)S(1)} %get-tuple-element.26.near_lse, bf16[8,80,128]{2,1,0:T(8,128)(2,1)S(1)} %all-to-all-done.1.coarse, f32[1,512]{1,0:T(1,128)S(1)} %bitcast.18, ...), custom_call_target="tpu_custom_call" | custom-call | flops 1000 | bytes 1000 | tf_op jit(solution)/shard_map/finish/pallas_call | solution.py:483
  (1 shorter events, 0.0 us)
Async XLA Ops:
  0.0 24.5 %copy-start.1 = (f32[512]{0:T(512)S(1)}, f32[512]{0:T(512)}, u32[]{:S(2)}) copy-start(f32[512]{0:T(512)} %param.19) | copy-start | bytes 6148
  0.1 36.9 %copy-start = (bf16[16,8,512]{2,1,0:T(8,128)(2,1)S(1)}, bf16[16,8,512]{2,1,0:T(8,128)(2,1)}, u32[]{:S(2)}) copy-start(bf16[16,8,512]{2,1,0:T(8,128)(2,1)} %param.15) | copy-start | bytes 393220
  0.1 37.0 %copy-start.2 = (s32[2]{0:T(128)S(1)}, s32[2]{0:T(128)}, u32[]{:S(2)}) copy-start(s32[2]{0:T(128)} %shifts.3) | copy-start | bytes 28
  2.7 33.0 %collective-permute-start = (bf16[752,128]{1,0:T(8,128)(2,1)S(1)}, bf16[752,128]{1,0:T(8,128)(2,1)S(1)}, u32[]{:S(2)}, u32[]{:S(2)}) collective-permute-start(bf16[752,128]{1,0:T(8,128)(2,1)S(1)} %get-tuple-element.20), channel_id=1, source_target_pairs={{0,504},{8,16},{16,8},{24,32},{32,24},{40,48},{48,40},{56,64},{64,... | collective-permute-start | bytes 577544 | tf_op jit(solution)/shard_map/ppermute | solution.py:537
  20.6 16.4 %collective-permute-start.1 = (bf16[752,128]{1,0:T(8,128)(2,1)S(1)}, bf16[752,128]{1,0:T(8,128)(2,1)S(1)}, u32[]{:S(2)}, u32[]{:S(2)}) collective-permute-start(bf16[752,128]{1,0:T(8,128)(2,1)S(1)} %get-tuple-element.21), channel_id=1, source_target_pairs={{0,8},{8,0},{16,24},{24,16},{32,40},{40,32},{48,56},{56,48},{64,72... | collective-permute-start | bytes 577544 | tf_op jit(solution)/shard_map/ppermute | solution.py:538
  22.5 24.4 %collective-permute-start.4 = (bf16[512,128]{1,0:T(8,128)(2,1)S(1)}, bf16[512,128]{1,0:T(8,128)(2,1)S(1)}, u32[]{:S(2)}, u32[]{:S(2)}) collective-permute-start(bf16[512,128]{1,0:T(8,128)(2,1)S(1)} %get-tuple-element.23.after.refs_3_.own), channel_id=1, source_target_pairs={{0,16},{8,24},{16,32},{24,40},{32,48},{40,56},{48,64},{56,72},{64,... | collective-permute-start | bytes 393224 | tf_op jit(solution)/shard_map/ppermute | solution.py:539
  26.6 17.6 %all-to-all-start = ((bf16[8,64,128]{2,1,0:T(8,128)(2,1)}), bf16[8,64,128]{2,1,0:T(8,128)(2,1)S(1)}, u32[]{:S(2)}, u32[]{:S(2)}) async-start(bf16[8,64,128]{2,1,0:T(8,128)(2,1)} %get-tuple-element.27), calls=%async_computation | async-start | bytes 262144 | tf_op jit(solution)/shard_map/all_to_all | solution.py:543
  30.8 13.4 %copy-start.4 = (s32[1,8]{1,0:T(1,128)S(1)}, s32[1,8]{1,0:T(1,128)}, u32[]{:S(2)}) copy-start(s32[1,8]{1,0:T(1,128)} %refs_1_.5) | copy-start | bytes 100
  35.7 11.2 %collective-permute-start.5 = (bf16[752,128]{1,0:T(8,128)(2,1)S(1)}, bf16[752,128]{1,0:T(8,128)(2,1)S(1)}, u32[]{:S(2)}, u32[]{:S(2)}) collective-permute-start(bf16[752,128]{1,0:T(8,128)(2,1)S(1)} %collective-permute-done.refs_0_.refs_4_.got_o), channel_id=1, source_target_pairs={{0,8},{128,136},{256,264},{384,392},{1,9},{129,137},{257,265},{385... | collective-permute-start | bytes 577544 | tf_op jit(solution)/shard_map/ppermute | solution.py:545
  37.7 10.1 %collective-permute-start.3 = (bf16[192,512]{1,0:T(8,128)(2,1)S(1)}, bf16[192,512]{1,0:T(8,128)(2,1)S(1)}, u32[]{:S(2)}, u32[]{:S(2)}) collective-permute-start(bf16[192,512]{1,0:T(8,128)(2,1)S(1)} %stack_rows.1.refs_3_), channel_id=1, source_target_pairs={{1,0},{2,1},{3,2},{4,3},{5,4},{6,5},{7,6},{9,8},{10,9},{11,10},{12... | collective-permute-start | bytes 589832 | tf_op jit(solution)/shard_map/ppermute | solution.py:551
  40.9 6.8 %collective-permute-start.2 = (bf16[192,512]{1,0:T(8,128)(2,1)S(1)}, bf16[192,512]{1,0:T(8,128)(2,1)S(1)}, u32[]{:S(2)}, u32[]{:S(2)}) collective-permute-start(bf16[192,512]{1,0:T(8,128)(2,1)S(1)} %stack_rows.1.refs_3_), channel_id=1, source_target_pairs={{0,1},{1,2},{2,3},{3,4},{4,5},{5,6},{6,7},{8,9},{9,10},{10,11},{11... | collective-permute-start | bytes 589832 | tf_op jit(solution)/shard_map/ppermute | solution.py:552
  50.1 10.9 %all-to-all-start.1 = ((bf16[8,80,128]{2,1,0:T(8,128)(2,1)}), bf16[8,80,128]{2,1,0:T(8,128)(2,1)S(1)}, u32[]{:S(2)}, u32[]{:S(2)}) async-start(bf16[8,80,128]{2,1,0:T(8,128)(2,1)} %before_attention.1), calls=%async_computation.1 | async-start | bytes 327680 | tf_op jit(solution)/shard_map/all_to_all | solution.py:556
  55.1 6.0 %copy-start.3 = (f32[512]{0:T(512)S(1)}, f32[512]{0:T(512)}, u32[]{:S(2)}) copy-start(f32[512]{0:T(512)} %param.26) | copy-start | bytes 6148

commit v7 on v6

--- a/solution.py
+++ b/solution.py
@@ -321,15 +321,6 @@
     return jnp.concatenate(tiles, axis=1)
 
 
-def bottom_rows(q_t, group):
-    low = iota((1, 128), 1) < 64
-    tiles = []
-    for pair in range(4):
-        a, b = (q_t[8 * group + 2 * pair + k].astype(F32) for k in range(2))
-        tiles.append(jnp.where(low, swap_halves(a), b).astype(BF16))
-    return jnp.concatenate(tiles, axis=1)
-
-
 def here_kernel(total, ids, table, q_t, own, got_o, got_e, out, store, turned):
     n_own = own.shape[0]
     per_strip = n_own // 128
@@ -343,15 +334,9 @@
     kv = jnp.concatenate([store[b] for b in chosen], axis=0)
     turned[...] = kv.astype(F32).T.astype(BF16)
     kv_t = turned[...]
-    low = iota((1, 128), 1) < 64
-    for group in range(q_t.shape[0] // 8):
-        top = attend(top_rows(q_t, group), kv, kv_t)
-        bottom = attend(bottom_rows(q_t, group), kv, kv_t)
-        for pair in range(4):
-            lanes = slice(128 * pair, 128 * pair + 128)
-            t, u = top[:, lanes], bottom[:, lanes]
-            out[8 * group + 2 * pair] = jnp.where(low, t, swap_halves(u)).astype(BF16)
-            out[8 * group + 2 * pair + 1] = jnp.where(low, swap_halves(t), u).astype(BF16)
+    mixed = attend(jnp.concatenate([q_t[m] for m in range(q_t.shape[0])], axis=1), kv, kv_t)
+    for m in range(q_t.shape[0]):
+        out[m] = mixed[:, 128 * m : 128 * m + 128].astype(BF16)
 
 
 def here_attention(ids, table, q_t, own, got_o, got_e, total):

time: 65.7 us -> 65.7 us (level)
  no operation moved by 1% of the time
where the time goes in v7:
time: 65.7 us; the launch traced here: 65.2 us
  starting transfers between devices  39.1 us (60%)
  Pallas kernels  18.8 us (29%)
  waiting for transfers between devices  7.02 us (11%)
    ppermute x1, starting transfers between devices, local(): got_o = lax.ppermute(pay_o, 'tile', odd_pairs)  17.9 us
    all_to_all x1, starting transfers between devices, local(): from_coarse = lax.all_to_all(from_coarse, 'narrow', 0, 0, tiled=True)  5.22 us
    ppermute x1, waiting for transfers between devices, local(): got_o = lax.ppermute(pay_o, 'tile', odd_pairs)  4.89 us
    all_to_all x1, starting transfers between devices, local(): q_head = lax.all_to_all(q_t, 'narrow', 0, 0, tiled=True)  4.24 us
    pallas_call x1, Pallas kernels, finish(): pl.pallas_call(finish_kernel, in_specs=[vmem] * 9 + [hbm] * 3, out_specs=...  4.15 us
    pallas_call x1, Pallas kernels, window_attention(): pl.pallas_call(lambda *refs: window_kernel(last, count, *refs), in_specs=...  3.86 us
    ppermute x1, starting transfers between devices, local(): lax.ppermute(stacked, 'narrow', [(i, i + 1) for i in range(members - 1)])  3.28 us
    ppermute x1, starting transfers between devices, local(): lax.ppermute(stacked, 'narrow', [(i, i - 1) for i in range(1, members)])  3.27 us
  transfers between devices with their start and end apart: 8, of which 2 were waited for; matrix products, arithmetic and copies ran while one was open for 0% of the time, Pallas kernels for 15%

profile of v7, /device:TPU:1, one launch (start us, length us, event | category | flops | bytes accessed | tf_op | source)
XLA Modules:
  0.0 65.2 jit_solution(5896592252838105846)
XLA Ops:
  0.0 0.0 copy-start.1
  0.0 0.1 pad_add_fusion.refs_0_.ids
  0.1 0.0 copy-start
  0.1 0.0 copy-start.2
  0.1 2.6 %project.1 = (bf16[512,128]{1,0:T(8,128)(2,1)S(1)}, bf16[752,128]{1,0:T(8,128)(2,1)S(1)}, bf16[752,128]{1,0:T(8,128)(2,1)S(1)}) custom-call(s32[2]{0:T(128)S(1)} %pad_add_fusion.refs_0_.ids, s32[1,8]{1,0:T(1,128)} %refs_1_.5, bf16[512,1024]{1,0:T(8,128)(2,1)} %bitcast.19, bf16[1024,512]{1,0:T(8,128)(2,1)} %refs_3_.1, bf16[1024,512]{1,0:T(8,128)(2,1)} %refs_4_.1, ...), custom_call_target="tpu_custom_call" | custom-call | flops 1000 | bytes 1000 | tf_op jit(solution)/shard_map/project/pallas_call | solution.py:108
  2.7 17.9 %collective-permute-start = (bf16[752,128]{1,0:T(8,128)(2,1)S(1)}, bf16[752,128]{1,0:T(8,128)(2,1)S(1)}, u32[]{:S(2)}, u32[]{:S(2)}) collective-permute-start(bf16[752,128]{1,0:T(8,128)(2,1)S(1)} %get-tuple-element.20), channel_id=1, source_target_pairs={{0,504},{8,16},{16,8},{24,32},{32,24},{40,48},{48,40},{56,64},{64,... | collective-permute-start | bytes 577544 | tf_op jit(solution)/shard_map/ppermute | solution.py:522
  20.6 1.9 %collective-permute-start.1 = (bf16[752,128]{1,0:T(8,128)(2,1)S(1)}, bf16[752,128]{1,0:T(8,128)(2,1)S(1)}, u32[]{:S(2)}, u32[]{:S(2)}) collective-permute-start(bf16[752,128]{1,0:T(8,128)(2,1)S(1)} %get-tuple-element.21), channel_id=1, source_target_pairs={{0,8},{8,0},{16,24},{24,16},{32,40},{40,32},{48,56},{56,48},{64,72... | collective-permute-start | bytes 577544 | tf_op jit(solution)/shard_map/ppermute | solution.py:523
  22.5 1.9 %collective-permute-start.4 = (bf16[512,128]{1,0:T(8,128)(2,1)S(1)}, bf16[512,128]{1,0:T(8,128)(2,1)S(1)}, u32[]{:S(2)}, u32[]{:S(2)}) collective-permute-start(bf16[512,128]{1,0:T(8,128)(2,1)S(1)} %get-tuple-element.23.after.refs_3_.own), channel_id=1, source_target_pairs={{0,16},{8,24},{16,32},{24,40},{32,48},{40,56},{48,64},{56,72},{64,... | collective-permute-start | bytes 393224 | tf_op jit(solution)/shard_map/ppermute | solution.py:524
  24.5 0.0 copy-done.1
  24.5 2.1 %queries.1 = (bf16[128,512]{1,0:T(8,128)(2,1)S(1)}, bf16[8,64,128]{2,1,0:T(8,128)(2,1)}) custom-call(bf16[512,128]{1,0:T(8,128)(2,1)S(1)} %get-tuple-element.23.after.refs_3_.own, bf16[128,512]{1,0:T(8,128)(2,1)} %bitcast.13, f32[1,512]{1,0:T(1,128)S(1)} %bitcast.16, bf16[512,512]{1,0:T(8,128)(2,1)} %w_q.1), custom_call_target="tpu_custom_call" | custom-call | flops 1000 | bytes 1000 | tf_op jit(solution)/shard_map/queries/pallas_call | solution.py:147
  26.6 4.2 %all-to-all-start = ((bf16[8,64,128]{2,1,0:T(8,128)(2,1)}), bf16[8,64,128]{2,1,0:T(8,128)(2,1)S(1)}, u32[]{:S(2)}, u32[]{:S(2)}) async-start(bf16[8,64,128]{2,1,0:T(8,128)(2,1)} %get-tuple-element.27), calls=%async_computation | async-start | bytes 262144 | tf_op jit(solution)/shard_map/all_to_all | solution.py:528
  30.8 0.0 copy-start.4
  30.8 4.9 %collective-permute-done.refs_0_.refs_4_.got_o = bf16[752,128]{1,0:T(8,128)(2,1)S(1)} collective-permute-done((bf16[752,128]{1,0:T(8,128)(2,1)S(1)}, bf16[752,128]{1,0:T(8,128)(2,1)S(1)}, u32[]{:S(2)}, u32[]{:S(2)}) %collective-permute-start) | collective-permute-done | bytes 192544 | tf_op jit(solution)/shard_map/ppermute | solution.py:522
  35.7 1.3 %collective-permute-start.5 = (bf16[752,128]{1,0:T(8,128)(2,1)S(1)}, bf16[752,128]{1,0:T(8,128)(2,1)S(1)}, u32[]{:S(2)}, u32[]{:S(2)}) collective-permute-start(bf16[752,128]{1,0:T(8,128)(2,1)S(1)} %collective-permute-done.refs_0_.refs_4_.got_o), channel_id=1, source_target_pairs={{0,8},{128,136},{256,264},{384,392},{1,9},{129,137},{257,265},{385... | collective-permute-start | bytes 577544 | tf_op jit(solution)/shard_map/ppermute | solution.py:530
  37.0 0.0 collective-permute-done.1.refs_1_.refs_5_.got_e
  37.0 0.0 copy-done
  37.0 0.0 copy-done.2
  37.0 0.6 stack_rows.1.refs_3_
  37.7 3.3 %collective-permute-start.3 = (bf16[192,512]{1,0:T(8,128)(2,1)S(1)}, bf16[192,512]{1,0:T(8,128)(2,1)S(1)}, u32[]{:S(2)}, u32[]{:S(2)}) collective-permute-start(bf16[192,512]{1,0:T(8,128)(2,1)S(1)} %stack_rows.1.refs_3_), channel_id=1, source_target_pairs={{1,0},{2,1},{3,2},{4,3},{5,4},{6,5},{7,6},{9,8},{10,9},{11,10},{12... | collective-permute-start | bytes 589832 | tf_op jit(solution)/shard_map/ppermute | solution.py:536
  40.9 3.3 %collective-permute-start.2 = (bf16[192,512]{1,0:T(8,128)(2,1)S(1)}, bf16[192,512]{1,0:T(8,128)(2,1)S(1)}, u32[]{:S(2)}, u32[]{:S(2)}) collective-permute-start(bf16[192,512]{1,0:T(8,128)(2,1)S(1)} %stack_rows.1.refs_3_), channel_id=1, source_target_pairs={{0,1},{1,2},{2,3},{3,4},{4,5},{5,6},{6,7},{8,9},{9,10},{10,11},{11... | collective-permute-start | bytes 589832 | tf_op jit(solution)/shard_map/ppermute | solution.py:537
  44.2 0.0 all-to-all-done.refs_2_.q_t
  44.2 0.0 copy-done.4
  44.2 2.4 %here_attention.1.after.here = bf16[8,80,128]{2,1,0:T(8,128)(2,1)S(1)} custom-call(s32[2]{0:T(128)S(1)} %pad_add_fusion.refs_0_.ids, s32[1,8]{1,0:T(1,128)S(1)} %copy-done.4, bf16[8,64,128]{2,1,0:T(8,128)(2,1)S(1)} %all-to-all-done.refs_2_.q_t, bf16[512,128]{1,0:T(8,128)(2,1)S(1)} %get-tuple-element.23.after.refs_3_.own, ...), custom_call_target="tpu_custom_call" | custom-call | flops 1000 | bytes 1000 | tf_op jit(solution)/shard_map/here_attention/pallas_call | solution.py:346
  46.6 0.0 collective-permute-done.4.far_straight
  46.7 0.0 collective-permute-done.5.far_handed
  46.7 0.8 %choose_blocks.1 = (bf16[1024,128]{1,0:T(8,128)(2,1)S(1)}, bf16[128,1024]{1,0:T(8,128)(2,1)S(1)}) custom-call(bf16[8,80,128]{2,1,0:T(8,128)(2,1)S(1)} %here_attention.1.after.here, s32[2]{0:T(128)S(1)} %pad_add_fusion.refs_0_.ids, s32[8]{0:T(128)S(1)} %fusion.1.table, bf16[512,128]{1,0:T(8,128)(2,1)S(1)} %collective-permute-done.4.far_straight, ...), custom_call_target="tpu_custom_call" | custom-call | flops 10000000000 | bytes 1000 | tf_op jit(solution)/shard_map/choose_blocks/pallas_call | solution.py:381
  47.5 0.0 collective-permute-done.3.refs_4_.after_too
  47.5 0.0 collective-permute-done.2.refs_2_.after
  47.5 2.4 %before_attention.1 = bf16[8,80,128]{2,1,0:T(8,128)(2,1)} custom-call(bf16[192,512]{1,0:T(8,128)(2,1)S(1)} %collective-permute-done.2.refs_2_.after, bf16[192,512]{1,0:T(8,128)(2,1)S(1)} %collective-permute-done.3.refs_4_.after_too, s32[2]{0:T(128)S(1)} %copy-done.2, bf16[8,64,128]{2,1,0:T(8,128)(2,1)S(1)} %all-to-all-done.refs_2_.q_t, ...), custom_call_target="tpu_custom_call" | custom-call | flops 1000 | bytes 1000 | tf_op jit(solution)/shard_map/before_attention/pallas_call | solution.py:408
  49.9 5.2 %all-to-all-start.1 = ((bf16[8,80,128]{2,1,0:T(8,128)(2,1)}), bf16[8,80,128]{2,1,0:T(8,128)(2,1)S(1)}, u32[]{:S(2)}, u32[]{:S(2)}) async-start(bf16[8,80,128]{2,1,0:T(8,128)(2,1)} %before_attention.1), calls=%async_computation.1 | async-start | bytes 327680 | tf_op jit(solution)/shard_map/all_to_all | solution.py:541
  55.1 0.0 copy-start.3
  55.1 3.9 %window_attention.1 = (f32[128,512]{1,0:T(8,128)S(1)}, f32[128,128]{1,0:T(8,128)S(1)}, bf16[512,512]{1,0:T(8,128)(2,1)S(1)}, bf16[512,512]{1,0:T(8,128)(2,1)S(1)...) custom-call(s32[2]{0:T(128)S(1)} %pad_add_fusion.refs_0_.ids, s32[2]{0:T(128)S(1)} %copy-done.2, ...), custom_call_target="tpu_custom_call" | custom-call | flops 1000 | bytes 1000 | tf_op jit(solution)/shard_map/window_attention/pallas_call | solution.py:276
  59.0 2.1 %all-to-all-done.1.coarse = bf16[8,80,128]{2,1,0:T(8,128)(2,1)S(1)} async-done(((bf16[8,80,128]{2,1,0:T(8,128)(2,1)}), bf16[8,80,128]{2,1,0:T(8,128)(2,1)S(1)}, u32[]{:S(2)}, u32[]{:S(2)}) %all-to-all-start.1) | async-done | bytes 163872 | tf_op jit(solution)/shard_map/all_to_all | solution.py:541
  61.1 0.0 copy-done.3
  61.1 4.1 %finish.1 = bf16[128,512]{1,0:T(8,128)(2,1)} custom-call(bf16[128,512]{1,0:T(8,128)(2,1)S(1)} %bitcast.15, f32[128,512]{1,0:T(8,128)S(1)} %get-tuple-element.25.near, f32[128,128]{1,0:T(8,128)S(1)} %get-tuple-element.26.near_lse, bf16[8,80,128]{2,1,0:T(8,128)(2,1)S(1)} %all-to-all-done.1.coarse, f32[1,512]{1,0:T(1,128)S(1)} %bitcast.18, ...), custom_call_target="tpu_custom_call" | custom-call | flops 1000 | bytes 1000 | tf_op jit(solution)/shard_map/finish/pallas_call | solution.py:468
  (1 shorter events, 0.0 us)
Async XLA Ops:
  0.0 24.5 %copy-start.1 = (f32[512]{0:T(512)S(1)}, f32[512]{0:T(512)}, u32[]{:S(2)}) copy-start(f32[512]{0:T(512)} %param.19) | copy-start | bytes 6148
  0.1 36.9 %copy-start = (bf16[16,8,512]{2,1,0:T(8,128)(2,1)S(1)}, bf16[16,8,512]{2,1,0:T(8,128)(2,1)}, u32[]{:S(2)}) copy-start(bf16[16,8,512]{2,1,0:T(8,128)(2,1)} %param.15) | copy-start | bytes 393220
  0.1 37.0 %copy-start.2 = (s32[2]{0:T(128)S(1)}, s32[2]{0:T(128)}, u32[]{:S(2)}) copy-start(s32[2]{0:T(128)} %shifts.3) | copy-start | bytes 28
  2.7 33.0 %collective-permute-start = (bf16[752,128]{1,0:T(8,128)(2,1)S(1)}, bf16[752,128]{1,0:T(8,128)(2,1)S(1)}, u32[]{:S(2)}, u32[]{:S(2)}) collective-permute-start(bf16[752,128]{1,0:T(8,128)(2,1)S(1)} %get-tuple-element.20), channel_id=1, source_target_pairs={{0,504},{8,16},{16,8},{24,32},{32,24},{40,48},{48,40},{56,64},{64,... | collective-permute-start | bytes 577544 | tf_op jit(solution)/shard_map/ppermute | solution.py:522
  20.6 16.4 %collective-permute-start.1 = (bf16[752,128]{1,0:T(8,128)(2,1)S(1)}, bf16[752,128]{1,0:T(8,128)(2,1)S(1)}, u32[]{:S(2)}, u32[]{:S(2)}) collective-permute-start(bf16[752,128]{1,0:T(8,128)(2,1)S(1)} %get-tuple-element.21), channel_id=1, source_target_pairs={{0,8},{8,0},{16,24},{24,16},{32,40},{40,32},{48,56},{56,48},{64,72... | collective-permute-start | bytes 577544 | tf_op jit(solution)/shard_map/ppermute | solution.py:523
  22.5 24.1 %collective-permute-start.4 = (bf16[512,128]{1,0:T(8,128)(2,1)S(1)}, bf16[512,128]{1,0:T(8,128)(2,1)S(1)}, u32[]{:S(2)}, u32[]{:S(2)}) collective-permute-start(bf16[512,128]{1,0:T(8,128)(2,1)S(1)} %get-tuple-element.23.after.refs_3_.own), channel_id=1, source_target_pairs={{0,16},{8,24},{16,32},{24,40},{32,48},{40,56},{48,64},{56,72},{64,... | collective-permute-start | bytes 393224 | tf_op jit(solution)/shard_map/ppermute | solution.py:524
  26.6 17.6 %all-to-all-start = ((bf16[8,64,128]{2,1,0:T(8,128)(2,1)}), bf16[8,64,128]{2,1,0:T(8,128)(2,1)S(1)}, u32[]{:S(2)}, u32[]{:S(2)}) async-start(bf16[8,64,128]{2,1,0:T(8,128)(2,1)} %get-tuple-element.27), calls=%async_computation | async-start | bytes 262144 | tf_op jit(solution)/shard_map/all_to_all | solution.py:528
  30.8 13.4 %copy-start.4 = (s32[1,8]{1,0:T(1,128)S(1)}, s32[1,8]{1,0:T(1,128)}, u32[]{:S(2)}) copy-start(s32[1,8]{1,0:T(1,128)} %refs_1_.5) | copy-start | bytes 100
  35.7 10.9 %collective-permute-start.5 = (bf16[752,128]{1,0:T(8,128)(2,1)S(1)}, bf16[752,128]{1,0:T(8,128)(2,1)S(1)}, u32[]{:S(2)}, u32[]{:S(2)}) collective-permute-start(bf16[752,128]{1,0:T(8,128)(2,1)S(1)} %collective-permute-done.refs_0_.refs_4_.got_o), channel_id=1, source_target_pairs={{0,8},{128,136},{256,264},{384,392},{1,9},{129,137},{257,265},{385... | collective-permute-start | bytes 577544 | tf_op jit(solution)/shard_map/ppermute | solution.py:530
  37.7 9.8 %collective-permute-start.3 = (bf16[192,512]{1,0:T(8,128)(2,1)S(1)}, bf16[192,512]{1,0:T(8,128)(2,1)S(1)}, u32[]{:S(2)}, u32[]{:S(2)}) collective-permute-start(bf16[192,512]{1,0:T(8,128)(2,1)S(1)} %stack_rows.1.refs_3_), channel_id=1, source_target_pairs={{1,0},{2,1},{3,2},{4,3},{5,4},{6,5},{7,6},{9,8},{10,9},{11,10},{12... | collective-permute-start | bytes 589832 | tf_op jit(solution)/shard_map/ppermute | solution.py:536
  40.9 6.5 %collective-permute-start.2 = (bf16[192,512]{1,0:T(8,128)(2,1)S(1)}, bf16[192,512]{1,0:T(8,128)(2,1)S(1)}, u32[]{:S(2)}, u32[]{:S(2)}) collective-permute-start(bf16[192,512]{1,0:T(8,128)(2,1)S(1)} %stack_rows.1.refs_3_), channel_id=1, source_target_pairs={{0,1},{1,2},{2,3},{3,4},{4,5},{5,6},{6,7},{8,9},{9,10},{10,11},{11... | collective-permute-start | bytes 589832 | tf_op jit(solution)/shard_map/ppermute | solution.py:537
  49.9 11.2 %all-to-all-start.1 = ((bf16[8,80,128]{2,1,0:T(8,128)(2,1)}), bf16[8,80,128]{2,1,0:T(8,128)(2,1)S(1)}, u32[]{:S(2)}, u32[]{:S(2)}) async-start(bf16[8,80,128]{2,1,0:T(8,128)(2,1)} %before_attention.1), calls=%async_computation.1 | async-start | bytes 327680 | tf_op jit(solution)/shard_map/all_to_all | solution.py:541
  55.1 6.0 %copy-start.3 = (f32[512]{0:T(512)S(1)}, f32[512]{0:T(512)}, u32[]{:S(2)}) copy-start(f32[512]{0:T(512)} %param.26) | copy-start | bytes 6148
